TPU v7x, 768 devices: a whole 4x8x12 slice. The times are simulated.
768 devices in a mesh: gz: 96 (over x, z, core), gy: 8 (over y).
Axes of the slice: x: 4, y: 8, z: 12, core: 2. Of those that a mesh axis runs over, the one named last changes fastest.
Arguments:
- source: float32 [384, 128, 512], P('gz', 'gy'), may hold values from -8 to 8
- conduct: float32 [384, 128, 512], P('gz', 'gy'), may hold values from 0.5 to 4
Outputs:
- adjoint: float32 [384, 128, 512], P('gz', 'gy')
- residual: float32 [384, 128, 512], P('gz', 'gy')
All inputs are finite; a program needn't handle non-finite values.
Results may differ from a plain program's by a relative error of at most 0.0003.
Values sent between devices are 32-bit elements; how exact they have to be, the bound alone decides.
No kernel may reach another device: no remote copies, remote signals or barrier semaphores. Data moves between devices by JAX's collectives and lax.ppermute only.
A program may use at most 64 MiB of HBM per device.

v0:
```python
import jax
import jax.numpy as jnp
from jax import lax
from jax.sharding import PartitionSpec as P

DEGREE = 3
COARSE_DEGREE = 4
CYCLES = 2


cheb_low = 0.3
cheb_high = 1.9
heat_step = 4.0


def extended(shard, sides, width):
    edges = {}
    for axis, dim in sides:
        devices, length = (lax.axis_size(axis), shard.shape[dim])
        up = [(i, (i + 1) % devices) for i in range(devices)]
        last = lax.slice_in_dim(shard, length - width, length, axis=dim)
        first = lax.slice_in_dim(shard, 0, width, axis=dim)
        edges[dim] = (
            lax.ppermute(last, axis, up),
            lax.ppermute(first, axis, [(b, a) for a, b in up]),
        )
    done = []
    for _, dim in sides:
        low, high = edges[dim]
        around = [(width, width) if d in done else (0, 0) for d in range(shard.ndim)]
        shard = jnp.concatenate([jnp.pad(low, around), shard, jnp.pad(high, around)], axis=dim)
        done.append(dim)
    return shard


def padded_2(shard, sides, width):
    for axis, dim in sides:
        devices, length = (lax.axis_size(axis), shard.shape[dim])
        up = [(i, (i + 1) % devices) for i in range(devices)]
        down = [(j, i) for i, j in up]
        last = lax.slice_in_dim(shard, length - width, length, axis=dim)
        first = lax.slice_in_dim(shard, 0, width, axis=dim)
        before = lax.ppermute(last, axis, up)
        after = lax.ppermute(first, axis, down)
        shard = jnp.concatenate([before, shard, after], axis=dim)
    return shard


def laid_out(pieces, dim):
    shape = list(pieces.shape[1:])
    shape[dim] *= pieces.shape[0]
    return jnp.moveaxis(pieces, 0, dim).reshape(shape)


def from_everyone(shard, axis):
    copies = jnp.broadcast_to(shard, (lax.axis_size(axis), *shard.shape))
    return lax.all_to_all(copies, axis, split_axis=0, concat_axis=0, tiled=True)


def gather_directly(shard, axis, dim):
    return laid_out(from_everyone(shard, axis), dim)


def side_by_side(arrays, axis, dim, along):
    widths = [a.shape[along] for a in arrays]
    both = jnp.concatenate(arrays, axis=along)
    result = gather_directly(both, axis, dim)
    return tuple(jnp.split(result, [sum(widths[:k]) for k in range(1, len(widths))], axis=along))


def spread_apply(field, conduct, scale):
    w = conduct * field
    padded = extended(w, (("gz", 0), ("gy", 1)), 1)
    beside = padded[2:, 1:-1, :] + padded[:-2, 1:-1, :]
    beside = beside + padded[1:-1, 2:, :] + padded[1:-1, :-2, :]
    wide = jnp.pad(w, ((0, 0), (0, 0), (1, 1)))
    beside = beside + wide[:, :, 2:] + wide[:, :, :-2]
    return field + scale * (6.0 * w - beside)


def group_apply(field, conduct, scale):
    w = conduct * field
    padded = padded_2(w, (("gz", 0),), 1)
    beside = padded[2:] + padded[:-2]
    beside = beside + jnp.roll(w, -1, 1) + jnp.roll(w, 1, 1)
    wide = jnp.pad(w, ((0, 0), (0, 0), (1, 1)))
    beside = beside + wide[:, :, 2:] + wide[:, :, :-2]
    return field + scale * (6.0 * w - beside)


def deep_halo(field):
    return padded_2(field, (("gz", 0), ("gy", 1)), DEGREE)


def trim(field):
    return field[1:-1, 1:-1, :]


def margin_apply(field, conduct, scale):
    w = conduct * field
    beside = w[2:, 1:-1, :] + w[:-2, 1:-1, :]
    beside = beside + w[1:-1, 2:, :] + w[1:-1, :-2, :]
    inner = trim(w)
    wide = jnp.pad(inner, ((0, 0), (0, 0), (1, 1)))
    beside = beside + wide[:, :, 2:] + wide[:, :, :-2]
    return trim(field) + scale * (6.0 * inner - beside)


def margin_smooth(rhs_pad, cond_pad, start_pad, scale, steps):
    theta = (cheb_high + cheb_low) / 2.0
    delta = (cheb_high - cheb_low) / 2.0
    sigma = theta / delta
    rho = 1.0 / sigma
    field = jnp.zeros_like(rhs_pad) if start_pad is None else start_pad
    rhs = rhs_pad
    cond = cond_pad
    inverse = 1.0 / (1.0 + 6.0 * scale * cond_pad)
    change = None
    for step in range(steps):
        image = margin_apply(field, cond, scale)
        rhs = trim(rhs)
        inverse = trim(inverse)
        cond = trim(cond)
        field = trim(field)
        correct = inverse * (rhs - image)
        if step == 0:
            change = correct / theta
        else:
            rho_next = 1.0 / (2.0 * sigma - rho)
            change = rho_next * rho * trim(change) + 2.0 * rho_next / delta * correct
            rho = rho_next
        field = field + change
    return field


def restrict(field):
    z, y, x = field.shape
    return field.reshape(z // 2, 2, y // 2, 2, x // 2, 2).mean(axis=(1, 3, 5))


def prolong(field):
    return jnp.repeat(jnp.repeat(jnp.repeat(field, 2, 0), 2, 1), 2, 2)


def smooth(apply_fn, rhs, start, inv_diag, steps):
    theta = (cheb_high + cheb_low) / 2.0
    delta = (cheb_high - cheb_low) / 2.0
    sigma = theta / delta
    rho = 1.0 / sigma
    if start is None:
        correct = inv_diag * rhs
        change = correct / theta
        field = change
    else:
        correct = inv_diag * (rhs - apply_fn(start))
        change = correct / theta
        field = start + change
    for step in range(steps - 1):
        rho_next = 1.0 / (2.0 * sigma - rho)
        correct = inv_diag * (rhs - apply_fn(field))
        change = rho_next * rho * change + 2.0 * rho_next / delta * correct
        field = field + change
        rho = rho_next
    return field


def bind(apply_fn, conduct, scale):

    def inner(field):
        return apply_fn(field, conduct, scale)

    return inner


def coarse_solve(rhs_low, low_cond, scale):
    whole_rhs, whole_cond = side_by_side((rhs_low, low_cond), "gy", 1, 0)
    diag = 1.0 / (1.0 + 6.0 * scale * whole_cond)
    result = smooth(bind(group_apply, whole_cond, scale), whole_rhs, None, diag, COARSE_DEGREE)
    rows = rhs_low.shape[1]
    return lax.dynamic_slice_in_dim(result, lax.axis_index("gy") * rows, rows, 1)


def vcycle(rhs, conducts, scales, cond_pad):
    ops = [bind(spread_apply, conducts[i], scales[i]) for i in range(2)]
    diags = [1.0 / (1.0 + 6.0 * scales[i] * conducts[i]) for i in range(2)]
    rhs_pad = None
    rhs_pad = deep_halo(rhs)
    fine = margin_smooth(rhs_pad, cond_pad, None, scales[0], DEGREE)
    rhs_mid = restrict(rhs - ops[0](fine))
    middle = smooth(ops[1], rhs_mid, None, diags[1], DEGREE)
    rhs_low = restrict(rhs_mid - ops[1](middle))
    lowest = coarse_solve(rhs_low, conducts[2], scales[2])
    middle = smooth(ops[1], rhs_mid, middle + prolong(lowest), diags[1], DEGREE)
    start_pad = deep_halo(fine + prolong(middle))
    fine = margin_smooth(rhs_pad, cond_pad, start_pad, scales[0], DEGREE)
    return fine


def local(source, conduct):
    mid_cond = restrict(conduct)
    conducts = [conduct, mid_cond, restrict(mid_cond)]
    scales = [heat_step, heat_step / 4.0, heat_step / 16.0]
    cond_pad = None
    cond_pad = deep_halo(conduct)
    adjoint = jnp.zeros_like(source)
    remain = source
    for cycle in range(CYCLES):
        adjoint = adjoint + vcycle(remain, conducts, scales, cond_pad)
        remain = source - spread_apply(adjoint, conduct, heat_step)
    return (adjoint, remain)


def solution(mesh):
    placed = (P("gz", "gy", None), P("gz", "gy", None))
    return jax.shard_map(
        local,
        mesh=mesh,
        in_specs=placed,
        out_specs=(P("gz", "gy", None), P("gz", "gy", None)),
        check_vma=False,
    )
```

profile of v0, /device:TPU:1, one launch (start us, length us, event | category | flops | bytes accessed | tf_op | source)
XLA Modules:
  0.0 525.8 jit_solution(4385613702837971313)
XLA Ops:
  7.1 9.0 %collective-permute-start.1 = (f32[3,16,512]{2,1,0:T(8,128)S(1)}, f32[3,16,512]{2,1,0:T(8,128)S(1)}, u32[]{:S(2)}, u32[]{:S(2)}) collective-permute-start(f32[3,16,512]{2,1,0:T(8,128)S(1)} %get-tuple-element.100), channel_id=1, source_target_pairs={{8,0},{16,8},{24,16},{32,24},{40,32},{48,40},{56,48},{64,56},{72,6... | collective-permute-start | bytes 294920 | tf_op jit(solution)/shard_map/ppermute | solution.py:44
  19.0 7.2 %collective-permute-start.5 = (f32[3,16,512]{2,1,0:T(8,128)S(1)}, f32[3,16,512]{2,1,0:T(8,128)S(1)}, u32[]{:S(2)}, u32[]{:S(2)}) collective-permute-start(f32[3,16,512]{2,1,0:T(8,128)S(1)} %get-tuple-element.98), channel_id=1, source_target_pairs={{8,0},{16,8},{24,16},{32,24},{40,32},{48,40},{56,48},{64,56},{72,6... | collective-permute-start | bytes 294920 | tf_op jit(solution)/shard_map/ppermute | solution.py:44
  44.6 8.4 %collective-permute-start.8 = (f32[1,16,512]{2,1,0:T(8,128)S(1)}, f32[1,16,512]{2,1,0:T(8,128)S(1)}, u32[]{:S(2)}, u32[]{:S(2)}) collective-permute-start(f32[1,16,512]{2,1,0:T(8,128)S(1)} %get-tuple-element.97), channel_id=1, source_target_pairs={{8,0},{16,8},{24,16},{32,24},{40,32},{48,40},{56,48},{64,56},{72,6... | collective-permute-start | bytes 98312 | tf_op jit(solution)/shard_map/ppermute | solution.py:25
  62.1 9.8 %reshape.265 = f32[2,2,8,2,256,2]{5,4,3,2,1,0:T(8,128)} reshape(f32[4,16,512]{2,1,0:T(8,128)S(1)} %copy-done) | data formatting | bytes 262144 | tf_op jit(solution)/shard_map/reshape | solution.py:138
  76.1 9.8 %reshape.266 = f32[2,2,8,2,256,2]{5,4,3,2,1,0:T(8,128)} reshape(f32[4,16,512]{2,1,0:T(8,128)S(1)} %fusion.71) | data formatting | bytes 262144 | tf_op jit(solution)/shard_map/reshape | solution.py:138
  146.0 6.9 %all-to-all-done = f32[8,2,4,128]{3,2,1,0:T(4,128)S(1)} async-done(((f32[8,2,4,128]{3,2,1,0:T(4,128)}), f32[8,2,4,128]{3,2,1,0:T(4,128)S(1)}, u32[]{:S(2)}, u32[]{:S(2)}) %all-to-all-start) | async-done | bytes 32800 | tf_op jit(solution)/shard_map/all_to_all | solution.py:57
  152.9 8.4 %collective-permute-start.24 = (f32[1,32,128]{2,1,0:T(8,128)S(1)}, f32[1,32,128]{2,1,0:T(8,128)S(1)}, u32[]{:S(2)}, u32[]{:S(2)}) collective-permute-start(f32[1,32,128]{2,1,0:T(8,128)S(1)} %multiply_multiply_fusion.4), channel_id=1, source_target_pairs={{8,0},{16,8},{24,16},{32,24},{40,32},{48,40},{56,48},{64,56},{72,6... | collective-permute-start | bytes 49160 | tf_op jit(solution)/shard_map/ppermute | solution.py:44
  166.5 7.7 %collective-permute-start.26 = (f32[1,32,128]{2,1,0:T(8,128)S(1)}, f32[1,32,128]{2,1,0:T(8,128)S(1)}, u32[]{:S(2)}, u32[]{:S(2)}) collective-permute-start(f32[1,32,128]{2,1,0:T(8,128)S(1)} %get-tuple-element.47), channel_id=1, source_target_pairs={{8,0},{16,8},{24,16},{32,24},{40,32},{48,40},{56,48},{64,56},{72,6... | collective-permute-start | bytes 49160 | tf_op jit(solution)/shard_map/ppermute | solution.py:44
  177.4 7.2 %collective-permute-start.28 = (f32[1,32,128]{2,1,0:T(8,128)S(1)}, f32[1,32,128]{2,1,0:T(8,128)S(1)}, u32[]{:S(2)}, u32[]{:S(2)}) collective-permute-start(f32[1,32,128]{2,1,0:T(8,128)S(1)} %get-tuple-element.44), channel_id=1, source_target_pairs={{8,0},{16,8},{24,16},{32,24},{40,32},{48,40},{56,48},{64,56},{72,6... | collective-permute-start | bytes 49160 | tf_op jit(solution)/shard_map/ppermute | solution.py:44
  188.0 7.2 %collective-permute-start.30 = (f32[1,8,256]{2,1,0:T(8,128)S(1)}, f32[1,8,256]{2,1,0:T(8,128)S(1)}, u32[]{:S(2)}, u32[]{:S(2)}) collective-permute-start(f32[1,8,256]{2,1,0:T(8,128)S(1)} %get-tuple-element.154), channel_id=1, source_target_pairs={{8,0},{16,8},{24,16},{32,24},{40,32},{48,40},{56,48},{64,56},{72,6... | collective-permute-start | bytes 24584 | tf_op jit(solution)/shard_map/ppermute | solution.py:25
  240.4 7.0 %collective-permute-start.43 = (f32[3,16,512]{2,1,0:T(8,128)S(1)}, f32[3,16,512]{2,1,0:T(8,128)S(1)}, u32[]{:S(2)}, u32[]{:S(2)}) collective-permute-start(f32[3,16,512]{2,1,0:T(8,128)S(1)} %get-tuple-element.93), channel_id=1, source_target_pairs={{8,0},{16,8},{24,16},{32,24},{40,32},{48,40},{56,48},{64,56},{72,6... | collective-permute-start | bytes 294920 | tf_op jit(solution)/shard_map/ppermute | solution.py:44
  258.8 9.4 %collective-permute-start.46 = (f32[1,16,512]{2,1,0:T(8,128)S(1)}, f32[1,16,512]{2,1,0:T(8,128)S(1)}, u32[]{:S(2)}, u32[]{:S(2)}) collective-permute-start(f32[1,16,512]{2,1,0:T(8,128)S(1)} %get-tuple-element.91), channel_id=1, source_target_pairs={{8,0},{16,8},{24,16},{32,24},{40,32},{48,40},{56,48},{64,56},{72,6... | collective-permute-start | bytes 98312 | tf_op jit(solution)/shard_map/ppermute | solution.py:25
  283.1 7.1 %collective-permute-start.51 = (f32[3,16,512]{2,1,0:T(8,128)S(1)}, f32[3,16,512]{2,1,0:T(8,128)S(1)}, u32[]{:S(2)}, u32[]{:S(2)}) collective-permute-start(f32[3,16,512]{2,1,0:T(8,128)S(1)} %get-tuple-element.87), channel_id=1, source_target_pairs={{8,0},{16,8},{24,16},{32,24},{40,32},{48,40},{56,48},{64,56},{72,6... | collective-permute-start | bytes 294920 | tf_op jit(solution)/shard_map/ppermute | solution.py:44
  300.1 9.4 %collective-permute-start.54 = (f32[1,16,512]{2,1,0:T(8,128)S(1)}, f32[1,16,512]{2,1,0:T(8,128)S(1)}, u32[]{:S(2)}, u32[]{:S(2)}) collective-permute-start(f32[1,16,512]{2,1,0:T(8,128)S(1)} %get-tuple-element.85), channel_id=1, source_target_pairs={{8,0},{16,8},{24,16},{32,24},{40,32},{48,40},{56,48},{64,56},{72,6... | collective-permute-start | bytes 98312 | tf_op jit(solution)/shard_map/ppermute | solution.py:25
  322.4 9.8 %reshape.270 = f32[2,2,8,2,256,2]{5,4,3,2,1,0:T(8,128)} reshape(f32[4,16,512]{2,1,0:T(8,128)S(1)} %fusion.103) | data formatting | bytes 262144 | tf_op jit(solution)/shard_map/reshape | solution.py:138
  336.3 7.1 %collective-permute-start.58 = (f32[1,8,256]{2,1,0:T(8,128)S(1)}, f32[1,8,256]{2,1,0:T(8,128)S(1)}, u32[]{:S(2)}, u32[]{:S(2)}) collective-permute-start(f32[1,8,256]{2,1,0:T(8,128)S(1)} %get-tuple-element.142), channel_id=1, source_target_pairs={{8,0},{16,8},{24,16},{32,24},{40,32},{48,40},{56,48},{64,56},{72,6... | collective-permute-start | bytes 24584 | tf_op jit(solution)/shard_map/ppermute | solution.py:25
  369.1 7.0 %collective-permute-start.66 = (f32[1,8,256]{2,1,0:T(8,128)S(1)}, f32[1,8,256]{2,1,0:T(8,128)S(1)}, u32[]{:S(2)}, u32[]{:S(2)}) collective-permute-start(f32[1,8,256]{2,1,0:T(8,128)S(1)} %get-tuple-element.134), channel_id=1, source_target_pairs={{8,0},{16,8},{24,16},{32,24},{40,32},{48,40},{56,48},{64,56},{72,6... | collective-permute-start | bytes 24584 | tf_op jit(solution)/shard_map/ppermute | solution.py:25
  386.2 10.7 %all_to_all.10 = f32[8,2,4,128]{3,2,1,0:T(4,128)S(1)} all-to-all(f32[8,2,4,128]{3,2,1,0:T(4,128)S(1)} %broadcast_in_dim.59), channel_id=1, replica_groups=mesh['gz'=96,'gy'=8] {'gy'}, dimensions={0} | all-to-all | bytes 65536 | tf_op jit(solution)/shard_map/all_to_all | solution.py:57
  396.9 8.4 %collective-permute-start.70 = (f32[1,32,128]{2,1,0:T(8,128)S(1)}, f32[1,32,128]{2,1,0:T(8,128)S(1)}, u32[]{:S(2)}, u32[]{:S(2)}) collective-permute-start(f32[1,32,128]{2,1,0:T(8,128)S(1)} %multiply_multiply_fusion.2), channel_id=1, source_target_pairs={{8,0},{16,8},{24,16},{32,24},{40,32},{48,40},{56,48},{64,56},{72,6... | collective-permute-start | bytes 49160 | tf_op jit(solution)/shard_map/ppermute | solution.py:44
  410.5 7.7 %collective-permute-start.72 = (f32[1,32,128]{2,1,0:T(8,128)S(1)}, f32[1,32,128]{2,1,0:T(8,128)S(1)}, u32[]{:S(2)}, u32[]{:S(2)}) collective-permute-start(f32[1,32,128]{2,1,0:T(8,128)S(1)} %get-tuple-element.23), channel_id=1, source_target_pairs={{8,0},{16,8},{24,16},{32,24},{40,32},{48,40},{56,48},{64,56},{72,6... | collective-permute-start | bytes 49160 | tf_op jit(solution)/shard_map/ppermute | solution.py:44
  421.4 7.2 %collective-permute-start.74 = (f32[1,32,128]{2,1,0:T(8,128)S(1)}, f32[1,32,128]{2,1,0:T(8,128)S(1)}, u32[]{:S(2)}, u32[]{:S(2)}) collective-permute-start(f32[1,32,128]{2,1,0:T(8,128)S(1)} %get-tuple-element.20), channel_id=1, source_target_pairs={{8,0},{16,8},{24,16},{32,24},{40,32},{48,40},{56,48},{64,56},{72,6... | collective-permute-start | bytes 49160 | tf_op jit(solution)/shard_map/ppermute | solution.py:44
  432.0 7.2 %collective-permute-start.76 = (f32[1,8,256]{2,1,0:T(8,128)S(1)}, f32[1,8,256]{2,1,0:T(8,128)S(1)}, u32[]{:S(2)}, u32[]{:S(2)}) collective-permute-start(f32[1,8,256]{2,1,0:T(8,128)S(1)} %get-tuple-element.117), channel_id=1, source_target_pairs={{8,0},{16,8},{24,16},{32,24},{40,32},{48,40},{56,48},{64,56},{72,6... | collective-permute-start | bytes 24584 | tf_op jit(solution)/shard_map/ppermute | solution.py:25
  484.3 7.0 %collective-permute-start.89 = (f32[3,16,512]{2,1,0:T(8,128)S(1)}, f32[3,16,512]{2,1,0:T(8,128)S(1)}, u32[]{:S(2)}, u32[]{:S(2)}) collective-permute-start(f32[3,16,512]{2,1,0:T(8,128)S(1)} %get-tuple-element.81), channel_id=1, source_target_pairs={{8,0},{16,8},{24,16},{32,24},{40,32},{48,40},{56,48},{64,56},{72,6... | collective-permute-start | bytes 294920 | tf_op jit(solution)/shard_map/ppermute | solution.py:44
  502.7 9.4 %collective-permute-start.92 = (f32[1,16,512]{2,1,0:T(8,128)S(1)}, f32[1,16,512]{2,1,0:T(8,128)S(1)}, u32[]{:S(2)}, u32[]{:S(2)}) collective-permute-start(f32[1,16,512]{2,1,0:T(8,128)S(1)} %get-tuple-element.79), channel_id=1, source_target_pairs={{8,0},{16,8},{24,16},{32,24},{40,32},{48,40},{56,48},{64,56},{72,6... | collective-permute-start | bytes 98312 | tf_op jit(solution)/shard_map/ppermute | solution.py:25
  (365 shorter events, 327.4 us)
Async XLA Ops:
  1.7 24.5 %collective-permute-start = (f32[3,16,512]{2,1,0:T(8,128)S(1)}, f32[3,16,512]{2,1,0:T(8,128)S(1)}, u32[]{:S(2)}, u32[]{:S(2)}) collective-permute-start(f32[3,16,512]{2,1,0:T(8,128)S(1)} %get-tuple-element.101), channel_id=1, source_target_pairs={{0,8},{8,16},{16,24},{24,32},{32,40},{40,48},{48,56},{56,64},{64,7... | collective-permute-start | bytes 294920 | tf_op jit(solution)/shard_map/ppermute | solution.py:43
  7.1 20.0 %collective-permute-start.1 = (f32[3,16,512]{2,1,0:T(8,128)S(1)}, f32[3,16,512]{2,1,0:T(8,128)S(1)}, u32[]{:S(2)}, u32[]{:S(2)}) collective-permute-start(f32[3,16,512]{2,1,0:T(8,128)S(1)} %get-tuple-element.100), channel_id=1, source_target_pairs={{8,0},{16,8},{24,16},{32,24},{40,32},{48,40},{56,48},{64,56},{72,6... | collective-permute-start | bytes 294920 | tf_op jit(solution)/shard_map/ppermute | solution.py:44
  17.0 17.2 %collective-permute-start.4 = (f32[3,16,512]{2,1,0:T(8,128)S(1)}, f32[3,16,512]{2,1,0:T(8,128)S(1)}, u32[]{:S(2)}, u32[]{:S(2)}) collective-permute-start(f32[3,16,512]{2,1,0:T(8,128)S(1)} %get-tuple-element.99), channel_id=1, source_target_pairs={{0,8},{8,16},{16,24},{24,32},{32,40},{40,48},{48,56},{56,64},{64,7... | collective-permute-start | bytes 294920 | tf_op jit(solution)/shard_map/ppermute | solution.py:43
  19.0 16.2 %collective-permute-start.5 = (f32[3,16,512]{2,1,0:T(8,128)S(1)}, f32[3,16,512]{2,1,0:T(8,128)S(1)}, u32[]{:S(2)}, u32[]{:S(2)}) collective-permute-start(f32[3,16,512]{2,1,0:T(8,128)S(1)} %get-tuple-element.98), channel_id=1, source_target_pairs={{8,0},{16,8},{24,16},{32,24},{40,32},{48,40},{56,48},{64,56},{72,6... | collective-permute-start | bytes 294920 | tf_op jit(solution)/shard_map/ppermute | solution.py:44
  27.2 14.6 %collective-permute-start.2 = (f32[10,3,512]{2,1,0:T(4,128)S(1)}, f32[10,3,512]{2,1,0:T(4,128)S(1)}, u32[]{:S(2)}, u32[]{:S(2)}) collective-permute-start(f32[10,3,512]{2,1,0:T(4,128)S(1)} %get-tuple-element.74), channel_id=1, source_target_pairs={{0,1},{1,2},{2,3},{3,4},{4,5},{5,6},{6,7},{7,0},{8,9},{9,10},{10,1... | collective-permute-start | bytes 184328 | tf_op jit(solution)/shard_map/ppermute | solution.py:43
  44.6 31.4 %collective-permute-start.8 = (f32[1,16,512]{2,1,0:T(8,128)S(1)}, f32[1,16,512]{2,1,0:T(8,128)S(1)}, u32[]{:S(2)}, u32[]{:S(2)}) collective-permute-start(f32[1,16,512]{2,1,0:T(8,128)S(1)} %get-tuple-element.97), channel_id=1, source_target_pairs={{8,0},{16,8},{24,16},{32,24},{40,32},{48,40},{56,48},{64,56},{72,6... | collective-permute-start | bytes 98312 | tf_op jit(solution)/shard_map/ppermute | solution.py:25
  53.0 23.0 %collective-permute-start.9 = (f32[1,16,512]{2,1,0:T(8,128)S(1)}, f32[1,16,512]{2,1,0:T(8,128)S(1)}, u32[]{:S(2)}, u32[]{:S(2)}) collective-permute-start(f32[1,16,512]{2,1,0:T(8,128)S(1)} %get-tuple-element.96), channel_id=1, source_target_pairs={{0,8},{8,16},{16,24},{24,32},{32,40},{40,48},{48,56},{56,64},{64,7... | collective-permute-start | bytes 98312 | tf_op jit(solution)/shard_map/ppermute | solution.py:24
  54.9 21.0 %collective-permute-start.10 = (f32[4,1,512]{2,0,1:T(4,128)S(1)}, f32[4,1,512]{2,0,1:T(4,128)S(1)}, u32[]{:S(2)}, u32[]{:S(2)}) collective-permute-start(f32[4,1,512]{2,0,1:T(4,128)S(1)} %copy.236), channel_id=1, source_target_pairs={{1,0},{2,1},{3,2},{4,3},{5,4},{6,5},{7,6},{0,7},{9,8},{10,9},{11,1... | collective-permute-start | bytes 24584 | tf_op jit(solution)/shard_map/ppermute | solution.py:25
  60.2 15.7 %collective-permute-start.11 = (f32[4,1,512]{2,0,1:T(4,128)S(1)}, f32[4,1,512]{2,0,1:T(4,128)S(1)}, u32[]{:S(2)}, u32[]{:S(2)}) collective-permute-start(f32[4,1,512]{2,0,1:T(4,128)S(1)} %copy.238), channel_id=1, source_target_pairs={{0,1},{1,2},{2,3},{3,4},{4,5},{5,6},{6,7},{7,0},{8,9},{9,10},{10,1... | collective-permute-start | bytes 24584 | tf_op jit(solution)/shard_map/ppermute | solution.py:24
  89.9 15.7 %collective-permute-start.12 = (f32[1,8,256]{2,1,0:T(8,128)S(1)}, f32[1,8,256]{2,1,0:T(8,128)S(1)}, u32[]{:S(2)}, u32[]{:S(2)}) collective-permute-start(f32[1,8,256]{2,1,0:T(8,128)S(1)} %get-tuple-element.181), channel_id=1, source_target_pairs={{8,0},{16,8},{24,16},{32,24},{40,32},{48,40},{56,48},{64,56},{72,6... | collective-permute-start | bytes 24584 | tf_op jit(solution)/shard_map/ppermute | solution.py:25
  105.8 16.1 %collective-permute-start.16 = (f32[1,8,256]{2,1,0:T(8,128)S(1)}, f32[1,8,256]{2,1,0:T(8,128)S(1)}, u32[]{:S(2)}, u32[]{:S(2)}) collective-permute-start(f32[1,8,256]{2,1,0:T(8,128)S(1)} %get-tuple-element.177), channel_id=1, source_target_pairs={{8,0},{16,8},{24,16},{32,24},{40,32},{48,40},{56,48},{64,56},{72,6... | collective-permute-start | bytes 24584 | tf_op jit(solution)/shard_map/ppermute | solution.py:25
  122.0 16.9 %collective-permute-start.20 = (f32[1,8,256]{2,1,0:T(8,128)S(1)}, f32[1,8,256]{2,1,0:T(8,128)S(1)}, u32[]{:S(2)}, u32[]{:S(2)}) collective-permute-start(f32[1,8,256]{2,1,0:T(8,128)S(1)} %get-tuple-element.171), channel_id=1, source_target_pairs={{8,0},{16,8},{24,16},{32,24},{40,32},{48,40},{56,48},{64,56},{72,6... | collective-permute-start | bytes 24584 | tf_op jit(solution)/shard_map/ppermute | solution.py:25
  188.0 16.7 %collective-permute-start.30 = (f32[1,8,256]{2,1,0:T(8,128)S(1)}, f32[1,8,256]{2,1,0:T(8,128)S(1)}, u32[]{:S(2)}, u32[]{:S(2)}) collective-permute-start(f32[1,8,256]{2,1,0:T(8,128)S(1)} %get-tuple-element.154), channel_id=1, source_target_pairs={{8,0},{16,8},{24,16},{32,24},{40,32},{48,40},{56,48},{64,56},{72,6... | collective-permute-start | bytes 24584 | tf_op jit(solution)/shard_map/ppermute | solution.py:25
  204.8 13.3 %collective-permute-start.34 = (f32[1,8,256]{2,1,0:T(8,128)S(1)}, f32[1,8,256]{2,1,0:T(8,128)S(1)}, u32[]{:S(2)}, u32[]{:S(2)}) collective-permute-start(f32[1,8,256]{2,1,0:T(8,128)S(1)} %get-tuple-element.150), channel_id=1, source_target_pairs={{8,0},{16,8},{24,16},{32,24},{40,32},{48,40},{56,48},{64,56},{72,6... | collective-permute-start | bytes 24584 | tf_op jit(solution)/shard_map/ppermute | solution.py:25
  218.2 15.7 %collective-permute-start.38 = (f32[1,8,256]{2,1,0:T(8,128)S(1)}, f32[1,8,256]{2,1,0:T(8,128)S(1)}, u32[]{:S(2)}, u32[]{:S(2)}) collective-permute-start(f32[1,8,256]{2,1,0:T(8,128)S(1)} %get-tuple-element.146), channel_id=1, source_target_pairs={{8,0},{16,8},{24,16},{32,24},{40,32},{48,40},{56,48},{64,56},{72,6... | collective-permute-start | bytes 24584 | tf_op jit(solution)/shard_map/ppermute | solution.py:25
  258.8 22.2 %collective-permute-start.46 = (f32[1,16,512]{2,1,0:T(8,128)S(1)}, f32[1,16,512]{2,1,0:T(8,128)S(1)}, u32[]{:S(2)}, u32[]{:S(2)}) collective-permute-start(f32[1,16,512]{2,1,0:T(8,128)S(1)} %get-tuple-element.91), channel_id=1, source_target_pairs={{8,0},{16,8},{24,16},{32,24},{40,32},{48,40},{56,48},{64,56},{72,6... | collective-permute-start | bytes 98312 | tf_op jit(solution)/shard_map/ppermute | solution.py:25
  300.1 22.2 %collective-permute-start.54 = (f32[1,16,512]{2,1,0:T(8,128)S(1)}, f32[1,16,512]{2,1,0:T(8,128)S(1)}, u32[]{:S(2)}, u32[]{:S(2)}) collective-permute-start(f32[1,16,512]{2,1,0:T(8,128)S(1)} %get-tuple-element.85), channel_id=1, source_target_pairs={{8,0},{16,8},{24,16},{32,24},{40,32},{48,40},{56,48},{64,56},{72,6... | collective-permute-start | bytes 98312 | tf_op jit(solution)/shard_map/ppermute | solution.py:25
  336.3 16.5 %collective-permute-start.58 = (f32[1,8,256]{2,1,0:T(8,128)S(1)}, f32[1,8,256]{2,1,0:T(8,128)S(1)}, u32[]{:S(2)}, u32[]{:S(2)}) collective-permute-start(f32[1,8,256]{2,1,0:T(8,128)S(1)} %get-tuple-element.142), channel_id=1, source_target_pairs={{8,0},{16,8},{24,16},{32,24},{40,32},{48,40},{56,48},{64,56},{72,6... | collective-permute-start | bytes 24584 | tf_op jit(solution)/shard_map/ppermute | solution.py:25
  352.8 16.1 %collective-permute-start.62 = (f32[1,8,256]{2,1,0:T(8,128)S(1)}, f32[1,8,256]{2,1,0:T(8,128)S(1)}, u32[]{:S(2)}, u32[]{:S(2)}) collective-permute-start(f32[1,8,256]{2,1,0:T(8,128)S(1)} %get-tuple-element.138), channel_id=1, source_target_pairs={{8,0},{16,8},{24,16},{32,24},{40,32},{48,40},{56,48},{64,56},{72,6... | collective-permute-start | bytes 24584 | tf_op jit(solution)/shard_map/ppermute | solution.py:25
  369.1 16.4 %collective-permute-start.66 = (f32[1,8,256]{2,1,0:T(8,128)S(1)}, f32[1,8,256]{2,1,0:T(8,128)S(1)}, u32[]{:S(2)}, u32[]{:S(2)}) collective-permute-start(f32[1,8,256]{2,1,0:T(8,128)S(1)} %get-tuple-element.134), channel_id=1, source_target_pairs={{8,0},{16,8},{24,16},{32,24},{40,32},{48,40},{56,48},{64,56},{72,6... | collective-permute-start | bytes 24584 | tf_op jit(solution)/shard_map/ppermute | solution.py:25
  432.0 16.7 %collective-permute-start.76 = (f32[1,8,256]{2,1,0:T(8,128)S(1)}, f32[1,8,256]{2,1,0:T(8,128)S(1)}, u32[]{:S(2)}, u32[]{:S(2)}) collective-permute-start(f32[1,8,256]{2,1,0:T(8,128)S(1)} %get-tuple-element.117), channel_id=1, source_target_pairs={{8,0},{16,8},{24,16},{32,24},{40,32},{48,40},{56,48},{64,56},{72,6... | collective-permute-start | bytes 24584 | tf_op jit(solution)/shard_map/ppermute | solution.py:25
  448.8 13.3 %collective-permute-start.80 = (f32[1,8,256]{2,1,0:T(8,128)S(1)}, f32[1,8,256]{2,1,0:T(8,128)S(1)}, u32[]{:S(2)}, u32[]{:S(2)}) collective-permute-start(f32[1,8,256]{2,1,0:T(8,128)S(1)} %get-tuple-element.113), channel_id=1, source_target_pairs={{8,0},{16,8},{24,16},{32,24},{40,32},{48,40},{56,48},{64,56},{72,6... | collective-permute-start | bytes 24584 | tf_op jit(solution)/shard_map/ppermute | solution.py:25
  462.2 15.7 %collective-permute-start.84 = (f32[1,8,256]{2,1,0:T(8,128)S(1)}, f32[1,8,256]{2,1,0:T(8,128)S(1)}, u32[]{:S(2)}, u32[]{:S(2)}) collective-permute-start(f32[1,8,256]{2,1,0:T(8,128)S(1)} %get-tuple-element.109), channel_id=1, source_target_pairs={{8,0},{16,8},{24,16},{32,24},{40,32},{48,40},{56,48},{64,56},{72,6... | collective-permute-start | bytes 24584 | tf_op jit(solution)/shard_map/ppermute | solution.py:25
  502.7 22.2 %collective-permute-start.92 = (f32[1,16,512]{2,1,0:T(8,128)S(1)}, f32[1,16,512]{2,1,0:T(8,128)S(1)}, u32[]{:S(2)}, u32[]{:S(2)}) collective-permute-start(f32[1,16,512]{2,1,0:T(8,128)S(1)} %get-tuple-element.79), channel_id=1, source_target_pairs={{8,0},{16,8},{24,16},{32,24},{40,32},{48,40},{56,48},{64,56},{72,6... | collective-permute-start | bytes 98312 | tf_op jit(solution)/shard_map/ppermute | solution.py:25
  (81 other events, 739.6 us)
where the time goes:
time: 530 us; the launch traced here: 526 us
  starting transfers between devices  380 us (72%)
  waiting for transfers between devices  64.4 us (12%)
  local copies, waits for them, and re-layouts  43.4 us (8%)
  other arithmetic  24.4 us (5%)
  blocking collectives  10.7 us (2%)
    ppermute x32, starting transfers between devices, extended(): lax.ppermute(first, axis, [(b, a) for a, b in up])  155 us
    ppermute x16, starting transfers between devices, padded_2(): after = lax.ppermute(first, axis, down)  105 us
    ppermute x32, starting transfers between devices, extended(): lax.ppermute(last, axis, up)  77.3 us
    ppermute x32, waiting for transfers between devices, extended(): lax.ppermute(last, axis, up)  38.7 us
    ppermute x16, starting transfers between devices, padded_2(): before = lax.ppermute(last, axis, up)  36.4 us
    reshape x3, local copies, waits for them, and re-layouts, restrict(): return field.reshape(z // 2, 2, y // 2, 2, x // 2, 2).mean(axis=(1, 3, 5))  29.3 us
    reduce_sum x9, other arithmetic, restrict(): return field.reshape(z // 2, 2, y // 2, 2, x // 2, 2).mean(axis=(1, 3, 5))  12.7 us
    all_to_all x1, blocking collectives, from_everyone(): return lax.all_to_all(copies, axis, split_axis=0, concat_axis=0, tiled=True)  10.7 us
  transfers between devices with their start and end apart: 97, of which 29 were waited for; matrix products, arithmetic and copies ran while one was open for 3% of the time, Pallas kernels for 0%

commit v1 on v0

v1 whole, which is shorter than its diff:
```python
import functools

import jax
import jax.numpy as jnp
from jax import lax
from jax.experimental import pallas as pl
from jax.experimental.pallas import tpu as pltpu
from jax.sharding import PartitionSpec as P

DEGREE = 3
COARSE_DEGREE = 4
CYCLES = 2

CHEB_LOW = 0.3
CHEB_HIGH = 1.9
SCALES = (4.0, 1.0, 0.25)
LANES = 128
VMEM_LIMIT = 48 * 1024 * 1024


def chebyshev(steps):
    theta = (CHEB_HIGH + CHEB_LOW) / 2.0
    delta = (CHEB_HIGH - CHEB_LOW) / 2.0
    sigma = theta / delta
    rho = 1.0 / sigma
    pairs = [(0.0, 1.0 / theta)]
    for _ in range(steps - 1):
        rho_next = 1.0 / (2.0 * sigma - rho)
        pairs.append((rho_next * rho, 2.0 * rho_next / delta))
        rho = rho_next
    return pairs


def lanes(c):
    return slice(c * LANES, (c + 1) * LANES)


def load(ref, z, size):
    return [[ref[z, d, :, lanes(c)] for c in range(size)] for d in range(size)]


def load_ends(ref, z, size):
    top = ref.shape[2]
    return [
        [
            jnp.concatenate([ref[z, d, 0:8, lanes(c)], ref[z, d, top - 8 : top, lanes(c)]], axis=0)
            for c in range(size)
        ]
        for d in range(size)
    ]


def neighbours(below, here, above, size):
    rows = here[0][0].shape[0]
    lane = lax.broadcasted_iota(jnp.int32, (rows, LANES), 1)
    first, last = lane == 0, lane == LANES - 1
    out = []
    for d in range(size):
        line = []
        for c in range(size):
            if c > 0:
                left = here[d][c - 1]
            else:
                left = jnp.where(first, 0.0, pltpu.roll(here[d][size - 1], 1, 1))
            if c < size - 1:
                right = here[d][c + 1]
            else:
                right = jnp.where(last, 0.0, pltpu.roll(here[d][0], LANES - 1, 1))
            low = here[d - 1][c] if d > 0 else pltpu.roll(here[size - 1][c], 1, 0)
            high = here[d + 1][c] if d < size - 1 else pltpu.roll(here[0][c], rows - 1, 0)
            line.append(((below[d][c] + above[d][c]) + (left + right)) + (low + high))
        out.append(line)
    return out


def first_step(lo, hi, rhs, inv, w, dw, size, beta):
    def body(z, carry):
        for d in range(size):
            for c in range(size):
                value = (beta * rhs[z, d, :, lanes(c)]) * inv[z, d, :, lanes(c)]
                w[z, d, :, lanes(c)] = value
                dw[z, d, :, lanes(c)] = value
        return carry

    lax.fori_loop(lo, hi, body, 0)


def sweep(lo, hi, src, dst, dst_shift, dw, rhs, inv, shift, size, scale, alpha, beta, loader=load):
    def body(z, carry):
        here = load(src, z, size)
        near = neighbours(load(src, z - 1, size), here, load(src, z + 1, size), size)
        f = loader(rhs, z + shift, size)
        i = loader(inv, z + shift, size)
        for d in range(size):
            for c in range(size):
                q = i[d][c] * (f[d][c] + scale * near[d][c]) - here[d][c]
                change = beta * q
                if alpha != 0.0:
                    change = change + alpha * dw[z, d, :, lanes(c)]
                dw[z, d, :, lanes(c)] = change
                dst[z + dst_shift, d, :, lanes(c)] = here[d][c] + change
        return carry

    lax.fori_loop(lo, hi, body, 0)


def residual_plane(src, z, rhs, inv, zr, size, scale):
    here = load(src, z, size)
    near = neighbours(load(src, z - 1, size), here, load(src, z + 1, size), size)
    out = []
    for d in range(size):
        line = []
        for c in range(size):
            i = inv[zr, d, :, lanes(c)]
            line.append((rhs[zr, d, :, lanes(c)] + scale * near[d][c]) - here[d][c] / i)
        out.append(line)
    return out


def halve(one, two, size):
    half = size // 2
    return [
        [
            0.125
            * (
                ((one[2 * d][2 * c] + one[2 * d][2 * c + 1]) + (one[2 * d + 1][2 * c] + one[2 * d + 1][2 * c + 1]))
                + ((two[2 * d][2 * c] + two[2 * d][2 * c + 1]) + (two[2 * d + 1][2 * c] + two[2 * d + 1][2 * c + 1]))
            )
            for c in range(half)
        ]
        for d in range(half)
    ]


def inverse_of(cond, scale):
    return 1.0 / (1.0 / cond + 6.0 * scale)


def selector(to_tiles):
    rows = lax.broadcasted_iota(jnp.int32, (512, 512), 0)
    cols = lax.broadcasted_iota(jnp.int32, (512, 512), 1)
    if to_tiles:
        hit = rows == 4 * (cols % LANES) + cols // LANES
    else:
        hit = cols == 4 * (rows % LANES) + rows // LANES
    return jnp.where(hit, 1.0, 0.0).astype(jnp.float32)


def reorder(rows, to_tiles):
    return jnp.dot(
        rows, selector(to_tiles), precision=lax.Precision.HIGHEST, preferred_element_type=jnp.float32
    )


def prepare_kernel(source, cond, out, work):
    rows = jnp.concatenate([source[...].reshape(64, 512), cond[...].reshape(64, 512)], axis=0)
    tiles = reorder(rows, True)
    for c in range(4):
        work[c] = tiles[:, lanes(c)]
    for a in range(2):
        for z in range(4):
            for d in range(4):
                for c in range(4):
                    out[z, 4 * a + d, :, lanes(c)] = work[c, pl.ds(64 * a + 16 * z + d, 4, stride=4), :]


def finish_kernel(adjoint, remain, out_a, out_r, work):
    for a, ref in enumerate((adjoint, remain)):
        for z in range(4):
            for d in range(4):
                for c in range(4):
                    work[c, pl.ds(64 * a + 16 * z + d, 4, stride=4), :] = ref[z, d, :, lanes(c)]
    rows = reorder(jnp.concatenate([work[c] for c in range(4)], axis=1), False)
    out_a[...] = rows[0:64].reshape(4, 16, 512)
    out_r[...] = rows[64:128].reshape(4, 16, 512)


def fine_down_kernel(first, prm, chip, side, more, *refs):
    if first:
        rhs, field, low, cond, inv, wa, wb, dw = refs
    else:
        inv, rhs, field, low, wa, wb, dw = refs
    core = prm[0]

    def put(t, ref, *index):
        rhs[t] = ref[(*index, slice(0, 4))]
        if first:
            cond[t] = ref[(*index, slice(4, 8))]

    @pl.when(core == 0)
    def _():
        for t in range(6):
            put(t, side, 0, t)
        for t in range(8):
            put(6 + t, chip, t // 4, t % 4)
        for t in range(2):
            put(14 + t, more, 1, t)

    @pl.when(core == 1)
    def _():
        for t in range(2):
            put(t, more, 0, t)
        for t in range(8):
            put(2 + t, chip, t // 4, t % 4)
        for t in range(6):
            put(10 + t, side, 1, t)

    if first:

        def fill(t, carry):
            inv[t] = inverse_of(cond[t], SCALES[0])
            return carry

        lax.fori_loop(0, 16, fill, 0)
    steps = chebyshev(DEGREE)
    first_step(0, 16, rhs, inv, wa, dw, 4, steps[0][1])
    sweep(1, 15, wa, wb, 0, dw, rhs, inv, 0, 4, SCALES[0], *steps[1])
    sweep(2, 14, wb, field, -2, dw, rhs, inv, 0, 4, SCALES[0], *steps[2])
    for t in range(2):
        z = 6 + 2 * t
        one = residual_plane(field, z - 2, rhs, inv, z, 4, SCALES[0])
        two = residual_plane(field, z - 1, rhs, inv, z + 1, 4, SCALES[0])
        mean = halve(one, two, 4)
        for d in range(2):
            for c in range(2):
                low[0, t, d, :, lanes(c)] = mean[d][c][0:4]
        if first:
            mean = halve(load(cond, z, 4), load(cond, z + 1, 4), 4)
            for d in range(2):
                for c in range(2):
                    low[1, t, d, :, lanes(c)] = mean[d][c][0:4]


def middle_down_kernel(first, prm, chip, far, *refs):
    if first:
        rhs, field, low, cond, inv, wa, wb, dw = refs
    else:
        inv, rhs, field, low, wa, wb, dw = refs
    core, me = prm[0], prm[1]
    for j in range(8):
        y = lax.rem(me + j, 8)
        for t in range(12):
            if t < 4:
                ref, index = far, (0, t // 2, y)
            elif t < 8:
                ref, index = chip, ((t - 4) // 2, y)
            else:
                ref, index = far, (1, (t - 8) // 2, y)
            for d in range(2):
                rhs[t, d, 4 * j : 4 * j + 4, :] = ref[(*index, 0, t % 2, d)]
                if first:
                    cond[t, d, 4 * j : 4 * j + 4, :] = ref[(*index, 1, t % 2, d)]
    if first:

        def fill(t, carry):
            inv[t] = inverse_of(cond[t], SCALES[1])
            return carry

        lax.fori_loop(0, 12, fill, 0)
    steps = chebyshev(DEGREE)
    first_step(0, 12, rhs, inv, wa, dw, 2, steps[0][1])
    sweep(1, 11, wa, wb, 0, dw, rhs, inv, 0, 2, SCALES[1], *steps[1])
    sweep(2, 10, wb, field, -2, dw, rhs, inv, 0, 2, SCALES[1], *steps[2])
    z = 4 + 2 * core
    one = residual_plane(field, z - 2, rhs, inv, z, 2, SCALES[1])
    two = residual_plane(field, z - 1, rhs, inv, z + 1, 2, SCALES[1])
    low[0] = halve(one, two, 2)[0][0]
    if first:
        low[1] = halve(load(cond, z, 2), load(cond, z + 1, 2), 2)[0][0]


def coarse_kernel(first, prm, block, far, middle, mid_cond, *refs):
    if first:
        start, send, cond, inv, rhs, wa, wb, dw = refs
    else:
        cond, inv, start, send, rhs, wa, wb, dw = refs
    core, half = prm[0], prm[2]
    for t in range(12):
        if t < 4:
            ref, index = far, (0, t)
        elif t < 8:
            ref, index = block, (t - 4,)
        else:
            ref, index = far, (3, t - 8)
        rhs[t, 0] = ref[(*index, 0)]
        if first:
            value = ref[(*index, 1)]
            cond[t, 0] = value
            inv[t, 0] = inverse_of(value, SCALES[2])
    steps = chebyshev(COARSE_DEGREE)
    first_step(0, 12, rhs, inv, wa, dw, 1, steps[0][1])
    sweep(1, 11, wa, wb, 0, dw, rhs, inv, 0, 1, SCALES[2], *steps[1])
    sweep(2, 10, wb, wa, 0, dw, rhs, inv, 0, 1, SCALES[2], *steps[2])
    sweep(3, 9, wa, wb, 0, dw, rhs, inv, 0, 1, SCALES[2], *steps[3])
    for u in range(8):
        t = 3 + 2 * half + u // 2
        value = wb[t, 0] / cond[t, 0]
        value = jnp.concatenate([value[0:8], value[24:32]], axis=0)
        k = load_ends(mid_cond, u + 2, 2)
        w = load_ends(middle, u, 2)
        for d in range(2):
            for c in range(2):
                start[u, d, :, lanes(c)] = w[d][c] + k[d][c] * value
    for t in range(3):
        send[t] = start[4 - 3 * core + t]


def up_kernel(last, prm, start, side, more, mid_rhs, mid_cond, mid_inv, rhs, fine, cond, inv, *refs):
    if last:
        before, adjoint, remain, mid_a, mid_b, mid_dw, wa, wb, dw = refs
    else:
        adjoint, remain, mid_a, mid_b, mid_dw, wa, wb, dw = refs
    core = prm[0]

    @pl.when(core == 0)
    def _():
        for t in range(3):
            mid_a[t] = side[0, t]
        for t in range(8):
            mid_a[3 + t] = start[t]
        mid_a[11] = more[1]

    @pl.when(core == 1)
    def _():
        mid_a[0] = more[0]
        for t in range(8):
            mid_a[1 + t] = start[t]
        for t in range(3):
            mid_a[9 + t] = side[1, t]

    steps = chebyshev(DEGREE)
    shift = 2 * core - 1
    sweep(1, 11, mid_a, mid_b, 0, mid_dw, mid_rhs, mid_inv, shift, 2, SCALES[1], *steps[0], loader=load_ends)
    sweep(2, 10, mid_b, mid_a, 0, mid_dw, mid_rhs, mid_inv, shift, 2, SCALES[1], *steps[1], loader=load_ends)
    sweep(3, 9, mid_a, mid_b, 0, mid_dw, mid_rhs, mid_inv, shift, 2, SCALES[1], *steps[2], loader=load_ends)

    near = lax.broadcasted_iota(jnp.int32, (8, LANES), 0) < 6

    def correct(t, carry):
        k = load_ends(mid_cond, t + shift, 2)
        for d in range(2):
            for c in range(2):
                value = mid_b[t, d, :, lanes(c)] / k[d][c]
                value = jnp.where(near, value[0:8], value[8:16])
                for z in range(2):
                    v = 2 * (t - 3) + z
                    for dd in (2 * d, 2 * d + 1):
                        for cc in (2 * c, 2 * c + 1):
                            wa[v, dd, :, lanes(cc)] = fine[v, dd, :, lanes(cc)] + cond[v + 2, dd, :, lanes(cc)] * value
        return carry

    lax.fori_loop(3, 9, correct, 0)
    sweep(1, 11, wa, wb, 0, dw, rhs, inv, 2, 4, SCALES[0], *steps[0])
    sweep(2, 10, wb, wa, 0, dw, rhs, inv, 2, 4, SCALES[0], *steps[1])
    sweep(3, 9, wa, wb, 0, dw, rhs, inv, 2, 4, SCALES[0], *steps[2])

    def finish(t, carry):
        left = residual_plane(wb, t + 4, rhs, inv, t + 6, 4, SCALES[0])
        for d in range(4):
            for c in range(4):
                value = wb[t + 4, d, :, lanes(c)] / cond[t + 6, d, :, lanes(c)]
                value = value[0:4]
                if last:
                    value = value + before[t, d, :, lanes(c)]
                adjoint[t, d, :, lanes(c)] = value
                remain[t, d, :, lanes(c)] = left[d][c][0:4]
        return carry

    lax.fori_loop(0, 4, finish, 0)


def f32(*shape):
    return jax.ShapeDtypeStruct(shape, jnp.float32)


def call(body, outs, scratch, *args, scalars=True, name=None):
    specs = [pl.BlockSpec(memory_space=pltpu.VMEM)] * len(args)
    if scalars:
        specs[0] = pl.BlockSpec(memory_space=pltpu.SMEM)
    return pl.pallas_call(
        body,
        out_shape=outs,
        in_specs=specs,
        out_specs=[pl.BlockSpec(memory_space=pltpu.VMEM)] * len(outs),
        scratch_shapes=[pltpu.VMEM(s, jnp.float32) for s in scratch],
        compiler_params=pltpu.CompilerParams(vmem_limit_bytes=VMEM_LIMIT),
        name=name,
    )(*args)


def groups(axis, size, shift):
    devices = lax.axis_size(axis)
    return [[(g * size + i + shift) % devices for i in range(size)] for g in range(devices // size)]


def gather(value, size, shift):
    return lax.all_gather(value, "gz", axis_index_groups=groups("gz", size, shift))


def row_halo(own):
    devices = lax.axis_size("gy")
    up = [(i, (i + 1) % devices) for i in range(devices)]
    down = [(j, i) for i, j in up]
    after = lax.ppermute(own[:, :, 0:2], "gy", down)
    before = lax.ppermute(own[:, :, 2:4], "gy", up)
    return jnp.concatenate([own, after, before], axis=2)


def local(source, conduct):
    z = lax.axis_index("gz")
    y = lax.axis_index("gy")
    core = z % 2
    prm = jnp.stack([core, y, (z % 4) // 2, 0]).astype(jnp.int32)
    (remain,) = call(
        prepare_kernel, [f32(4, 8, 4, 512)], [(4, 128, 128)], source, conduct, scalars=False, name="prepare"
    )
    adjoint = None
    kept = None
    for cycle in range(CYCLES):
        first, last = cycle == 0, cycle == CYCLES - 1
        parts = 2 if first else 1
        own = row_halo(remain)
        chip = gather(own, 2, 0)
        whole = chip.reshape(8, *chip.shape[2:])
        side = gather(lax.dynamic_slice_in_dim(whole, 2 * core, 6, 0), 2, 1)
        flat = side.reshape(12, *side.shape[2:])
        more = gather(lax.dynamic_slice_in_dim(flat, 4 + 2 * core, 2, 0), 2, 0)
        outs = [f32(16, 4, 8, 512), f32(12, 4, 8, 512), f32(parts, 2, 2, 4, 256)]
        state = [f32(16, 4, 8, 512)] * 2
        scratch = [(16, 4, 8, 512)] * 3
        body = functools.partial(fine_down_kernel, first)
        if first:
            rhs0, field0, low, cond0, inv0 = call(
                body, outs + state, scratch, prm, chip, side, more, name="fine_down_first"
            )
        else:
            cond0, inv0 = kept[0:2]
            rhs0, field0, low = call(body, outs, scratch, prm, chip, side, more, inv0, name="fine_down")
        copies = jnp.broadcast_to(low, (lax.axis_size("gy"), *low.shape))
        rows = lax.all_to_all(copies, "gy", split_axis=0, concat_axis=0, tiled=True)
        chip = gather(rows, 2, 0)
        side = gather(chip, 2, 1)
        far = gather(lax.dynamic_index_in_dim(side, core, 0, keepdims=False), 2, 0)
        outs = [f32(12, 2, 32, 256), f32(8, 2, 32, 256), f32(parts, 32, 128)]
        state = [f32(12, 2, 32, 256)] * 2
        scratch = [(12, 2, 32, 256)] * 3
        body = functools.partial(middle_down_kernel, first)
        if first:
            rhs1, field1, low, cond1, inv1 = call(
                body, outs + state, scratch, prm, chip, far, name="middle_down_first"
            )
        else:
            cond1, inv1 = kept[2:4]
            rhs1, field1, low = call(body, outs, scratch, prm, chip, far, inv1, name="middle_down")
        block = gather(low, 4, 0)
        side = gather(block, 4, 2)
        half = prm[2]
        far = gather(lax.dynamic_index_in_dim(side, 2 * half, 0, keepdims=False), 4, 0)
        outs = [f32(8, 2, 16, 256), f32(3, 2, 16, 256)]
        state = [f32(12, 1, 32, 128)] * 2
        scratch = [(12, 1, 32, 128)] * 4
        body = functools.partial(coarse_kernel, first)
        if first:
            start, send, cond2, inv2 = call(
                body, outs + state, scratch, prm, block, far, field1, cond1, name="coarse_first"
            )
        else:
            cond2, inv2 = kept[4:6]
            start, send = call(
                body, outs, scratch, prm, block, far, field1, cond1, cond2, inv2, name="coarse"
            )
        side = gather(send, 2, 1)
        flat = side.reshape(6, *side.shape[2:])
        more = gather(lax.dynamic_index_in_dim(flat, 2 + core, 0, keepdims=False), 2, 0)
        outs = [f32(4, 4, 4, 512)] * 2
        scratch = [(12, 2, 16, 256)] * 3 + [(12, 4, 8, 512)] * 3
        args = [prm, start, side, more, rhs1, cond1, inv1, rhs0, field0, cond0, inv0]
        if last:
            args.append(adjoint)
        adjoint, remain = call(functools.partial(up_kernel, last), outs, scratch, *args, name="up")
        kept = (cond0, inv0, cond1, inv1, cond2, inv2)
    return tuple(
        call(
            finish_kernel,
            [f32(4, 16, 512)] * 2,
            [(4, 128, 128)],
            adjoint,
            remain,
            scalars=False,
            name="finish",
        )
    )


def solution(mesh):
    placed = (P("gz", "gy", None), P("gz", "gy", None))
    return jax.shard_map(local, mesh=mesh, in_specs=placed, out_specs=placed, check_vma=False)
```

time: 530 us -> 319 us (0.60)
  starting transfers between devices: 380 us -> 14.4 us
  blocking collectives: 10.7 us -> 136 us
  waiting for transfers between devices: 64.4 us -> 107 us
  Pallas kernels: 0 us -> 33.5 us
  local copies, waits for them, and re-layouts: 43.4 us -> 12.1 us
  other arithmetic: 24.4 us -> 1.14 us
  between operations: 2.79 us -> 14.1 us
    ppermute x96 -> x4, starting transfers between devices: 374 us -> 14.2 us  [the longest x2 10.4 us: row_halo(): after = lax.ppermute(own[:, :, 0:2], 'gy', down)]
    all_gather x0 -> x18, blocking collectives: none -> 107 us  [gather(): lax.all_gather(value, 'gz', axis_index_groups=groups('gz', size, shift))]
    all_gather x0 -> x4, waiting for transfers between devices: none -> 97.5 us  [gather(): lax.all_gather(value, 'gz', axis_index_groups=groups('gz', size, shift))]
    ppermute x96 -> x4, waiting for transfers between devices: 57.6 us -> 9.27 us  [the longest x2 9.27 us: row_halo(): before = lax.ppermute(own[:, :, 2:4], 'gy', up)]
    pallas_call x0 -> x10, Pallas kernels: none -> 33.5 us  [call(): pl.pallas_call(body, out_shape=outs, in_specs=specs, out_specs=[pl.BlockS...]
    reshape x9 -> x0, local copies, waits for them, and re-layouts: 33.3 us -> none  [the longest x3 29.3 us: restrict(): return field.reshape(z // 2, 2, y // 2, 2, x // 2, 2).mean(axis=(1, 3, 5))]
    all_to_all x1 -> x2, blocking collectives: 10.7 us -> 29.2 us  [local(): rows = lax.all_to_all(copies, 'gy', split_axis=0, concat_axis=0, tiled=True)]
    reduce_sum x9 -> x0, other arithmetic: 12.7 us -> none  [restrict(): return field.reshape(z // 2, 2, y // 2, 2, x // 2, 2).mean(axis=(1, 3, 5))]
  transfers between devices with their start and end apart: 97 -> 8, of which waited for: 29 -> 6; matrix products, arithmetic and copies ran while one was open for 3% -> 0% of each run, Pallas kernels for 0% -> 0%
where the time goes in v1:
time: 319 us; the launch traced here: 318 us
  blocking collectives  136 us (43%)
  waiting for transfers between devices  107 us (34%)
  Pallas kernels  33.5 us (11%)
  starting transfers between devices  14.4 us (5%)
  between operations  14.1 us (4%)
  local copies, waits for them, and re-layouts  12.1 us (4%)
    all_gather x18, blocking collectives, gather(): lax.all_gather(value, 'gz', axis_index_groups=groups('gz', size, shift))  107 us
    all_gather x4, waiting for transfers between devices, gather(): lax.all_gather(value, 'gz', axis_index_groups=groups('gz', size, shift))  97.5 us
    pallas_call x10, Pallas kernels, call(): pl.pallas_call(body, out_shape=outs, in_specs=specs, out_specs=[pl.BlockS...  33.5 us
    all_to_all x2, blocking collectives, local(): rows = lax.all_to_all(copies, 'gy', split_axis=0, concat_axis=0, tiled=True)  29.2 us
    ppermute x2, starting transfers between devices, row_halo(): after = lax.ppermute(own[:, :, 0:2], 'gy', down)  10.4 us
    ppermute x2, waiting for transfers between devices, row_halo(): before = lax.ppermute(own[:, :, 2:4], 'gy', up)  9.27 us
  transfers between devices with their start and end apart: 8, of which 6 were waited for; matrix products, arithmetic and copies ran while one was open for 0% of the time, Pallas kernels for 0%

profile of v1, /device:TPU:1, one launch (start us, length us, event | category | flops | bytes accessed | tf_op | source)
XLA Modules:
  0.0 317.8 jit_solution(17059087923146954964)
XLA Ops:
  9.9 5.9 %collective-permute-start = (f32[4,8,2,512]{3,2,1,0:T(2,128)S(1)}, f32[4,8,2,512]{3,2,1,0:T(2,128)S(1)}, u32[]{:S(2)}, u32[]{:S(2)}) collective-permute-start(f32[4,8,2,512]{3,2,1,0:T(2,128)S(1)} %get-tuple-element.54), channel_id=1, source_target_pairs={{1,0},{2,1},{3,2},{4,3},{5,4},{6,5},{7,6},{0,7},{9,8},{10,9},{11,1... | collective-permute-start | bytes 393224 | tf_op jit(solution)/shard_map/ppermute | solution.py:404
  17.8 5.0 %collective-permute-done.1 = f32[4,8,2,512]{3,2,1,0:T(2,128)S(1)} collective-permute-done((f32[4,8,2,512]{3,2,1,0:T(2,128)S(1)}, f32[4,8,2,512]{3,2,1,0:T(2,128)S(1)}, u32[]{:S(2)}, u32[]{:S(2)}) %collective-permute-start.1) | collective-permute-done | bytes 131104 | tf_op jit(solution)/shard_map/ppermute | solution.py:405
  23.9 27.3 %all-gather.23.cloned.1.call-done = f32[8,8,8,512]{3,2,1,0:T(8,128)} async-done(((f32[4,8,8,512]{3,2,1,0:T(8,128)}), f32[8,8,8,512]{3,2,1,0:T(8,128)}) %all-gather.23.cloned.1.call-update) | async-done | bytes 1048592 | tf_op jit(solution)/shard_map/all_gather | solution.py:397
  53.6 29.4 %all-gather.25.cloned.1.call-done = f32[12,8,8,512]{3,2,1,0:T(8,128)} async-done(((f32[6,8,8,512]{3,2,1,0:T(8,128)}), f32[12,8,8,512]{3,2,1,0:T(8,128)}) %all-gather.25.cloned.1.call-update) | async-done | bytes 1572880 | tf_op jit(solution)/shard_map/all_gather | solution.py:397
  84.0 6.9 %all-gather.2 = f32[4,8,8,512]{3,2,1,0:T(8,128)S(1)} all-gather(f32[2,8,8,512]{3,2,1,0:T(8,128)S(1)} %constant_dynamic-slice_fusion.8), channel_id=4, replica_groups={{0,8},{16,24},{32,40},{48,56},{64,72},{80,88},{96,104},{112,120},{128,1..., dimensions={0}, use_global_device_ids=true | all-gather | bytes 786432 | tf_op jit(solution)/shard_map/all_gather | solution.py:397
  97.4 17.3 %all_to_all.10 = f32[8,2,2,2,4,256]{5,4,3,2,1,0:T(4,128)S(1)} all-to-all(f32[8,2,2,2,4,256]{5,4,3,2,1,0:T(4,128)S(1)} %broadcast_in_dim.6), channel_id=1, replica_groups=mesh['gz'=96,'gy'=8] {'gy'}, dimensions={0} | all-to-all | bytes 524288 | tf_op jit(solution)/shard_map/all_to_all | solution.py:440
  119.5 18.1 %all-gather.27.cloned.1.call-done = f32[4,8,2,2,2,4,256]{6,1,5,4,3,2,0:T(8,128)} async-done(((f32[2,8,2,2,2,4,256]{6,1,5,4,3,2,0:T(8,128)}), f32[4,8,2,2,2,4,256]{6,1,5,4,3,2,0:T(8,128)}) %all-gather.27.cloned.1.call-update) | async-done | bytes 1048592 | tf_op jit(solution)/shard_map/all_gather | solution.py:397
  139.5 22.7 %all-gather.21.cloned.1.call-done = f32[2,2,8,2,2,2,4,256]{7,2,6,5,4,3,1,0:T(8,128)} async-done(((f32[1,2,8,2,2,2,4,256]{7,2,6,5,4,3,1,0:T(8,128)}), f32[2,2,8,2,2,2,4,256]{7,2,6,5,4,3,1,0:T(8,128)}) %all-gather.21.cloned.1.call-update) | async-done | bytes 1048592 | tf_op jit(solution)/shard_map/all_gather | solution.py:397
  167.0 5.5 %all-gather.5 = f32[8,32,128]{2,1,0:T(8,128)S(1)} all-gather(f32[2,32,128]{2,1,0:T(8,128)S(1)} %get-tuple-element.29), channel_id=7, replica_groups={{0,8,16,24},{32,40,48,56},{64,72,80,88},{96,104,112,120},{128,136,144,1..., dimensions={0}, use_global_device_ids=true | all-gather | bytes 163840 | tf_op jit(solution)/shard_map/all_gather | solution.py:397
  172.5 10.8 %all-gather.6 = f32[16,2,32,128]{3,2,1,0:T(8,128)S(1)} all-gather(f32[4,2,32,128]{3,2,1,0:T(8,128)S(1)} %bitcast.32), channel_id=8, replica_groups={{16,24,32,40},{48,56,64,72},{80,88,96,104},{112,120,128,136},{144,152,1..., dimensions={0}, use_global_device_ids=true | all-gather | bytes 655360 | tf_op jit(solution)/shard_map/all_gather | solution.py:397
  183.3 7.4 %all_gather.135.far = f32[4,4,2,32,128]{4,3,2,1,0:T(8,128)S(1)} all-gather(f32[1,4,2,32,128]{4,3,2,1,0:T(8,128)S(1)} %constant_dynamic-slice_fusion.6), channel_id=1, replica_groups={{0,8,16,24},{32,40,48,56},{64,72,80,88},{96,104,112,120},{128,136,144,1..., dimensions={0}, use_global_device_ids=true | all-gather | bytes 655360 | tf_op jit(solution)/shard_map/all_gather | solution.py:397
  193.5 4.7 %all-gather.7 = f32[6,2,16,256]{3,2,1,0:T(8,128)S(1)} all-gather(f32[3,2,16,256]{3,2,1,0:T(8,128)S(1)} %get-tuple-element.33), channel_id=9, replica_groups={{8,16},{24,32},{40,48},{56,64},{72,80},{88,96},{104,112},{120,128},{136..., dimensions={0}, use_global_device_ids=true | all-gather | bytes 294912 | tf_op jit(solution)/shard_map/all_gather | solution.py:397
  198.2 5.0 %all_gather.138.more = f32[2,2,16,256]{3,2,1,0:T(8,128)S(1)} all-gather(f32[1,2,16,256]{3,2,1,0:T(8,128)S(1)} %constant_dynamic-slice_fusion.5), channel_id=1, replica_groups={{0,8},{16,24},{32,40},{48,56},{64,72},{80,88},{96,104},{112,120},{128,1..., dimensions={0}, use_global_device_ids=true | all-gather | bytes 98304 | tf_op jit(solution)/shard_map/all_gather | solution.py:397
  203.2 5.9 %up.2 = (f32[4,4,4,512]{3,2,1,0:T(4,128)S(1)}, f32[4,4,4,512]{3,2,1,0:T(4,128)S(1)}) custom-call(s32[4]{0:T(128)S(1)} %pad_add_fusion.prm, f32[8,2,16,256]{3,2,1,0:T(8,128)S(1)} %get-tuple-element.32.start, f32[2,3,2,16,256]{4,3,2,1,0:T(8,128)S(1)} %bitcast.36, f32[2,2,16,256]{3,2,1,0:T(8,128)S(1)} %all_gather.138.more, ...), custom_call_target="tpu_custom_call" | custom-call | tf_op jit(solution)/shard_map/up/pallas_call | solution.py:380
  223.7 8.2 %all-gather.9 = f32[12,4,8,512]{3,2,1,0:T(8,128)S(1)} all-gather(f32[6,4,8,512]{3,2,1,0:T(8,128)S(1)} %constant_dynamic-slice_fusion.4), channel_id=11, replica_groups={{8,16},{24,32},{40,48},{56,64},{72,80},{88,96},{104,112},{120,128},{136..., dimensions={0}, use_global_device_ids=true | all-gather | bytes 1179648 | tf_op jit(solution)/shard_map/all_gather | solution.py:397
  231.9 5.0 %all-gather.10 = f32[4,4,8,512]{3,2,1,0:T(8,128)S(1)} all-gather(f32[2,4,8,512]{3,2,1,0:T(8,128)S(1)} %constant_dynamic-slice_fusion.3), channel_id=12, replica_groups={{0,8},{16,24},{32,40},{48,56},{64,72},{80,88},{96,104},{112,120},{128,1..., dimensions={0}, use_global_device_ids=true | all-gather | bytes 393216 | tf_op jit(solution)/shard_map/all_gather | solution.py:397
  240.2 11.9 %all_to_all.11 = f32[8,1,2,2,4,256]{5,4,3,2,1,0:T(4,128)S(1)} all-to-all(f32[8,1,2,2,4,256]{5,4,3,2,1,0:T(4,128)S(1)} %broadcast_in_dim.7), channel_id=1, replica_groups=mesh['gz'=96,'gy'=8] {'gy'}, dimensions={0} | all-to-all | bytes 262144 | tf_op jit(solution)/shard_map/all_to_all | solution.py:440
  256.0 6.8 %all-gather.12 = f32[4,8,1,2,2,4,256]{6,1,5,4,3,2,0:T(8,128)S(1)} all-gather(f32[2,8,1,2,2,4,256]{6,1,5,4,3,2,0:T(8,128)S(1)} %copy.6), channel_id=14, replica_groups={{8,16},{24,32},{40,48},{56,64},{72,80},{88,96},{104,112},{120,128},{136..., dimensions={0}, use_global_device_ids=true | all-gather | bytes 786432 | tf_op jit(solution)/shard_map/all_gather | solution.py:397
  262.8 5.2 %all_gather.149 = f32[2,2,8,1,2,2,4,256]{7,2,6,5,4,3,1,0:T(8,128)S(1)} all-gather(f32[1,2,8,1,2,2,4,256]{7,2,6,5,4,3,1,0:T(8,128)S(1)} %constant_dynamic-slice_fusion.2), channel_id=1, replica_groups={{0,8},{16,24},{32,40},{48,56},{64,72},{80,88},{96,104},{112,120},{128,1..., dimensions={0}, use_global_device_ids=true | all-gather | bytes 786432 | tf_op jit(solution)/shard_map/all_gather | solution.py:397
  270.9 5.4 %all-gather.13 = f32[4,32,128]{2,1,0:T(8,128)S(1)} all-gather(f32[1,32,128]{2,1,0:T(8,128)S(1)} %get-tuple-element.42), channel_id=15, replica_groups={{0,8,16,24},{32,40,48,56},{64,72,80,88},{96,104,112,120},{128,136,144,1..., dimensions={0}, use_global_device_ids=true | all-gather | bytes 81920 | tf_op jit(solution)/shard_map/all_gather | solution.py:397
  276.4 9.2 %all-gather.14 = f32[16,32,128]{2,1,0:T(8,128)S(1)} all-gather(f32[4,32,128]{2,1,0:T(8,128)S(1)} %all-gather.13), channel_id=16, replica_groups={{16,24,32,40},{48,56,64,72},{80,88,96,104},{112,120,128,136},{144,152,1..., dimensions={0}, use_global_device_ids=true | all-gather | bytes 327680 | tf_op jit(solution)/shard_map/all_gather | solution.py:397
  285.5 5.8 %all_gather.154.far = f32[4,4,1,32,128]{4,3,2,1,0:T(8,128)S(1)} all-gather(f32[1,4,1,32,128]{4,3,2,1,0:T(8,128)S(1)} %constant_dynamic-slice_fusion.1), channel_id=1, replica_groups={{0,8,16,24},{32,40,48,56},{64,72,80,88},{96,104,112,120},{128,136,144,1..., dimensions={0}, use_global_device_ids=true | all-gather | bytes 327680 | tf_op jit(solution)/shard_map/all_gather | solution.py:397
  298.9 5.0 %all_gather.157.more = f32[2,2,16,256]{3,2,1,0:T(8,128)S(1)} all-gather(f32[1,2,16,256]{3,2,1,0:T(8,128)S(1)} %constant_dynamic-slice_fusion), channel_id=1, replica_groups={{0,8},{16,24},{32,40},{48,56},{64,72},{80,88},{96,104},{112,120},{128,1..., dimensions={0}, use_global_device_ids=true | all-gather | bytes 98304 | tf_op jit(solution)/shard_map/all_gather | solution.py:397
  303.9 5.9 %up.3 = (f32[4,4,4,512]{3,2,1,0:T(4,128)S(1)}, f32[4,4,4,512]{3,2,1,0:T(4,128)S(1)}) custom-call(s32[4]{0:T(128)S(1)} %pad_add_fusion.prm, f32[8,2,16,256]{3,2,1,0:T(8,128)S(1)} %get-tuple-element.46.start, f32[2,3,2,16,256]{4,3,2,1,0:T(8,128)S(1)} %bitcast.35, f32[2,2,16,256]{3,2,1,0:T(8,128)S(1)} %all_gather.157.more, ...), custom_call_target="tpu_custom_call" | custom-call | tf_op jit(solution)/shard_map/up/pallas_call | solution.py:380
  (61 shorter events, 63.5 us)
Async XLA Ops:
  7.2 44.0 %all-gather.23.cloned.1.call-start = ((), (), s32[]{:S(2)}) async-start(), calls=%async_computation.3 | async-start | bytes 1572864 | tf_op jit(solution)/shard_map/all_gather | solution.py:397
  7.2 0.9 copy-start.5
  8.1 0.9 copy-start.6
  9.9 7.9 %collective-permute-start = (f32[4,8,2,512]{3,2,1,0:T(2,128)S(1)}, f32[4,8,2,512]{3,2,1,0:T(2,128)S(1)}, u32[]{:S(2)}, u32[]{:S(2)}) collective-permute-start(f32[4,8,2,512]{3,2,1,0:T(2,128)S(1)} %get-tuple-element.54), channel_id=1, source_target_pairs={{1,0},{2,1},{3,2},{4,3},{5,4},{6,5},{7,6},{0,7},{9,8},{10,9},{11,1... | collective-permute-start | bytes 393224 | tf_op jit(solution)/shard_map/ppermute | solution.py:404
  15.9 6.9 %collective-permute-start.1 = (f32[4,8,2,512]{3,2,1,0:T(2,128)S(1)}, f32[4,8,2,512]{3,2,1,0:T(2,128)S(1)}, u32[]{:S(2)}, u32[]{:S(2)}) collective-permute-start(f32[4,8,2,512]{3,2,1,0:T(2,128)S(1)} %get-tuple-element.55), channel_id=1, source_target_pairs={{0,1},{1,2},{2,3},{3,4},{4,5},{5,6},{6,7},{7,0},{8,9},{9,10},{10,1... | collective-permute-start | bytes 393224 | tf_op jit(solution)/shard_map/ppermute | solution.py:405
  23.8 59.2 %all-gather.25.cloned.1.call-start = ((), (), s32[]{:S(2)}) async-start(), calls=%async_computation.4 | async-start | bytes 2359296 | tf_op jit(solution)/shard_map/all_gather | solution.py:397
  51.2 39.7 %copy-start.2 = (f32[8,8,8,512]{3,2,1,0:T(8,128)S(1)}, f32[8,8,8,512]{3,2,1,0:T(8,128)}, u32[]{:S(2)}) copy-start(f32[8,8,8,512]{3,2,1,0:T(8,128)} %all-gather.23.cloned.1.call-done) | copy-start | bytes 3145732
  53.4 84.2 %all-gather.27.cloned.1.call-start = ((), (), s32[]{:S(2)}) async-start(), calls=%async_computation.5 | async-start | bytes 1572864 | tf_op jit(solution)/shard_map/all_gather | solution.py:397
  95.5 1.0 copy-start
  96.5 0.9 copy-start.3
  119.5 42.7 %all-gather.21.cloned.1.call-start = ((), (), s32[]{:S(2)}) async-start(), calls=%async_computation.2 | async-start | bytes 1572864 | tf_op jit(solution)/shard_map/all_gather | solution.py:397
  183.3 20.0 %copy-start.4 = (f32[12,4,8,512]{3,2,1,0:T(8,128)S(1)}, f32[12,4,8,512]{3,2,1,0:T(8,128)}, u32[]{:S(2)}) copy-start(f32[12,4,8,512]{3,2,1,0:T(8,128)} %copy-done.3) | copy-start | bytes 2359300
  209.2 6.4 %collective-permute-start.2 = (f32[4,4,2,512]{3,2,1,0:T(2,128)S(1)}, f32[4,4,2,512]{3,2,1,0:T(2,128)S(1)}, u32[]{:S(2)}, u32[]{:S(2)}) collective-permute-start(f32[4,4,2,512]{3,2,1,0:T(2,128)S(1)} %get-tuple-element.56), channel_id=1, source_target_pairs={{1,0},{2,1},{3,2},{4,3},{5,4},{6,5},{7,6},{0,7},{9,8},{10,9},{11,1... | collective-permute-start | bytes 196616 | tf_op jit(solution)/shard_map/ppermute | solution.py:404
  213.6 6.2 %collective-permute-start.3 = (f32[4,4,2,512]{3,2,1,0:T(2,128)S(1)}, f32[4,4,2,512]{3,2,1,0:T(2,128)S(1)}, u32[]{:S(2)}, u32[]{:S(2)}) collective-permute-start(f32[4,4,2,512]{3,2,1,0:T(2,128)S(1)} %get-tuple-element.57), channel_id=1, source_target_pairs={{0,1},{1,2},{2,3},{3,4},{4,5},{5,6},{6,7},{7,0},{8,9},{9,10},{10,1... | collective-permute-start | bytes 196616 | tf_op jit(solution)/shard_map/ppermute | solution.py:405
  220.0 17.0 %copy-start.1 = (f32[16,4,8,512]{3,2,1,0:T(8,128)S(1)}, f32[16,4,8,512]{3,2,1,0:T(8,128)}, u32[]{:S(2)}) copy-start(f32[16,4,8,512]{3,2,1,0:T(8,128)} %copy-done) | copy-start | bytes 3145732
Sparse Core Ops, SparseCore 0:
  23.9 27.2 all-gather.22
  53.6 29.3 all-gather.24
  119.6 17.9 all-gather.26
  139.8 22.3 all-gather.20

commit v2 on v1

--- a/solution.py
+++ b/solution.py
@@ -73,35 +73,42 @@
     return out
 
 
-def first_step(lo, hi, rhs, inv, w, dw, size, beta):
-    def body(z, carry):
-        for d in range(size):
-            for c in range(size):
-                value = (beta * rhs[z, d, :, lanes(c)]) * inv[z, d, :, lanes(c)]
-                w[z, d, :, lanes(c)] = value
-                dw[z, d, :, lanes(c)] = value
+def first_step(lo, hi, rhs, inv, w, dw, size, beta, group=1):
+    def body(step, carry):
+        for z in [lo + step * group + g for g in range(group)]:
+            for d in range(size):
+                for c in range(size):
+                    value = (beta * rhs[z, d, :, lanes(c)]) * inv[z, d, :, lanes(c)]
+                    w[z, d, :, lanes(c)] = value
+                    dw[z, d, :, lanes(c)] = value
         return carry
 
-    lax.fori_loop(lo, hi, body, 0)
-
-
-def sweep(lo, hi, src, dst, dst_shift, dw, rhs, inv, shift, size, scale, alpha, beta, loader=load):
-    def body(z, carry):
-        here = load(src, z, size)
-        near = neighbours(load(src, z - 1, size), here, load(src, z + 1, size), size)
-        f = loader(rhs, z + shift, size)
-        i = loader(inv, z + shift, size)
-        for d in range(size):
-            for c in range(size):
-                q = i[d][c] * (f[d][c] + scale * near[d][c]) - here[d][c]
-                change = beta * q
-                if alpha != 0.0:
-                    change = change + alpha * dw[z, d, :, lanes(c)]
-                dw[z, d, :, lanes(c)] = change
-                dst[z + dst_shift, d, :, lanes(c)] = here[d][c] + change
+    lax.fori_loop(0, (hi - lo) // group, body, 0)
+
+
+def sweep(lo, hi, src, dst, dst_shift, dw, rhs, inv, shift, size, scale, alpha, beta, loader=load, group=1):
+    def body(step, carry):
+        start = lo + step * group
+        planes = {g: load(src, start + g, size) for g in range(-1, group + 1)}
+        done = []
+        for g in range(group):
+            z, here = start + g, planes[g]
+            near = neighbours(planes[g - 1], here, planes[g + 1], size)
+            f = loader(rhs, z + shift, size)
+            i = loader(inv, z + shift, size)
+            for d in range(size):
+                for c in range(size):
+                    q = i[d][c] * (f[d][c] + scale * near[d][c]) - here[d][c]
+                    change = beta * q
+                    if alpha != 0.0:
+                        change = change + alpha * dw[z, d, :, lanes(c)]
+                    done.append((z, d, c, change, here[d][c] + change))
+        for z, d, c, change, value in done:
+            dw[z, d, :, lanes(c)] = change
+            dst[z + dst_shift, d, :, lanes(c)] = value
         return carry
 
-    lax.fori_loop(lo, hi, body, 0)
+    lax.fori_loop(0, (hi - lo) // group, body, 0)
 
 
 def residual_plane(src, z, rhs, inv, zr, size, scale):
@@ -175,35 +182,48 @@
     out_r[...] = rows[64:128].reshape(4, 16, 512)
 
 
-def fine_down_kernel(first, prm, chip, side, more, *refs):
+def rows_kernel(parts, prm, chip, halves, *outs):
+    core, odd = prm[0], prm[1]
+    for a in range(parts):
+        whole, send = outs[2 * a : 2 * a + 2]
+        for t in range(8):
+            for d in range(4):
+                whole[t, d, 0:4, :] = chip[t // 4, t % 4, 4 * a + d]
+                whole[t, d, 4:6, :] = halves[odd, t, 4 * a + d]
+                whole[t, d, 6:8, :] = halves[1 - odd, t, 4 * a + d]
+        for t in range(6):
+            send[t] = whole[2 * core + t]
+
+
+def fine_down_kernel(first, prm, *refs):
     if first:
-        rhs, field, low, cond, inv, wa, wb, dw = refs
+        whole, side, whole_k, side_k, more, more_k, rhs, field, low, cond, inv, wa, wb, dw = refs
     else:
-        inv, rhs, field, low, wa, wb, dw = refs
+        whole, side, more, inv, rhs, field, low, wa, wb, dw = refs
     core = prm[0]
 
-    def put(t, ref, *index):
-        rhs[t] = ref[(*index, slice(0, 4))]
-        if first:
-            cond[t] = ref[(*index, slice(4, 8))]
-
-    @pl.when(core == 0)
-    def _():
-        for t in range(6):
-            put(t, side, 0, t)
-        for t in range(8):
-            put(6 + t, chip, t // 4, t % 4)
-        for t in range(2):
-            put(14 + t, more, 1, t)
-
-    @pl.when(core == 1)
-    def _():
-        for t in range(2):
-            put(t, more, 0, t)
-        for t in range(8):
-            put(2 + t, chip, t // 4, t % 4)
-        for t in range(6):
-            put(10 + t, side, 1, t)
+    def assemble(out, own, beside, beyond):
+        @pl.when(core == 0)
+        def _():
+            for t in range(6):
+                out[t] = beside[0, t]
+            for t in range(8):
+                out[6 + t] = own[t]
+            for t in range(2):
+                out[14 + t] = beyond[1, t]
+
+        @pl.when(core == 1)
+        def _():
+            for t in range(2):
+                out[t] = beyond[0, t]
+            for t in range(8):
+                out[2 + t] = own[t]
+            for t in range(6):
+                out[10 + t] = beside[1, t]
+
+    assemble(rhs, whole, side, more)
+    if first:
+        assemble(cond, whole_k, side_k, more_k)
 
     if first:
 
@@ -231,25 +251,31 @@
                     low[1, t, d, :, lanes(c)] = mean[d][c][0:4]
 
 
+def pick_kernel(prm, rows, out):
+    for j, step in enumerate((0, 1, 2, 6, 7)):
+        out[j] = rows[lax.rem(prm[2] + step, 8)]
+
+
 def middle_down_kernel(first, prm, chip, far, *refs):
     if first:
         rhs, field, low, cond, inv, wa, wb, dw = refs
     else:
         inv, rhs, field, low, wa, wb, dw = refs
-    core, me = prm[0], prm[1]
-    for j in range(8):
-        y = lax.rem(me + j, 8)
-        for t in range(12):
-            if t < 4:
-                ref, index = far, (0, t // 2, y)
-            elif t < 8:
-                ref, index = chip, ((t - 4) // 2, y)
-            else:
-                ref, index = far, (1, (t - 8) // 2, y)
-            for d in range(2):
-                rhs[t, d, 4 * j : 4 * j + 4, :] = ref[(*index, 0, t % 2, d)]
+    for t in range(12):
+        if t < 4:
+            ref, at = far.at[0], t
+        elif t < 8:
+            ref, at = chip, t - 4
+        else:
+            ref, at = far.at[1], t - 8
+        for d in range(2):
+            for j, row in enumerate((0, 4, 8, 16, 20)):
+                rhs[t, d, row : row + 4, :] = ref[at // 2, j, 0, at % 2, d]
                 if first:
-                    cond[t, d, 4 * j : 4 * j + 4, :] = ref[(*index, 1, t % 2, d)]
+                    cond[t, d, row : row + 4, :] = ref[at // 2, j, 1, at % 2, d]
+            rhs[t, d, 12:16, :] = jnp.zeros((4, 256), jnp.float32)
+            if first:
+                cond[t, d, 12:16, :] = jnp.ones((4, 256), jnp.float32)
     if first:
 
         def fill(t, carry):
@@ -258,15 +284,16 @@
 
         lax.fori_loop(0, 12, fill, 0)
     steps = chebyshev(DEGREE)
-    first_step(0, 12, rhs, inv, wa, dw, 2, steps[0][1])
-    sweep(1, 11, wa, wb, 0, dw, rhs, inv, 0, 2, SCALES[1], *steps[1])
-    sweep(2, 10, wb, field, -2, dw, rhs, inv, 0, 2, SCALES[1], *steps[2])
-    z = 4 + 2 * core
-    one = residual_plane(field, z - 2, rhs, inv, z, 2, SCALES[1])
-    two = residual_plane(field, z - 1, rhs, inv, z + 1, 2, SCALES[1])
-    low[0] = halve(one, two, 2)[0][0]
-    if first:
-        low[1] = halve(load(cond, z, 2), load(cond, z + 1, 2), 2)[0][0]
+    first_step(0, 12, rhs, inv, wa, dw, 2, steps[0][1], group=2)
+    sweep(1, 11, wa, wb, 0, dw, rhs, inv, 0, 2, SCALES[1], *steps[1], group=2)
+    sweep(2, 10, wb, field, -2, dw, rhs, inv, 0, 2, SCALES[1], *steps[2], group=2)
+    for h in range(2):
+        z = 4 + 2 * h
+        one = residual_plane(field, z - 2, rhs, inv, z, 2, SCALES[1])
+        two = residual_plane(field, z - 1, rhs, inv, z + 1, 2, SCALES[1])
+        low[0, h] = halve(one, two, 2)[0][0]
+        if first:
+            low[1, h] = halve(load(cond, z, 2), load(cond, z + 1, 2), 2)[0][0]
 
 
 def coarse_kernel(first, prm, block, far, middle, mid_cond, *refs):
@@ -274,28 +301,28 @@
         start, send, cond, inv, rhs, wa, wb, dw = refs
     else:
         cond, inv, start, send, rhs, wa, wb, dw = refs
-    core, half = prm[0], prm[2]
+    core, half = prm[0], prm[3]
     for t in range(12):
         if t < 4:
-            ref, index = far, (0, t)
+            ref, at = far.at[0], t
         elif t < 8:
-            ref, index = block, (t - 4,)
+            ref, at = block, t - 4
         else:
-            ref, index = far, (3, t - 8)
-        rhs[t, 0] = ref[(*index, 0)]
+            ref, at = far.at[1], t - 8
+        rhs[t, 0] = ref[at // 2, 0, at % 2]
         if first:
-            value = ref[(*index, 1)]
+            value = ref[at // 2, 1, at % 2]
             cond[t, 0] = value
             inv[t, 0] = inverse_of(value, SCALES[2])
     steps = chebyshev(COARSE_DEGREE)
-    first_step(0, 12, rhs, inv, wa, dw, 1, steps[0][1])
-    sweep(1, 11, wa, wb, 0, dw, rhs, inv, 0, 1, SCALES[2], *steps[1])
-    sweep(2, 10, wb, wa, 0, dw, rhs, inv, 0, 1, SCALES[2], *steps[2])
-    sweep(3, 9, wa, wb, 0, dw, rhs, inv, 0, 1, SCALES[2], *steps[3])
+    first_step(0, 12, rhs, inv, wa, dw, 1, steps[0][1], group=12)
+    sweep(1, 11, wa, wb, 0, dw, rhs, inv, 0, 1, SCALES[2], *steps[1], group=10)
+    sweep(2, 10, wb, wa, 0, dw, rhs, inv, 0, 1, SCALES[2], *steps[2], group=8)
+    sweep(3, 9, wa, wb, 0, dw, rhs, inv, 0, 1, SCALES[2], *steps[3], group=6)
     for u in range(8):
         t = 3 + 2 * half + u // 2
         value = wb[t, 0] / cond[t, 0]
-        value = jnp.concatenate([value[0:8], value[24:32]], axis=0)
+        value = jnp.concatenate([value[0:8], value[16:24]], axis=0)
         k = load_ends(mid_cond, u + 2, 2)
         w = load_ends(middle, u, 2)
         for d in range(2):
@@ -330,9 +357,9 @@
 
     steps = chebyshev(DEGREE)
     shift = 2 * core - 1
-    sweep(1, 11, mid_a, mid_b, 0, mid_dw, mid_rhs, mid_inv, shift, 2, SCALES[1], *steps[0], loader=load_ends)
-    sweep(2, 10, mid_b, mid_a, 0, mid_dw, mid_rhs, mid_inv, shift, 2, SCALES[1], *steps[1], loader=load_ends)
-    sweep(3, 9, mid_a, mid_b, 0, mid_dw, mid_rhs, mid_inv, shift, 2, SCALES[1], *steps[2], loader=load_ends)
+    sweep(1, 11, mid_a, mid_b, 0, mid_dw, mid_rhs, mid_inv, shift, 2, SCALES[1], *steps[0], loader=load_ends, group=2)
+    sweep(2, 10, mid_b, mid_a, 0, mid_dw, mid_rhs, mid_inv, shift, 2, SCALES[1], *steps[1], loader=load_ends, group=2)
+    sweep(3, 9, mid_a, mid_b, 0, mid_dw, mid_rhs, mid_inv, shift, 2, SCALES[1], *steps[2], loader=load_ends, group=2)
 
     near = lax.broadcasted_iota(jnp.int32, (8, LANES), 0) < 6
 
@@ -388,29 +415,43 @@
     )(*args)
 
 
-def groups(axis, size, shift):
-    devices = lax.axis_size(axis)
-    return [[(g * size + i + shift) % devices for i in range(size)] for g in range(devices // size)]
-
-
-def gather(value, size, shift):
-    return lax.all_gather(value, "gz", axis_index_groups=groups("gz", size, shift))
-
-
-def row_halo(own):
-    devices = lax.axis_size("gy")
-    up = [(i, (i + 1) % devices) for i in range(devices)]
-    down = [(j, i) for i, j in up]
-    after = lax.ppermute(own[:, :, 0:2], "gy", down)
-    before = lax.ppermute(own[:, :, 2:4], "gy", up)
-    return jnp.concatenate([own, after, before], axis=2)
+def pairs(first, step, size):
+    devices = lax.axis_size("gz")
+    return [[(b + i) % devices, (b + i + step) % devices] for b in range(0, devices, size) for i in first]
+
+
+def gather(value, first, step, size):
+    return lax.all_gather(value, "gz", axis_index_groups=pairs(first, step, size))
+
+
+def cores(value):
+    return gather(value, (0,), 1, 2)
+
+
+def across(value):
+    return gather(value, (1,), 1, 2)
+
+
+def row_pairs(value):
+    planes, rows = lax.axis_size("gz"), lax.axis_size("gy")
+    members = []
+    for z in range(planes):
+        for y in range(z % 2, rows, 2):
+            members.append([z * rows + y, z * rows + (y + 1) % rows])
+    return lax.all_gather(value, ("gz", "gy"), axis_index_groups=members)
+
+
+def pick(value, index):
+    return lax.dynamic_index_in_dim(value, index, 0, keepdims=False)
 
 
 def local(source, conduct):
     z = lax.axis_index("gz")
     y = lax.axis_index("gy")
     core = z % 2
-    prm = jnp.stack([core, y, (z % 4) // 2, 0]).astype(jnp.int32)
+    half = (z % 4) // 2
+    prm = jnp.stack([core, y % 2, y, half]).astype(jnp.int32)
+    place = (core + y) % 2
     (remain,) = call(
         prepare_kernel, [f32(4, 8, 4, 512)], [(4, 128, 128)], source, conduct, scalars=False, name="prepare"
     )
@@ -419,31 +460,43 @@
     for cycle in range(CYCLES):
         first, last = cycle == 0, cycle == CYCLES - 1
         parts = 2 if first else 1
-        own = row_halo(remain)
-        chip = gather(own, 2, 0)
-        whole = chip.reshape(8, *chip.shape[2:])
-        side = gather(lax.dynamic_slice_in_dim(whole, 2 * core, 6, 0), 2, 1)
-        flat = side.reshape(12, *side.shape[2:])
-        more = gather(lax.dynamic_slice_in_dim(flat, 4 + 2 * core, 2, 0), 2, 0)
+        chip = cores(remain)
+        flat = chip.reshape(8, *chip.shape[2:])
+        halves = row_pairs(jnp.where(place == 0, flat[:, :, 2:4], flat[:, :, 0:2]))
+        halves = cores(jnp.where(place == 0, halves[1], halves[0]))
+        laid = call(
+            functools.partial(rows_kernel, parts),
+            [f32(8, 4, 8, 512), f32(6, 4, 8, 512)] * parts,
+            [],
+            prm,
+            chip,
+            halves,
+            name="rows",
+        )
+        args, mores = [prm], []
+        for a in range(parts):
+            side = across(laid[2 * a + 1])
+            args += [laid[2 * a], side]
+            flat = side.reshape(12, *side.shape[2:])
+            mores.append(cores(lax.dynamic_slice_in_dim(flat, 4 + 2 * core, 2, 0)))
+        args += mores
         outs = [f32(16, 4, 8, 512), f32(12, 4, 8, 512), f32(parts, 2, 2, 4, 256)]
         state = [f32(16, 4, 8, 512)] * 2
         scratch = [(16, 4, 8, 512)] * 3
         body = functools.partial(fine_down_kernel, first)
         if first:
-            rhs0, field0, low, cond0, inv0 = call(
-                body, outs + state, scratch, prm, chip, side, more, name="fine_down_first"
-            )
+            rhs0, field0, low, cond0, inv0 = call(body, outs + state, scratch, *args, name="fine_down_first")
         else:
             cond0, inv0 = kept[0:2]
-            rhs0, field0, low = call(body, outs, scratch, prm, chip, side, more, inv0, name="fine_down")
+            rhs0, field0, low = call(body, outs, scratch, *args, inv0, name="fine_down")
         copies = jnp.broadcast_to(low, (lax.axis_size("gy"), *low.shape))
         rows = lax.all_to_all(copies, "gy", split_axis=0, concat_axis=0, tiled=True)
-        chip = gather(rows, 2, 0)
-        side = gather(chip, 2, 1)
-        far = gather(lax.dynamic_index_in_dim(side, core, 0, keepdims=False), 2, 0)
-        outs = [f32(12, 2, 32, 256), f32(8, 2, 32, 256), f32(parts, 32, 128)]
-        state = [f32(12, 2, 32, 256)] * 2
-        scratch = [(12, 2, 32, 256)] * 3
+        (rows,) = call(pick_kernel, [f32(5, parts, 2, 2, 4, 256)], [], prm, rows, name="pick")
+        chip = cores(rows)
+        far = cores(pick(across(chip), core))
+        outs = [f32(12, 2, 24, 256), f32(8, 2, 24, 256), f32(parts, 2, 24, 128)]
+        state = [f32(12, 2, 24, 256)] * 2
+        scratch = [(12, 2, 24, 256)] * 3
         body = functools.partial(middle_down_kernel, first)
         if first:
             rhs1, field1, low, cond1, inv1 = call(
@@ -452,13 +505,12 @@
         else:
             cond1, inv1 = kept[2:4]
             rhs1, field1, low = call(body, outs, scratch, prm, chip, far, inv1, name="middle_down")
-        block = gather(low, 4, 0)
-        side = gather(block, 4, 2)
-        half = prm[2]
-        far = gather(lax.dynamic_index_in_dim(side, 2 * half, 0, keepdims=False), 4, 0)
+        block = gather(low, (0, 1), 2, 4)
+        side = gather(block, (2, 3), 2, 4)
+        far = gather(pick(side, half), (0, 1), 2, 4)
         outs = [f32(8, 2, 16, 256), f32(3, 2, 16, 256)]
-        state = [f32(12, 1, 32, 128)] * 2
-        scratch = [(12, 1, 32, 128)] * 4
+        state = [f32(12, 1, 24, 128)] * 2
+        scratch = [(12, 1, 24, 128)] * 4
         body = functools.partial(coarse_kernel, first)
         if first:
             start, send, cond2, inv2 = call(
@@ -469,9 +521,8 @@
             start, send = call(
                 body, outs, scratch, prm, block, far, field1, cond1, cond2, inv2, name="coarse"
             )
-        side = gather(send, 2, 1)
-        flat = side.reshape(6, *side.shape[2:])
-        more = gather(lax.dynamic_index_in_dim(flat, 2 + core, 0, keepdims=False), 2, 0)
+        side = across(send)
+        more = cores(pick(side.reshape(6, *side.shape[2:]), 2 + core))
         outs = [f32(4, 4, 4, 512)] * 2
         scratch = [(12, 2, 16, 256)] * 3 + [(12, 4, 8, 512)] * 3
         args = [prm, start, side, more, rhs1, cond1, inv1, rhs0, field0, cond0, inv0]

time: 319 us -> 222 us (0.70)
  waiting for transfers between devices: 107 us -> 11.1 us
  blocking collectives: 136 us -> 169 us
  between operations: 14.1 us -> 0.94 us
  starting transfers between devices: 14.4 us -> 6.32 us
  local copies, waits for them, and re-layouts: 12.1 us -> 5.44 us
  Pallas kernels: 33.5 us -> 28.7 us
    all_gather x4 -> x0, waiting for transfers between devices: 97.5 us -> none  [gather(): lax.all_gather(value, 'gz', axis_index_groups=groups('gz', size, shift))]
    all_gather x18 -> x28, blocking collectives: 107 us -> 158 us  [the longest x26 145 us: gather(): lax.all_gather(value, 'gz', axis_index_groups=pairs(first, step, size))]
    all_to_all x2 -> x1, blocking collectives: 29.2 us -> 10.8 us  [local(): rows = lax.all_to_all(copies, 'gy', split_axis=0, concat_axis=0, tiled=True)]
    ppermute x4 -> x0, starting transfers between devices: 14.2 us -> none  [the longest x2 10.4 us: row_halo(): after = lax.ppermute(own[:, :, 0:2], 'gy', down)]
    all_to_all x0 -> x1, waiting for transfers between devices: none -> 11.1 us  [local(): rows = lax.all_to_all(copies, 'gy', split_axis=0, concat_axis=0, tiled=True)]
    ppermute x4 -> x0, waiting for transfers between devices: 9.27 us -> none  [the longest x2 9.27 us: row_halo(): before = lax.ppermute(own[:, :, 2:4], 'gy', up)]
    all_to_all x0 -> x1, starting transfers between devices: none -> 6.32 us  [local(): rows = lax.all_to_all(copies, 'gy', split_axis=0, concat_axis=0, tiled=True)]
    dynamic_slice x10 -> x9, local copies, waits for them, and re-layouts: 5.11 us -> 0.08 us  [the longest x6 0.05 us: pick(): return lax.dynamic_index_in_dim(value, index, 0, keepdims=False)]
  transfers between devices with their start and end apart: 8 -> 1, of which waited for: 6 -> 1; matrix products, arithmetic and copies ran while one was open for 0% -> 0% of each run, Pallas kernels for 0% -> 0%
where the time goes in v2:
time: 222 us
  blocking collectives  169 us (76%)
  Pallas kernels  28.7 us (13%)
  waiting for transfers between devices  11.1 us (5%)
  starting transfers between devices  6.32 us (3%)
  local copies, waits for them, and re-layouts  5.44 us (2%)
    all_gather x26, blocking collectives, gather(): lax.all_gather(value, 'gz', axis_index_groups=pairs(first, step, size))  145 us
    pallas_call x14, Pallas kernels, call(): pl.pallas_call(body, out_shape=outs, in_specs=specs, out_specs=[pl.BlockS...  28.7 us
    all_gather x2, blocking collectives, row_pairs(): return lax.all_gather(value, ('gz', 'gy'), axis_index_groups=members)  12.8 us
    all_to_all x1, waiting for transfers between devices, local(): rows = lax.all_to_all(copies, 'gy', split_axis=0, concat_axis=0, tiled=True)  11.1 us
    all_to_all x1, blocking collectives, local(): rows = lax.all_to_all(copies, 'gy', split_axis=0, concat_axis=0, tiled=True)  10.8 us
    all_to_all x1, starting transfers between devices, local(): rows = lax.all_to_all(copies, 'gy', split_axis=0, concat_axis=0, tiled=True)  6.32 us
  transfers between devices with their start and end apart: 1, of which 1 were waited for; matrix products, arithmetic and copies ran while one was open for 0% of the time, Pallas kernels for 0%

profile of v2, /device:TPU:1, one launch (start us, length us, event | category | flops | bytes accessed | tf_op | source)
XLA Modules:
  0.0 221.7 jit_solution(16776103432194122342)
XLA Ops:
  3.4 12.3 %all-gather = f32[8,8,4,512]{3,1,2,0:T(8,128)S(1)} all-gather(f32[4,8,4,512]{3,1,2,0:T(8,128)S(1)} %copy.4), channel_id=2, replica_groups={{0,8},{16,24},{32,40},{48,56},{64,72},{80,88},{96,104},{112,120},{128,1..., dimensions={0}, use_global_device_ids=true | all-gather | bytes 786432 | tf_op jit(solution)/shard_map/all_gather | solution.py:424
  16.1 7.1 %all-gather.1 = f32[16,8,2,512]{3,1,2,0:T(8,128)S(1)} all-gather(f32[8,8,2,512]{3,1,2,0:T(8,128)S(1)} %slice_select_fusion.1), channel_id=3, replica_groups={{0,1},{2,3},{4,5},{6,7},{9,10},{11,12},{13,14},{15,8},{16,17},{18,19},{..., dimensions={0}, use_global_device_ids=true | all-gather | bytes 786432 | tf_op jit(solution)/shard_map/all_gather | solution.py:441
  27.6 8.2 %all-gather.2 = f32[12,4,8,512]{3,2,1,0:T(8,128)S(1)} all-gather(f32[6,4,8,512]{3,2,1,0:T(8,128)S(1)} %get-tuple-element.35), channel_id=4, replica_groups={{8,16},{24,32},{40,48},{56,64},{72,80},{88,96},{104,112},{120,128},{136..., dimensions={0}, use_global_device_ids=true | all-gather | bytes 1179648 | tf_op jit(solution)/shard_map/all_gather | solution.py:424
  35.8 6.1 %all-gather.4 = f32[4,4,8,512]{3,2,1,0:T(8,128)S(1)} all-gather(f32[2,4,8,512]{3,2,1,0:T(8,128)S(1)} %constant_dynamic-slice_fusion.8), channel_id=6, replica_groups={{0,8},{16,24},{32,40},{48,56},{64,72},{80,88},{96,104},{112,120},{128,1..., dimensions={0}, use_global_device_ids=true | all-gather | bytes 393216 | tf_op jit(solution)/shard_map/all_gather | solution.py:424
  41.9 8.2 %all-gather.3 = f32[12,4,8,512]{3,2,1,0:T(8,128)S(1)} all-gather(f32[6,4,8,512]{3,2,1,0:T(8,128)S(1)} %get-tuple-element.37), channel_id=5, replica_groups={{8,16},{24,32},{40,48},{56,64},{72,80},{88,96},{104,112},{120,128},{136..., dimensions={0}, use_global_device_ids=true | all-gather | bytes 1179648 | tf_op jit(solution)/shard_map/all_gather | solution.py:424
  50.0 5.2 %all-gather.5 = f32[4,4,8,512]{3,2,1,0:T(8,128)S(1)} all-gather(f32[2,4,8,512]{3,2,1,0:T(8,128)S(1)} %constant_dynamic-slice_fusion.7), channel_id=7, replica_groups={{0,8},{16,24},{32,40},{48,56},{64,72},{80,88},{96,104},{112,120},{128,1..., dimensions={0}, use_global_device_ids=true | all-gather | bytes 393216 | tf_op jit(solution)/shard_map/all_gather | solution.py:424
  61.4 6.3 %all-to-all-start = ((f32[8,2,2,2,4,256]{5,4,3,2,1,0:T(4,128)}), f32[8,2,2,2,4,256]{5,4,3,2,1,0:T(4,128)S(1)}, u32[]{:S(2)}, u32[]{:S(2)}) async-start(f32[8,2,2,2,4,256]{5,4,3,2,1,0:T(4,128)} %broadcast_in_dim.6), calls=%async_computation | async-start | bytes 524288 | tf_op jit(solution)/shard_map/all_to_all | solution.py:493
  67.8 11.1 %all-to-all-done.rows = f32[8,2,2,2,4,256]{5,4,3,2,1,0:T(4,128)S(1)} async-done(((f32[8,2,2,2,4,256]{5,4,3,2,1,0:T(4,128)}), f32[8,2,2,2,4,256]{5,4,3,2,1,0:T(4,128)S(1)}, u32[]{:S(2)}, u32[]{:S(2)}) %all-to-all-start) | async-done | bytes 262176 | tf_op jit(solution)/shard_map/all_to_all | solution.py:493
  82.8 7.5 %all-gather.7 = f32[4,5,2,2,2,4,256]{6,5,4,3,2,1,0:T(4,128)S(1)} all-gather(f32[2,5,2,2,2,4,256]{6,5,4,3,2,1,0:T(4,128)S(1)} %bitcast.32), channel_id=9, replica_groups={{8,16},{24,32},{40,48},{56,64},{72,80},{88,96},{104,112},{120,128},{136..., dimensions={0}, use_global_device_ids=true | all-gather | bytes 983040 | tf_op jit(solution)/shard_map/all_gather | solution.py:424
  90.3 5.3 %all_gather.169.far = f32[2,2,5,2,2,2,4,256]{7,6,5,4,3,2,1,0:T(4,128)S(1)} all-gather(f32[1,2,5,2,2,2,4,256]{7,6,5,4,3,2,1,0:T(4,128)S(1)} %constant_dynamic-slice_fusion.6), channel_id=1, replica_groups={{0,8},{16,24},{32,40},{48,56},{64,72},{80,88},{96,104},{112,120},{128,1..., dimensions={0}, use_global_device_ids=true | all-gather | bytes 983040 | tf_op jit(solution)/shard_map/all_gather | solution.py:424
  101.5 7.7 %all-gather.9 = f32[4,2,2,24,128]{4,3,2,1,0:T(8,128)S(1)} all-gather(f32[2,2,2,24,128]{4,3,2,1,0:T(8,128)S(1)} %bitcast.45), channel_id=11, replica_groups={{16,32},{24,40},{48,64},{56,72},{80,96},{88,104},{112,128},{120,136},{1..., dimensions={0}, use_global_device_ids=true | all-gather | bytes 294912 | tf_op jit(solution)/shard_map/all_gather | solution.py:424
  114.2 6.1 %all-gather.10 = f32[6,2,16,256]{3,2,1,0:T(8,128)S(1)} all-gather(f32[3,2,16,256]{3,2,1,0:T(8,128)S(1)} %get-tuple-element.43), channel_id=12, replica_groups={{8,16},{24,32},{40,48},{56,64},{72,80},{88,96},{104,112},{120,128},{136..., dimensions={0}, use_global_device_ids=true | all-gather | bytes 294912 | tf_op jit(solution)/shard_map/all_gather | solution.py:424
  120.3 7.0 %all_gather.177.more = f32[2,2,16,256]{3,2,1,0:T(8,128)S(1)} all-gather(f32[1,2,16,256]{3,2,1,0:T(8,128)S(1)} %constant_dynamic-slice_fusion.4), channel_id=1, replica_groups={{0,8},{16,24},{32,40},{48,56},{64,72},{80,88},{96,104},{112,120},{128,1..., dimensions={0}, use_global_device_ids=true | all-gather | bytes 98304 | tf_op jit(solution)/shard_map/all_gather | solution.py:424
  127.3 5.0 %up.2 = (f32[4,4,4,512]{3,2,1,0:T(4,128)S(1)}, f32[4,4,4,512]{3,2,1,0:T(4,128)S(1)}) custom-call(s32[4]{0:T(128)S(1)} %pad_add_fusion.prm, f32[8,2,16,256]{3,2,1,0:T(8,128)S(1)} %get-tuple-element.42.start, f32[2,3,2,16,256]{4,3,2,1,0:T(8,128)S(1)} %bitcast.44, f32[2,2,16,256]{3,2,1,0:T(8,128)S(1)} %all_gather.177.more, ...), custom_call_target="tpu_custom_call" | custom-call | tf_op jit(solution)/shard_map/up/pallas_call | solution.py:407
  134.5 5.7 %all-gather.12 = f32[16,4,2,512]{3,1,2,0:T(4,128)S(1)} all-gather(f32[8,4,2,512]{3,1,2,0:T(4,128)S(1)} %copy.7), channel_id=14, replica_groups={{0,1},{2,3},{4,5},{6,7},{9,10},{11,12},{13,14},{15,8},{16,17},{18,19},{..., dimensions={0}, use_global_device_ids=true | all-gather | bytes 393216 | tf_op jit(solution)/shard_map/all_gather | solution.py:441
  143.2 8.3 %all-gather.13 = f32[12,4,8,512]{3,2,1,0:T(8,128)S(1)} all-gather(f32[6,4,8,512]{3,2,1,0:T(8,128)S(1)} %get-tuple-element.52), channel_id=15, replica_groups={{8,16},{24,32},{40,48},{56,64},{72,80},{88,96},{104,112},{120,128},{136..., dimensions={0}, use_global_device_ids=true | all-gather | bytes 1179648 | tf_op jit(solution)/shard_map/all_gather | solution.py:424
  151.5 4.9 %all-gather.14 = f32[4,4,8,512]{3,2,1,0:T(8,128)S(1)} all-gather(f32[2,4,8,512]{3,2,1,0:T(8,128)S(1)} %constant_dynamic-slice_fusion.3), channel_id=16, replica_groups={{0,8},{16,24},{32,40},{48,56},{64,72},{80,88},{96,104},{112,120},{128,1..., dimensions={0}, use_global_device_ids=true | all-gather | bytes 393216 | tf_op jit(solution)/shard_map/all_gather | solution.py:424
  159.8 10.8 %all_to_all.10.rows = f32[8,1,2,2,4,256]{5,4,3,2,1,0:T(4,128)S(1)} all-to-all(f32[8,1,2,2,4,256]{5,4,3,2,1,0:T(4,128)S(1)} %broadcast_in_dim.7), channel_id=1, replica_groups=mesh['gz'=96,'gy'=8] {'gy'}, dimensions={0} | all-to-all | bytes 262144 | tf_op jit(solution)/shard_map/all_to_all | solution.py:493
  174.3 5.7 %all-gather.16 = f32[4,5,1,2,2,4,256]{6,5,4,3,2,1,0:T(4,128)S(1)} all-gather(f32[2,5,1,2,2,4,256]{6,5,4,3,2,1,0:T(4,128)S(1)} %bitcast.37), channel_id=18, replica_groups={{8,16},{24,32},{40,48},{56,64},{72,80},{88,96},{104,112},{120,128},{136..., dimensions={0}, use_global_device_ids=true | all-gather | bytes 491520 | tf_op jit(solution)/shard_map/all_gather | solution.py:424
  180.0 5.1 %all_gather.191.far = f32[2,2,5,1,2,2,4,256]{7,6,5,4,3,2,1,0:T(4,128)S(1)} all-gather(f32[1,2,5,1,2,2,4,256]{7,6,5,4,3,2,1,0:T(4,128)S(1)} %constant_dynamic-slice_fusion.2), channel_id=1, replica_groups={{0,8},{16,24},{32,40},{48,56},{64,72},{80,88},{96,104},{112,120},{128,1..., dimensions={0}, use_global_device_ids=true | all-gather | bytes 491520 | tf_op jit(solution)/shard_map/all_gather | solution.py:424
  190.3 6.9 %all-gather.18 = f32[4,2,24,128]{3,2,1,0:T(8,128)S(1)} all-gather(f32[2,2,24,128]{3,2,1,0:T(8,128)S(1)} %all-gather.17), channel_id=20, replica_groups={{16,32},{24,40},{48,64},{56,72},{80,96},{88,104},{112,128},{120,136},{1..., dimensions={0}, use_global_device_ids=true | all-gather | bytes 147456 | tf_op jit(solution)/shard_map/all_gather | solution.py:424
  201.7 6.4 %all-gather.19 = f32[6,2,16,256]{3,2,1,0:T(8,128)S(1)} all-gather(f32[3,2,16,256]{3,2,1,0:T(8,128)S(1)} %get-tuple-element.59), channel_id=21, replica_groups={{8,16},{24,32},{40,48},{56,64},{72,80},{88,96},{104,112},{120,128},{136..., dimensions={0}, use_global_device_ids=true | all-gather | bytes 294912 | tf_op jit(solution)/shard_map/all_gather | solution.py:424
  208.1 7.0 %all_gather.199.more = f32[2,2,16,256]{3,2,1,0:T(8,128)S(1)} all-gather(f32[1,2,16,256]{3,2,1,0:T(8,128)S(1)} %constant_dynamic-slice_fusion), channel_id=1, replica_groups={{0,8},{16,24},{32,40},{48,56},{64,72},{80,88},{96,104},{112,120},{128,1..., dimensions={0}, use_global_device_ids=true | all-gather | bytes 98304 | tf_op jit(solution)/shard_map/all_gather | solution.py:424
  215.1 5.1 %up.3 = (f32[4,4,4,512]{3,2,1,0:T(4,128)S(1)}, f32[4,4,4,512]{3,2,1,0:T(4,128)S(1)}) custom-call(s32[4]{0:T(128)S(1)} %pad_add_fusion.prm, f32[8,2,16,256]{3,2,1,0:T(8,128)S(1)} %get-tuple-element.58.start, f32[2,3,2,16,256]{4,3,2,1,0:T(8,128)S(1)} %bitcast.43, f32[2,2,16,256]{3,2,1,0:T(8,128)S(1)} %all_gather.199.more, ...), custom_call_target="tpu_custom_call" | custom-call | tf_op jit(solution)/shard_map/up/pallas_call | solution.py:407
  (58 shorter events, 51.8 us)
Async XLA Ops:
  0.7 0.9 copy-start.5
  1.6 0.9 copy-start.6
  26.8 0.8 copy-start.3
  50.0 5.2 %copy-start.4 = (f32[8,4,8,512]{3,2,1,0:T(8,128)S(1)}, f32[8,4,8,512]{3,2,1,0:T(8,128)}, u32[]{:S(2)}) copy-start(f32[8,4,8,512]{3,2,1,0:T(8,128)} %copy-done.3) | copy-start | bytes 1572868
  59.8 0.9 copy-start.1
  61.4 17.5 %all-to-all-start = ((f32[8,2,2,2,4,256]{5,4,3,2,1,0:T(4,128)}), f32[8,2,2,2,4,256]{5,4,3,2,1,0:T(4,128)S(1)}, u32[]{:S(2)}, u32[]{:S(2)}) async-start(f32[8,2,2,2,4,256]{5,4,3,2,1,0:T(4,128)} %broadcast_in_dim.6), calls=%async_computation | async-start | bytes 524288 | tf_op jit(solution)/shard_map/all_to_all | solution.py:493
  113.3 14.0 %copy-start.2 = (f32[12,4,8,512]{3,2,1,0:T(8,128)S(1)}, f32[12,4,8,512]{3,2,1,0:T(8,128)}, u32[]{:S(2)}) copy-start(f32[12,4,8,512]{3,2,1,0:T(8,128)} %copy-done.1) | copy-start | bytes 2359300
  143.2 13.3 %copy-start = (f32[16,4,8,512]{3,2,1,0:T(8,128)S(1)}, f32[16,4,8,512]{3,2,1,0:T(8,128)}, u32[]{:S(2)}) copy-start(f32[16,4,8,512]{3,2,1,0:T(8,128)} %get-tuple-element.49.inv.refs_3_) | copy-start | bytes 3145732

commit v3 on v2

--- a/solution.py
+++ b/solution.py
@@ -15,7 +15,7 @@
 CHEB_HIGH = 1.9
 SCALES = (4.0, 1.0, 0.25)
 LANES = 128
-VMEM_LIMIT = 48 * 1024 * 1024
+VMEM_LIMIT = 16 * 1024 * 1024
 
 
 def chebyshev(steps):
@@ -197,33 +197,32 @@
 
 def fine_down_kernel(first, prm, *refs):
     if first:
-        whole, side, whole_k, side_k, more, more_k, rhs, field, low, cond, inv, wa, wb, dw = refs
+        whole, side, whole_k, side_k, rhs, field, low, edge, cond, inv, wa, wb, dw = refs
     else:
-        whole, side, more, inv, rhs, field, low, wa, wb, dw = refs
+        whole, side, inv, rhs, field, low, edge, wa, wb, dw = refs
     core = prm[0]
 
-    def assemble(out, own, beside, beyond):
-        @pl.when(core == 0)
-        def _():
-            for t in range(6):
-                out[t] = beside[0, t]
-            for t in range(8):
-                out[6 + t] = own[t]
-            for t in range(2):
-                out[14 + t] = beyond[1, t]
-
-        @pl.when(core == 1)
-        def _():
-            for t in range(2):
-                out[t] = beyond[0, t]
-            for t in range(8):
-                out[2 + t] = own[t]
-            for t in range(6):
-                out[10 + t] = beside[1, t]
-
-    assemble(rhs, whole, side, more)
-    if first:
-        assemble(cond, whole_k, side_k, more_k)
+    @pl.when(core == 0)
+    def _():
+        for t in range(6):
+            rhs[t] = side[0, t]
+            if first:
+                cond[t] = side_k[t]
+        for t in range(8):
+            rhs[6 + t] = whole[t]
+            if first:
+                cond[6 + t] = whole_k[t]
+
+    @pl.when(core == 1)
+    def _():
+        for t in range(8):
+            rhs[t] = whole[t]
+            if first:
+                cond[t] = whole_k[t]
+        for t in range(6):
+            rhs[8 + t] = side[1, t]
+            if first:
+                cond[8 + t] = side_k[t]
 
     if first:
 
@@ -231,13 +230,18 @@
             inv[t] = inverse_of(cond[t], SCALES[0])
             return carry
 
-        lax.fori_loop(0, 16, fill, 0)
+        lax.fori_loop(0, 14, fill, 0)
     steps = chebyshev(DEGREE)
-    first_step(0, 16, rhs, inv, wa, dw, 4, steps[0][1])
-    sweep(1, 15, wa, wb, 0, dw, rhs, inv, 0, 4, SCALES[0], *steps[1])
-    sweep(2, 14, wb, field, -2, dw, rhs, inv, 0, 4, SCALES[0], *steps[2])
+    first_step(0, 14, rhs, inv, wa, dw, 4, steps[0][1])
+    sweep(1, 13, wa, wb, 0, dw, rhs, inv, 0, 4, SCALES[0], *steps[1])
+    sweep(2, 12, wb, field, -2, dw, rhs, inv, 0, 4, SCALES[0], *steps[2])
+    for q in range(2):
+        for d in range(4):
+            for c in range(4):
+                row = 8 * ((q * 4 + d) * 4 + c)
+                edge[row : row + 8, :] = field[4 + q, d, :, lanes(c)]
     for t in range(2):
-        z = 6 + 2 * t
+        z = 6 - 2 * core + 2 * t
         one = residual_plane(field, z - 2, rhs, inv, z, 4, SCALES[0])
         two = residual_plane(field, z - 1, rhs, inv, z + 1, 4, SCALES[0])
         mean = halve(one, two, 4)
@@ -301,26 +305,30 @@
         start, send, cond, inv, rhs, wa, wb, dw = refs
     else:
         cond, inv, start, send, rhs, wa, wb, dw = refs
-    core, half = prm[0], prm[3]
-    for t in range(12):
-        if t < 4:
-            ref, at = far.at[0], t
-        elif t < 8:
-            ref, at = block, t - 4
-        else:
-            ref, at = far.at[1], t - 8
-        rhs[t, 0] = ref[at // 2, 0, at % 2]
-        if first:
-            value = ref[at // 2, 1, at % 2]
-            cond[t, 0] = value
-            inv[t, 0] = inverse_of(value, SCALES[2])
+    core = prm[0]
+    parts = 2 if first else 1
+    for a in range(parts):
+        for t in range(10):
+            if t < 4:
+                row = 256 + 48 * (a + parts * (1 - t // 2)) + 24 * (t % 2)
+                value = far[0, row : row + 24, :]
+            elif t < 6:
+                value = block[a, t - 4]
+            else:
+                row = 256 + 48 * (a + parts * (t // 2 - 3)) + 24 * (t % 2)
+                value = far[1, row : row + 24, :]
+            if a == 0:
+                rhs[t, 0] = value
+            else:
+                cond[t, 0] = value
+                inv[t, 0] = inverse_of(value, SCALES[2])
     steps = chebyshev(COARSE_DEGREE)
-    first_step(0, 12, rhs, inv, wa, dw, 1, steps[0][1], group=12)
-    sweep(1, 11, wa, wb, 0, dw, rhs, inv, 0, 1, SCALES[2], *steps[1], group=10)
-    sweep(2, 10, wb, wa, 0, dw, rhs, inv, 0, 1, SCALES[2], *steps[2], group=8)
-    sweep(3, 9, wa, wb, 0, dw, rhs, inv, 0, 1, SCALES[2], *steps[3], group=6)
+    first_step(0, 10, rhs, inv, wa, dw, 1, steps[0][1], group=10)
+    sweep(1, 9, wa, wb, 0, dw, rhs, inv, 0, 1, SCALES[2], *steps[1], group=8)
+    sweep(2, 8, wb, wa, 0, dw, rhs, inv, 0, 1, SCALES[2], *steps[2], group=6)
+    sweep(3, 7, wa, wb, 0, dw, rhs, inv, 0, 1, SCALES[2], *steps[3], group=4)
     for u in range(8):
-        t = 3 + 2 * half + u // 2
+        t = 3 + u // 2
         value = wb[t, 0] / cond[t, 0]
         value = jnp.concatenate([value[0:8], value[16:24]], axis=0)
         k = load_ends(mid_cond, u + 2, 2)
@@ -332,12 +340,19 @@
         send[t] = start[4 - 3 * core + t]
 
 
-def up_kernel(last, prm, start, side, more, mid_rhs, mid_cond, mid_inv, rhs, fine, cond, inv, *refs):
+def up_kernel(last, prm, start, side, more, far, mid_rhs, mid_cond, mid_inv, rhs, fine, cond, inv, *refs):
     if last:
         before, adjoint, remain, mid_a, mid_b, mid_dw, wa, wb, dw = refs
     else:
         adjoint, remain, mid_a, mid_b, mid_dw, wa, wb, dw = refs
     core = prm[0]
+
+    def beyond(other, at):
+        for q in range(2):
+            for d in range(4):
+                for c in range(4):
+                    row = 8 * ((q * 4 + d) * 4 + c)
+                    wa[at + q, d, :, lanes(c)] = far[other, row : row + 8, :]
 
     @pl.when(core == 0)
     def _():
@@ -346,6 +361,9 @@
         for t in range(8):
             mid_a[3 + t] = start[t]
         mid_a[11] = more[1]
+        for t in range(10):
+            wa[t] = fine[t]
+        beyond(1, 10)
 
     @pl.when(core == 1)
     def _():
@@ -354,6 +372,9 @@
             mid_a[1 + t] = start[t]
         for t in range(3):
             mid_a[9 + t] = side[1, t]
+        for t in range(10):
+            wa[2 + t] = fine[t]
+        beyond(0, 0)
 
     steps = chebyshev(DEGREE)
     shift = 2 * core - 1
@@ -362,6 +383,7 @@
     sweep(3, 9, mid_a, mid_b, 0, mid_dw, mid_rhs, mid_inv, shift, 2, SCALES[1], *steps[2], loader=load_ends, group=2)
 
     near = lax.broadcasted_iota(jnp.int32, (8, LANES), 0) < 6
+    ahead = 2 - 2 * core
 
     def correct(t, carry):
         k = load_ends(mid_cond, t + shift, 2)
@@ -373,19 +395,21 @@
                     v = 2 * (t - 3) + z
                     for dd in (2 * d, 2 * d + 1):
                         for cc in (2 * c, 2 * c + 1):
-                            wa[v, dd, :, lanes(cc)] = fine[v, dd, :, lanes(cc)] + cond[v + 2, dd, :, lanes(cc)] * value
+                            wa[v, dd, :, lanes(cc)] = (
+                                wa[v, dd, :, lanes(cc)] + cond[v + ahead, dd, :, lanes(cc)] * value
+                            )
         return carry
 
     lax.fori_loop(3, 9, correct, 0)
-    sweep(1, 11, wa, wb, 0, dw, rhs, inv, 2, 4, SCALES[0], *steps[0])
-    sweep(2, 10, wb, wa, 0, dw, rhs, inv, 2, 4, SCALES[0], *steps[1])
-    sweep(3, 9, wa, wb, 0, dw, rhs, inv, 2, 4, SCALES[0], *steps[2])
+    sweep(1, 11, wa, wb, 0, dw, rhs, inv, ahead, 4, SCALES[0], *steps[0])
+    sweep(2, 10, wb, wa, 0, dw, rhs, inv, ahead, 4, SCALES[0], *steps[1])
+    sweep(3, 9, wa, wb, 0, dw, rhs, inv, ahead, 4, SCALES[0], *steps[2])
 
     def finish(t, carry):
-        left = residual_plane(wb, t + 4, rhs, inv, t + 6, 4, SCALES[0])
+        left = residual_plane(wb, t + 4, rhs, inv, t + 4 + ahead, 4, SCALES[0])
         for d in range(4):
             for c in range(4):
-                value = wb[t + 4, d, :, lanes(c)] / cond[t + 6, d, :, lanes(c)]
+                value = wb[t + 4, d, :, lanes(c)] / cond[t + 4 + ahead, d, :, lanes(c)]
                 value = value[0:4]
                 if last:
                     value = value + before[t, d, :, lanes(c)]
@@ -432,6 +456,14 @@
     return gather(value, (1,), 1, 2)
 
 
+def swap(value, step):
+    devices = lax.axis_size("gz")
+    ways = []
+    for i in range(1, devices, 2):
+        ways += [(i, (i + step) % devices), ((i + step) % devices, i)]
+    return lax.ppermute(value, "gz", ways)
+
+
 def row_pairs(value):
     planes, rows = lax.axis_size("gz"), lax.axis_size("gy")
     members = []
@@ -449,8 +481,7 @@
     z = lax.axis_index("gz")
     y = lax.axis_index("gy")
     core = z % 2
-    half = (z % 4) // 2
-    prm = jnp.stack([core, y % 2, y, half]).astype(jnp.int32)
+    prm = jnp.stack([core, y % 2, y, z]).astype(jnp.int32)
     place = (core + y) % 2
     (remain,) = call(
         prepare_kernel, [f32(4, 8, 4, 512)], [(4, 128, 128)], source, conduct, scalars=False, name="prepare"
@@ -473,22 +504,21 @@
             halves,
             name="rows",
         )
-        args, mores = [prm], []
-        for a in range(parts):
-            side = across(laid[2 * a + 1])
-            args += [laid[2 * a], side]
-            flat = side.reshape(12, *side.shape[2:])
-            mores.append(cores(lax.dynamic_slice_in_dim(flat, 4 + 2 * core, 2, 0)))
-        args += mores
-        outs = [f32(16, 4, 8, 512), f32(12, 4, 8, 512), f32(parts, 2, 2, 4, 256)]
-        state = [f32(16, 4, 8, 512)] * 2
-        scratch = [(16, 4, 8, 512)] * 3
+        args = [prm]
+        if first:
+            side_k = swap(laid[3], 1)
+        args += [laid[0], across(laid[1])]
+        if first:
+            args += [laid[2], side_k]
+        outs = [f32(14, 4, 8, 512), f32(10, 4, 8, 512), f32(parts, 2, 2, 4, 256), f32(256, 128)]
+        state = [f32(14, 4, 8, 512)] * 2
+        scratch = [(14, 4, 8, 512)] * 3
         body = functools.partial(fine_down_kernel, first)
         if first:
-            rhs0, field0, low, cond0, inv0 = call(body, outs + state, scratch, *args, name="fine_down_first")
+            rhs0, field0, low, edge, cond0, inv0 = call(body, outs + state, scratch, *args, name="fine_down_first")
         else:
             cond0, inv0 = kept[0:2]
-            rhs0, field0, low = call(body, outs, scratch, *args, inv0, name="fine_down")
+            rhs0, field0, low, edge = call(body, outs, scratch, *args, inv0, name="fine_down")
         copies = jnp.broadcast_to(low, (lax.axis_size("gy"), *low.shape))
         rows = lax.all_to_all(copies, "gy", split_axis=0, concat_axis=0, tiled=True)
         (rows,) = call(pick_kernel, [f32(5, parts, 2, 2, 4, 256)], [], prm, rows, name="pick")
@@ -505,27 +535,26 @@
         else:
             cond1, inv1 = kept[2:4]
             rhs1, field1, low = call(body, outs, scratch, prm, chip, far, inv1, name="middle_down")
-        block = gather(low, (0, 1), 2, 4)
-        side = gather(block, (2, 3), 2, 4)
-        far = gather(pick(side, half), (0, 1), 2, 4)
+        beside = [swap(low, 1), swap(low, 3)]
+        far = cores(jnp.concatenate([edge] + [v.reshape(48 * parts, 128) for v in beside], axis=0))
         outs = [f32(8, 2, 16, 256), f32(3, 2, 16, 256)]
-        state = [f32(12, 1, 24, 128)] * 2
-        scratch = [(12, 1, 24, 128)] * 4
+        state = [f32(10, 1, 24, 128)] * 2
+        scratch = [(10, 1, 24, 128)] * 4
         body = functools.partial(coarse_kernel, first)
         if first:
             start, send, cond2, inv2 = call(
-                body, outs + state, scratch, prm, block, far, field1, cond1, name="coarse_first"
+                body, outs + state, scratch, prm, low, far, field1, cond1, name="coarse_first"
             )
         else:
             cond2, inv2 = kept[4:6]
             start, send = call(
-                body, outs, scratch, prm, block, far, field1, cond1, cond2, inv2, name="coarse"
+                body, outs, scratch, prm, low, far, field1, cond1, cond2, inv2, name="coarse"
             )
         side = across(send)
         more = cores(pick(side.reshape(6, *side.shape[2:]), 2 + core))
         outs = [f32(4, 4, 4, 512)] * 2
         scratch = [(12, 2, 16, 256)] * 3 + [(12, 4, 8, 512)] * 3
-        args = [prm, start, side, more, rhs1, cond1, inv1, rhs0, field0, cond0, inv0]
+        args = [prm, start, side, more, far, rhs1, cond1, inv1, rhs0, field0, cond0, inv0]
         if last:
             args.append(adjoint)
         adjoint, remain = call(functools.partial(up_kernel, last), outs, scratch, *args, name="up")

time: 222 us -> 199 us (0.90)
  blocking collectives: 169 us -> 130 us
  starting transfers between devices: 6.32 us -> 20 us
  waiting for transfers between devices: 11.1 us -> 13.4 us
    all_gather x26 -> x18, blocking collectives: 145 us -> 107 us  [gather(): lax.all_gather(value, 'gz', axis_index_groups=pairs(first, step, size))]
    ppermute x0 -> x5, starting transfers between devices: none -> 16.6 us  [swap(): return lax.ppermute(value, 'gz', ways)]
    ppermute x0 -> x5, waiting for transfers between devices: none -> 4.15 us  [swap(): return lax.ppermute(value, 'gz', ways)]
    all_to_all x1, starting transfers between devices: 6.32 us -> 3.41 us  [local(): rows = lax.all_to_all(copies, 'gy', split_axis=0, concat_axis=0, tiled=True)]
    unnamed x14 -> x16, local copies, waits for them, and re-layouts: 3.52 us -> 4.44 us
  transfers between devices with their start and end apart: 1 -> 6, of which waited for: 1 -> 3; matrix products, arithmetic and copies ran while one was open for 0% -> 0% of each run, Pallas kernels for 0% -> 0%
where the time goes in v3:
time: 199 us; the launch traced here: 198 us
  blocking collectives  130 us (65%)
  Pallas kernels  26.8 us (13%)
  starting transfers between devices  20 us (10%)
  waiting for transfers between devices  13.4 us (7%)
  local copies, waits for them, and re-layouts  6.32 us (3%)
    all_gather x18, blocking collectives, gather(): lax.all_gather(value, 'gz', axis_index_groups=pairs(first, step, size))  107 us
    pallas_call x14, Pallas kernels, call(): pl.pallas_call(body, out_shape=outs, in_specs=specs, out_specs=[pl.BlockS...  26.8 us
    ppermute x5, starting transfers between devices, swap(): return lax.ppermute(value, 'gz', ways)  16.6 us
    all_gather x2, blocking collectives, row_pairs(): return lax.all_gather(value, ('gz', 'gy'), axis_index_groups=members)  12.8 us
    all_to_all x1, blocking collectives, local(): rows = lax.all_to_all(copies, 'gy', split_axis=0, concat_axis=0, tiled=True)  10.4 us
    all_to_all x1, waiting for transfers between devices, local(): rows = lax.all_to_all(copies, 'gy', split_axis=0, concat_axis=0, tiled=True)  9.24 us
    unnamed x16, local copies, waits for them, and re-layouts  4.44 us
    ppermute x5, waiting for transfers between devices, swap(): return lax.ppermute(value, 'gz', ways)  4.15 us
  transfers between devices with their start and end apart: 6, of which 3 were waited for; matrix products, arithmetic and copies ran while one was open for 0% of the time, Pallas kernels for 0%

profile of v3, /device:TPU:1, one launch (start us, length us, event | category | flops | bytes accessed | tf_op | source)
XLA Modules:
  0.0 198.4 jit_solution(14298125316408249128)
XLA Ops:
  3.4 12.3 %all-gather = f32[8,8,4,512]{3,1,2,0:T(8,128)S(1)} all-gather(f32[4,8,4,512]{3,1,2,0:T(8,128)S(1)} %copy.4), channel_id=2, replica_groups={{0,8},{16,24},{32,40},{48,56},{64,72},{80,88},{96,104},{112,120},{128,1..., dimensions={0}, use_global_device_ids=true | all-gather | bytes 786432 | tf_op jit(solution)/shard_map/all_gather | solution.py:448
  16.1 7.1 %all-gather.1 = f32[16,8,2,512]{3,1,2,0:T(8,128)S(1)} all-gather(f32[8,8,2,512]{3,1,2,0:T(8,128)S(1)} %slice_select_fusion.1), channel_id=3, replica_groups={{0,1},{2,3},{4,5},{6,7},{9,10},{11,12},{13,14},{15,8},{16,17},{18,19},{..., dimensions={0}, use_global_device_ids=true | all-gather | bytes 786432 | tf_op jit(solution)/shard_map/all_gather | solution.py:473
  28.7 11.5 %all-gather.2 = f32[12,4,8,512]{3,2,1,0:T(8,128)S(1)} all-gather(f32[6,4,8,512]{3,2,1,0:T(8,128)S(1)} %get-tuple-element.37), channel_id=4, replica_groups={{8,16},{24,32},{40,48},{56,64},{72,80},{88,96},{104,112},{120,128},{136..., dimensions={0}, use_global_device_ids=true | all-gather | bytes 1179648 | tf_op jit(solution)/shard_map/all_gather | solution.py:448
  40.2 3.4 %fine_down_first.1 = (f32[14,4,8,512]{3,2,1,0:T(8,128)S(1)}, f32[10,4,8,512]{3,2,1,0:T(8,128)S(1)}, f32[2,2,2,4,256]{4,3,2,1,0:T(4,128)S(1)}, f32[256,128]{1,0:T...) custom-call(s32[4]{0:T(128)S(1)} %pad_add_fusion.prm, ...), custom_call_target="tpu_custom_call" | custom-call | tf_op jit(solution)/shard_map/fine_down_first/pallas_call | solution.py:431
  46.2 3.4 %all-to-all-start = ((f32[8,2,2,2,4,256]{5,4,3,2,1,0:T(4,128)}), f32[8,2,2,2,4,256]{5,4,3,2,1,0:T(4,128)S(1)}, u32[]{:S(2)}, u32[]{:S(2)}) async-start(f32[8,2,2,2,4,256]{5,4,3,2,1,0:T(4,128)} %broadcast_in_dim.6), calls=%async_computation | async-start | bytes 524288 | tf_op jit(solution)/shard_map/all_to_all | solution.py:523
  49.6 9.2 %all-to-all-done.rows = f32[8,2,2,2,4,256]{5,4,3,2,1,0:T(4,128)S(1)} async-done(((f32[8,2,2,2,4,256]{5,4,3,2,1,0:T(4,128)}), f32[8,2,2,2,4,256]{5,4,3,2,1,0:T(4,128)S(1)}, u32[]{:S(2)}, u32[]{:S(2)}) %all-to-all-start) | async-done | bytes 262176 | tf_op jit(solution)/shard_map/all_to_all | solution.py:523
  59.4 12.2 %all-gather.3 = f32[10,2,2,2,4,256]{5,4,3,2,1,0:T(4,128)S(1)} all-gather(f32[5,2,2,2,4,256]{5,4,3,2,1,0:T(4,128)S(1)} %pick.2), channel_id=5, replica_groups={{0,8},{16,24},{32,40},{48,56},{64,72},{80,88},{96,104},{112,120},{128,1..., dimensions={0}, use_global_device_ids=true | all-gather | bytes 491520 | tf_op jit(solution)/shard_map/all_gather | solution.py:448
  71.7 7.5 %all-gather.4 = f32[4,5,2,2,2,4,256]{6,5,4,3,2,1,0:T(4,128)S(1)} all-gather(f32[2,5,2,2,2,4,256]{6,5,4,3,2,1,0:T(4,128)S(1)} %bitcast.31), channel_id=6, replica_groups={{8,16},{24,32},{40,48},{56,64},{72,80},{88,96},{104,112},{120,128},{136..., dimensions={0}, use_global_device_ids=true | all-gather | bytes 983040 | tf_op jit(solution)/shard_map/all_gather | solution.py:448
  79.2 5.3 %all_gather.119.far = f32[2,2,5,2,2,2,4,256]{7,6,5,4,3,2,1,0:T(4,128)S(1)} all-gather(f32[1,2,5,2,2,2,4,256]{7,6,5,4,3,2,1,0:T(4,128)S(1)} %constant_dynamic-slice_fusion.3), channel_id=1, replica_groups={{0,8},{16,24},{32,40},{48,56},{64,72},{80,88},{96,104},{112,120},{128,1..., dimensions={0}, use_global_device_ids=true | all-gather | bytes 983040 | tf_op jit(solution)/shard_map/all_gather | solution.py:448
  90.0 6.0 %collective-permute-start.1 = (f32[2,2,24,128]{3,2,1,0:T(8,128)}, f32[2,2,24,128]{3,2,1,0:T(8,128)}, u32[]{:S(2)}, u32[]{:S(2)}) collective-permute-start(f32[2,2,24,128]{3,2,1,0:T(8,128)} %get-tuple-element.41.block), channel_id=1, source_target_pairs={{8,16},{16,8},{24,32},{32,24},{40,48},{48,40},{56,64},{64,56},{72,... | collective-permute-start | bytes 147464 | tf_op jit(solution)/shard_map/ppermute | solution.py:464
  103.4 4.7 %all-gather.6 = f32[6,2,16,256]{3,2,1,0:T(8,128)S(1)} all-gather(f32[3,2,16,256]{3,2,1,0:T(8,128)S(1)} %get-tuple-element.46), channel_id=8, replica_groups={{8,16},{24,32},{40,48},{56,64},{72,80},{88,96},{104,112},{120,128},{136..., dimensions={0}, use_global_device_ids=true | all-gather | bytes 294912 | tf_op jit(solution)/shard_map/all_gather | solution.py:448
  108.1 5.2 %all_gather.124.more = f32[2,2,16,256]{3,2,1,0:T(8,128)S(1)} all-gather(f32[1,2,16,256]{3,2,1,0:T(8,128)S(1)} %constant_dynamic-slice_fusion.2), channel_id=1, replica_groups={{0,8},{16,24},{32,40},{48,56},{64,72},{80,88},{96,104},{112,120},{128,1..., dimensions={0}, use_global_device_ids=true | all-gather | bytes 98304 | tf_op jit(solution)/shard_map/all_gather | solution.py:448
  113.3 4.4 %up.2 = (f32[4,4,4,512]{3,2,1,0:T(4,128)S(1)}, f32[4,4,4,512]{3,2,1,0:T(4,128)S(1)}) custom-call(s32[4]{0:T(128)S(1)} %pad_add_fusion.prm, f32[8,2,16,256]{3,2,1,0:T(8,128)S(1)} %get-tuple-element.45.start, f32[2,3,2,16,256]{4,3,2,1,0:T(8,128)S(1)} %bitcast.40, f32[2,2,16,256]{3,2,1,0:T(8,128)S(1)} %all_gather.124.more, f32[2,448,128]{2,1,0:T(8,128)S(1)} %bitcast.26, ...), custom_call_target="tpu_custom_call" | custom-call | tf_op jit(solution)/shard_map/up/pallas_call | solution.py:431
  119.8 5.7 %all-gather.8 = f32[16,4,2,512]{3,1,2,0:T(4,128)S(1)} all-gather(f32[8,4,2,512]{3,1,2,0:T(4,128)S(1)} %copy.7), channel_id=10, replica_groups={{0,1},{2,3},{4,5},{6,7},{9,10},{11,12},{13,14},{15,8},{16,17},{18,19},{..., dimensions={0}, use_global_device_ids=true | all-gather | bytes 393216 | tf_op jit(solution)/shard_map/all_gather | solution.py:473
  128.5 8.2 %all-gather.9 = f32[12,4,8,512]{3,2,1,0:T(8,128)S(1)} all-gather(f32[6,4,8,512]{3,2,1,0:T(8,128)S(1)} %get-tuple-element.55), channel_id=11, replica_groups={{8,16},{24,32},{40,48},{56,64},{72,80},{88,96},{104,112},{120,128},{136..., dimensions={0}, use_global_device_ids=true | all-gather | bytes 1179648 | tf_op jit(solution)/shard_map/all_gather | solution.py:448
  139.7 10.4 %all_to_all.10.rows = f32[8,1,2,2,4,256]{5,4,3,2,1,0:T(4,128)S(1)} all-to-all(f32[8,1,2,2,4,256]{5,4,3,2,1,0:T(4,128)S(1)} %broadcast_in_dim.7), channel_id=1, replica_groups=mesh['gz'=96,'gy'=8] {'gy'}, dimensions={0} | all-to-all | bytes 262144 | tf_op jit(solution)/shard_map/all_to_all | solution.py:523
  150.6 5.9 %all-gather.10 = f32[10,1,2,2,4,256]{5,4,3,2,1,0:T(4,128)S(1)} all-gather(f32[5,1,2,2,4,256]{5,4,3,2,1,0:T(4,128)S(1)} %pick.3), channel_id=12, replica_groups={{0,8},{16,24},{32,40},{48,56},{64,72},{80,88},{96,104},{112,120},{128,1..., dimensions={0}, use_global_device_ids=true | all-gather | bytes 245760 | tf_op jit(solution)/shard_map/all_gather | solution.py:448
  156.6 5.7 %all-gather.11 = f32[4,5,1,2,2,4,256]{6,5,4,3,2,1,0:T(4,128)S(1)} all-gather(f32[2,5,1,2,2,4,256]{6,5,4,3,2,1,0:T(4,128)S(1)} %bitcast.36), channel_id=13, replica_groups={{8,16},{24,32},{40,48},{56,64},{72,80},{88,96},{104,112},{120,128},{136..., dimensions={0}, use_global_device_ids=true | all-gather | bytes 491520 | tf_op jit(solution)/shard_map/all_gather | solution.py:448
  162.3 5.1 %all_gather.136.far = f32[2,2,5,1,2,2,4,256]{7,6,5,4,3,2,1,0:T(4,128)S(1)} all-gather(f32[1,2,5,1,2,2,4,256]{7,6,5,4,3,2,1,0:T(4,128)S(1)} %constant_dynamic-slice_fusion.1), channel_id=1, replica_groups={{0,8},{16,24},{32,40},{48,56},{64,72},{80,88},{96,104},{112,120},{128,1..., dimensions={0}, use_global_device_ids=true | all-gather | bytes 491520 | tf_op jit(solution)/shard_map/all_gather | solution.py:448
  171.2 4.9 %collective-permute-start.3 = (f32[1,2,24,128]{3,2,1,0:T(8,128)S(1)}, f32[1,2,24,128]{3,2,1,0:T(8,128)S(1)}, u32[]{:S(2)}, u32[]{:S(2)}) collective-permute-start(f32[1,2,24,128]{3,2,1,0:T(8,128)S(1)} %get-tuple-element.57.block), channel_id=1, source_target_pairs={{8,16},{16,8},{24,32},{32,24},{40,48},{48,40},{56,64},{64,56},{72,... | collective-permute-start | bytes 73736 | tf_op jit(solution)/shard_map/ppermute | solution.py:464
  177.8 3.9 %all-gather.12 = f32[704,128]{1,0:T(8,128)S(1)} all-gather(f32[352,128]{1,0:T(8,128)S(1)} %pad_maximum_fusion.1), channel_id=14, replica_groups={{0,8},{16,24},{32,40},{48,56},{64,72},{80,88},{96,104},{112,120},{128,1..., dimensions={0}, use_global_device_ids=true | all-gather | bytes 540672 | tf_op jit(solution)/shard_map/all_gather | solution.py:448
  182.5 4.7 %all-gather.13 = f32[6,2,16,256]{3,2,1,0:T(8,128)S(1)} all-gather(f32[3,2,16,256]{3,2,1,0:T(8,128)S(1)} %get-tuple-element.63), channel_id=15, replica_groups={{8,16},{24,32},{40,48},{56,64},{72,80},{88,96},{104,112},{120,128},{136..., dimensions={0}, use_global_device_ids=true | all-gather | bytes 294912 | tf_op jit(solution)/shard_map/all_gather | solution.py:448
  187.3 5.2 %all_gather.141.more = f32[2,2,16,256]{3,2,1,0:T(8,128)S(1)} all-gather(f32[1,2,16,256]{3,2,1,0:T(8,128)S(1)} %constant_dynamic-slice_fusion), channel_id=1, replica_groups={{0,8},{16,24},{32,40},{48,56},{64,72},{80,88},{96,104},{112,120},{128,1..., dimensions={0}, use_global_device_ids=true | all-gather | bytes 98304 | tf_op jit(solution)/shard_map/all_gather | solution.py:448
  192.5 4.4 %up.3 = (f32[4,4,4,512]{3,2,1,0:T(4,128)S(1)}, f32[4,4,4,512]{3,2,1,0:T(4,128)S(1)}) custom-call(s32[4]{0:T(128)S(1)} %pad_add_fusion.prm, f32[8,2,16,256]{3,2,1,0:T(8,128)S(1)} %get-tuple-element.62.start, f32[2,3,2,16,256]{4,3,2,1,0:T(8,128)S(1)} %bitcast.39, f32[2,2,16,256]{3,2,1,0:T(8,128)S(1)} %all_gather.141.more, f32[2,352,128]{2,1,0:T(8,128)S(1)} %bitcast.28, ...), custom_call_target="tpu_custom_call" | custom-call | tf_op jit(solution)/shard_map/up/pallas_call | solution.py:431
  (59 shorter events, 41.1 us)
Async XLA Ops:
  0.7 0.9 copy-start.6
  1.6 0.9 copy-start.7
  26.8 13.5 %collective-permute-start = (f32[6,4,8,512]{3,2,1,0:T(8,128)S(1)}, f32[6,4,8,512]{3,2,1,0:T(8,128)S(1)}, u32[]{:S(2)}, u32[]{:S(2)}) collective-permute-start(f32[6,4,8,512]{3,2,1,0:T(8,128)S(1)} %get-tuple-element.39), channel_id=1, source_target_pairs={{8,16},{16,8},{24,32},{32,24},{40,48},{48,40},{56,64},{64,56},{72,... | collective-permute-start | bytes 1179656 | tf_op jit(solution)/shard_map/ppermute | solution.py:464
  43.6 0.9 copy-start
  44.6 0.9 copy-start.2
  46.2 12.7 %all-to-all-start = ((f32[8,2,2,2,4,256]{5,4,3,2,1,0:T(4,128)}), f32[8,2,2,2,4,256]{5,4,3,2,1,0:T(4,128)S(1)}, u32[]{:S(2)}, u32[]{:S(2)}) async-start(f32[8,2,2,2,4,256]{5,4,3,2,1,0:T(4,128)} %broadcast_in_dim.6), calls=%async_computation | async-start | bytes 524288 | tf_op jit(solution)/shard_map/all_to_all | solution.py:523
  87.3 0.8 copy-start.4
  88.1 7.9 %collective-permute-start.2 = (f32[2,2,24,128]{3,2,1,0:T(8,128)}, f32[2,2,24,128]{3,2,1,0:T(8,128)}, u32[]{:S(2)}, u32[]{:S(2)}) collective-permute-start(f32[2,2,24,128]{3,2,1,0:T(8,128)} %get-tuple-element.41.block), channel_id=1, source_target_pairs={{8,32},{32,8},{24,48},{48,24},{40,64},{64,40},{56,80},{80,56},{72,... | collective-permute-start | bytes 147464 | tf_op jit(solution)/shard_map/ppermute | solution.py:464
  90.0 8.3 %collective-permute-start.1 = (f32[2,2,24,128]{3,2,1,0:T(8,128)}, f32[2,2,24,128]{3,2,1,0:T(8,128)}, u32[]{:S(2)}, u32[]{:S(2)}) collective-permute-start(f32[2,2,24,128]{3,2,1,0:T(8,128)} %get-tuple-element.41.block), channel_id=1, source_target_pairs={{8,16},{16,8},{24,32},{32,24},{40,48},{48,40},{56,64},{64,56},{72,... | collective-permute-start | bytes 147464 | tf_op jit(solution)/shard_map/ppermute | solution.py:464
  99.2 14.1 %copy-start.5 = (f32[12,2,24,256]{3,2,1,0:T(8,128)S(1)}, f32[12,2,24,256]{3,2,1,0:T(8,128)}, u32[]{:S(2)}) copy-start(f32[12,2,24,256]{3,2,1,0:T(8,128)} %copy-done.4) | copy-start | bytes 1769476
  102.2 11.2 %copy-start.1 = (f32[14,4,8,512]{3,2,1,0:T(8,128)S(1)}, f32[14,4,8,512]{3,2,1,0:T(8,128)}, u32[]{:S(2)}) copy-start(f32[14,4,8,512]{3,2,1,0:T(8,128)} %copy-done) | copy-start | bytes 2752516
  102.2 11.2 %copy-start.3 = (f32[10,4,8,512]{3,2,1,0:T(8,128)S(1)}, f32[10,4,8,512]{3,2,1,0:T(8,128)}, u32[]{:S(2)}) copy-start(f32[10,4,8,512]{3,2,1,0:T(8,128)} %copy-done.2) | copy-start | bytes 1966084
  169.2 6.8 %collective-permute-start.4 = (f32[1,2,24,128]{3,2,1,0:T(8,128)S(1)}, f32[1,2,24,128]{3,2,1,0:T(8,128)S(1)}, u32[]{:S(2)}, u32[]{:S(2)}) collective-permute-start(f32[1,2,24,128]{3,2,1,0:T(8,128)S(1)} %get-tuple-element.57.block), channel_id=1, source_target_pairs={{8,32},{32,8},{24,48},{48,24},{40,64},{64,40},{56,80},{80,56},{72,... | collective-permute-start | bytes 73736 | tf_op jit(solution)/shard_map/ppermute | solution.py:464
  171.2 6.7 %collective-permute-start.3 = (f32[1,2,24,128]{3,2,1,0:T(8,128)S(1)}, f32[1,2,24,128]{3,2,1,0:T(8,128)S(1)}, u32[]{:S(2)}, u32[]{:S(2)}) collective-permute-start(f32[1,2,24,128]{3,2,1,0:T(8,128)S(1)} %get-tuple-element.57.block), channel_id=1, source_target_pairs={{8,16},{16,8},{24,32},{32,24},{40,48},{48,40},{56,64},{64,56},{72,... | collective-permute-start | bytes 73736 | tf_op jit(solution)/shard_map/ppermute | solution.py:464

commit v4 on v3

--- a/solution.py
+++ b/solution.py
@@ -48,6 +48,23 @@
         ]
         for d in range(size)
     ]
+
+
+def pack(ref, row, tiles):
+    for d in range(2):
+        for c in range(2):
+            at = row + 16 * (2 * d + c)
+            ref[at : at + 16, :] = tiles[d][c]
+
+
+def unpack(ref, core, row):
+    return [[ref[core, row + 16 * (2 * d + c) : row + 16 * (2 * d + c) + 16, :] for c in range(2)] for d in range(2)]
+
+
+def store(ref, z, tiles):
+    for d, line in enumerate(tiles):
+        for c, tile in enumerate(line):
+            ref[z, d, :, lanes(c)] = tile
 
 
 def neighbours(below, here, above, size):
@@ -247,12 +264,14 @@
         mean = halve(one, two, 4)
         for d in range(2):
             for c in range(2):
-                low[0, t, d, :, lanes(c)] = mean[d][c][0:4]
+                for r in range(8):
+                    low[r, 0, t, d, :, lanes(c)] = mean[d][c][0:4]
         if first:
             mean = halve(load(cond, z, 4), load(cond, z + 1, 4), 4)
             for d in range(2):
                 for c in range(2):
-                    low[1, t, d, :, lanes(c)] = mean[d][c][0:4]
+                    for r in range(8):
+                        low[r, 1, t, d, :, lanes(c)] = mean[d][c][0:4]
 
 
 def pick_kernel(prm, rows, out):
@@ -262,9 +281,10 @@
 
 def middle_down_kernel(first, prm, chip, far, *refs):
     if first:
-        rhs, field, low, cond, inv, wa, wb, dw = refs
+        rhs, field, low, near, cond, inv, wa, wb, dw = refs
     else:
-        inv, rhs, field, low, wa, wb, dw = refs
+        inv, rhs, field, low, near, wa, wb, dw = refs
+    core = prm[0]
     for t in range(12):
         if t < 4:
             ref, at = far.at[0], t
@@ -298,54 +318,66 @@
         low[0, h] = halve(one, two, 2)[0][0]
         if first:
             low[1, h] = halve(load(cond, z, 2), load(cond, z + 1, 2), 2)[0][0]
-
-
-def coarse_kernel(first, prm, block, far, middle, mid_cond, *refs):
-    if first:
-        start, send, cond, inv, rhs, wa, wb, dw = refs
+    for t in range(3):
+        pack(near, 64 * t, load_ends(field, 4 - 3 * core + t, 2))
+    at = 192
+    if first:
+        pack(near, at, load_ends(cond, 8 - 5 * core, 2))
+        at += 64
+    for a in range(2 if first else 1):
+        for h in range(2):
+            row = at + 48 * a + 24 * h
+            near[row : row + 24, :] = low[a, h]
+
+
+def up_kernel(first, prm, low, far, middle, mid_rhs, mid_cond, mid_inv, fine, rhs, cond, inv, *refs):
+    if first:
+        adjoint, remain, ends, low_cond, low_inv = refs[:5]
     else:
-        cond, inv, start, send, rhs, wa, wb, dw = refs
+        ends, low_cond, low_inv, before, adjoint, remain = refs[:6]
+    low_rhs, la, lb, ldw, start, mid_a, mid_b, mid_dw, wa, wb, dw = refs[-11:]
     core = prm[0]
     parts = 2 if first else 1
+    base = 256 + 192 + (64 if first else 0)
+
     for a in range(parts):
-        for t in range(10):
-            if t < 4:
-                row = 256 + 48 * (a + parts * (1 - t // 2)) + 24 * (t % 2)
+        for t in range(14):
+            if t < 6:
+                row = base + 48 * parts * (2 - t // 2) + 48 * a + 24 * (t % 2)
                 value = far[0, row : row + 24, :]
-            elif t < 6:
-                value = block[a, t - 4]
+            elif t < 8:
+                value = low[a, t - 6]
             else:
-                row = 256 + 48 * (a + parts * (t // 2 - 3)) + 24 * (t % 2)
+                row = base + 48 * parts * (t // 2 - 4) + 48 * a + 24 * (t % 2)
                 value = far[1, row : row + 24, :]
             if a == 0:
-                rhs[t, 0] = value
+                low_rhs[t, 0] = value
             else:
-                cond[t, 0] = value
-                inv[t, 0] = inverse_of(value, SCALES[2])
+                low_cond[t, 0] = value
+                low_inv[t, 0] = inverse_of(value, SCALES[2])
     steps = chebyshev(COARSE_DEGREE)
-    first_step(0, 10, rhs, inv, wa, dw, 1, steps[0][1], group=10)
-    sweep(1, 9, wa, wb, 0, dw, rhs, inv, 0, 1, SCALES[2], *steps[1], group=8)
-    sweep(2, 8, wb, wa, 0, dw, rhs, inv, 0, 1, SCALES[2], *steps[2], group=6)
-    sweep(3, 7, wa, wb, 0, dw, rhs, inv, 0, 1, SCALES[2], *steps[3], group=4)
-    for u in range(8):
-        t = 3 + u // 2
-        value = wb[t, 0] / cond[t, 0]
+    first_step(0, 14, low_rhs, low_inv, la, ldw, 1, steps[0][1], group=14)
+    sweep(1, 13, la, lb, 0, ldw, low_rhs, low_inv, 0, 1, SCALES[2], *steps[1], group=6)
+    sweep(2, 12, lb, la, 0, ldw, low_rhs, low_inv, 0, 1, SCALES[2], *steps[2], group=5)
+    sweep(3, 11, la, lb, 0, ldw, low_rhs, low_inv, 0, 1, SCALES[2], *steps[3], group=4)
+
+    for t in range(3):
+        store(start, t, unpack(far, 0, 256 + 64 * t))
+        store(start, 11 + t, unpack(far, 1, 256 + 64 * t))
+    for t in range(8):
+        store(start, 3 + t, load_ends(middle, t, 2))
+    if first:
+        store(ends, 0, unpack(far, 0, 448))
+        store(ends, 13, unpack(far, 1, 448))
+        for t in range(12):
+            store(ends, 1 + t, load_ends(mid_cond, t, 2))
+    for t in range(12):
+        at = (t + 1) // 2 + 3 + core
+        value = lb[at, 0] / low_cond[at, 0]
         value = jnp.concatenate([value[0:8], value[16:24]], axis=0)
-        k = load_ends(mid_cond, u + 2, 2)
-        w = load_ends(middle, u, 2)
-        for d in range(2):
-            for c in range(2):
-                start[u, d, :, lanes(c)] = w[d][c] + k[d][c] * value
-    for t in range(3):
-        send[t] = start[4 - 3 * core + t]
-
-
-def up_kernel(last, prm, start, side, more, far, mid_rhs, mid_cond, mid_inv, rhs, fine, cond, inv, *refs):
-    if last:
-        before, adjoint, remain, mid_a, mid_b, mid_dw, wa, wb, dw = refs
-    else:
-        adjoint, remain, mid_a, mid_b, mid_dw, wa, wb, dw = refs
-    core = prm[0]
+        here = load(start, t + 2 * core, 2)
+        k = load(ends, t + 2 * core, 2)
+        store(mid_a, t, [[here[d][c] + k[d][c] * value for c in range(2)] for d in range(2)])
 
     def beyond(other, at):
         for q in range(2):
@@ -356,22 +388,12 @@
 
     @pl.when(core == 0)
     def _():
-        for t in range(3):
-            mid_a[t] = side[0, t]
-        for t in range(8):
-            mid_a[3 + t] = start[t]
-        mid_a[11] = more[1]
         for t in range(10):
             wa[t] = fine[t]
         beyond(1, 10)
 
     @pl.when(core == 1)
     def _():
-        mid_a[0] = more[0]
-        for t in range(8):
-            mid_a[1 + t] = start[t]
-        for t in range(3):
-            mid_a[9 + t] = side[1, t]
         for t in range(10):
             wa[2 + t] = fine[t]
         beyond(0, 0)
@@ -386,7 +408,7 @@
     ahead = 2 - 2 * core
 
     def correct(t, carry):
-        k = load_ends(mid_cond, t + shift, 2)
+        k = load(ends, t + 2 * core, 2)
         for d in range(2):
             for c in range(2):
                 value = mid_b[t, d, :, lanes(c)] / k[d][c]
@@ -411,7 +433,7 @@
             for c in range(4):
                 value = wb[t + 4, d, :, lanes(c)] / cond[t + 4 + ahead, d, :, lanes(c)]
                 value = value[0:4]
-                if last:
+                if not first:
                     value = value + before[t, d, :, lanes(c)]
                 adjoint[t, d, :, lanes(c)] = value
                 remain[t, d, :, lanes(c)] = left[d][c][0:4]
@@ -425,7 +447,7 @@
 
 
 def call(body, outs, scratch, *args, scalars=True, name=None):
-    specs = [pl.BlockSpec(memory_space=pltpu.VMEM)] * len(args)
+    specs = [pl.BlockSpec(memory_space=pltpu.VMEM) if scalars else pl.BlockSpec()] * len(args)
     if scalars:
         specs[0] = pl.BlockSpec(memory_space=pltpu.SMEM)
     return pl.pallas_call(
@@ -489,7 +511,7 @@
     adjoint = None
     kept = None
     for cycle in range(CYCLES):
-        first, last = cycle == 0, cycle == CYCLES - 1
+        first = cycle == 0
         parts = 2 if first else 1
         chip = cores(remain)
         flat = chip.reshape(8, *chip.shape[2:])
@@ -510,7 +532,7 @@
         args += [laid[0], across(laid[1])]
         if first:
             args += [laid[2], side_k]
-        outs = [f32(14, 4, 8, 512), f32(10, 4, 8, 512), f32(parts, 2, 2, 4, 256), f32(256, 128)]
+        outs = [f32(14, 4, 8, 512), f32(10, 4, 8, 512), f32(8, parts, 2, 2, 4, 256), f32(256, 128)]
         state = [f32(14, 4, 8, 512)] * 2
         scratch = [(14, 4, 8, 512)] * 3
         body = functools.partial(fine_down_kernel, first)
@@ -519,46 +541,35 @@
         else:
             cond0, inv0 = kept[0:2]
             rhs0, field0, low, edge = call(body, outs, scratch, *args, inv0, name="fine_down")
-        copies = jnp.broadcast_to(low, (lax.axis_size("gy"), *low.shape))
-        rows = lax.all_to_all(copies, "gy", split_axis=0, concat_axis=0, tiled=True)
+        rows = lax.all_to_all(low, "gy", split_axis=0, concat_axis=0, tiled=True)
         (rows,) = call(pick_kernel, [f32(5, parts, 2, 2, 4, 256)], [], prm, rows, name="pick")
         chip = cores(rows)
         far = cores(pick(across(chip), core))
-        outs = [f32(12, 2, 24, 256), f32(8, 2, 24, 256), f32(parts, 2, 24, 128)]
+        near_rows = 192 + (64 if first else 0) + 48 * parts
+        outs = [f32(12, 2, 24, 256), f32(8, 2, 24, 256), f32(parts, 2, 24, 128), f32(near_rows, 128)]
         state = [f32(12, 2, 24, 256)] * 2
         scratch = [(12, 2, 24, 256)] * 3
         body = functools.partial(middle_down_kernel, first)
         if first:
-            rhs1, field1, low, cond1, inv1 = call(
+            rhs1, field1, low, near, cond1, inv1 = call(
                 body, outs + state, scratch, prm, chip, far, name="middle_down_first"
             )
         else:
             cond1, inv1 = kept[2:4]
-            rhs1, field1, low = call(body, outs, scratch, prm, chip, far, inv1, name="middle_down")
-        beside = [swap(low, 1), swap(low, 3)]
-        far = cores(jnp.concatenate([edge] + [v.reshape(48 * parts, 128) for v in beside], axis=0))
-        outs = [f32(8, 2, 16, 256), f32(3, 2, 16, 256)]
-        state = [f32(10, 1, 24, 128)] * 2
-        scratch = [(10, 1, 24, 128)] * 4
-        body = functools.partial(coarse_kernel, first)
-        if first:
-            start, send, cond2, inv2 = call(
-                body, outs + state, scratch, prm, low, far, field1, cond1, name="coarse_first"
-            )
+            rhs1, field1, low, near = call(body, outs, scratch, prm, chip, far, inv1, name="middle_down")
+        flat = low.reshape(48 * parts, 128)
+        beside = [swap(near, 1), swap(flat, 3), swap(flat, 5)]
+        far = cores(jnp.concatenate([edge, *beside], axis=0))
+        outs = [f32(4, 4, 4, 512)] * 2
+        scratch = [(14, 1, 24, 128)] * 4 + [(14, 2, 16, 256)] + [(12, 2, 16, 256)] * 3 + [(12, 4, 8, 512)] * 3
+        args = [prm, low, far, field1, rhs1, cond1, inv1, field0, rhs0, cond0, inv0]
+        body = functools.partial(up_kernel, first)
+        if first:
+            state = [f32(14, 2, 16, 256), f32(14, 1, 24, 128), f32(14, 1, 24, 128)]
+            adjoint, remain, *coarse = call(body, outs + state, scratch, *args, name="up_first")
+            kept = (cond0, inv0, cond1, inv1, *coarse)
         else:
-            cond2, inv2 = kept[4:6]
-            start, send = call(
-                body, outs, scratch, prm, low, far, field1, cond1, cond2, inv2, name="coarse"
-            )
-        side = across(send)
-        more = cores(pick(side.reshape(6, *side.shape[2:]), 2 + core))
-        outs = [f32(4, 4, 4, 512)] * 2
-        scratch = [(12, 2, 16, 256)] * 3 + [(12, 4, 8, 512)] * 3
-        args = [prm, start, side, more, far, rhs1, cond1, inv1, rhs0, field0, cond0, inv0]
-        if last:
-            args.append(adjoint)
-        adjoint, remain = call(functools.partial(up_kernel, last), outs, scratch, *args, name="up")
-        kept = (cond0, inv0, cond1, inv1, cond2, inv2)
+            adjoint, remain = call(body, outs, scratch, *args, *kept[4:7], adjoint, name="up")
     return tuple(
         call(
             finish_kernel,

time: 199 us -> 185 us (0.930)
  blocking collectives: 130 us -> 109 us
  starting transfers between devices: 20 us -> 31.6 us
  local copies, waits for them, and re-layouts: 6.32 us -> 3.76 us
    all_gather x18 -> x14, blocking collectives: 107 us -> 85.6 us  [gather(): lax.all_gather(value, 'gz', axis_index_groups=pairs(first, step, size))]
    ppermute x5 -> x7, starting transfers between devices: 16.6 us -> 28.2 us  [swap(): return lax.ppermute(value, 'gz', ways)]
    unnamed x16 -> x8, local copies, waits for them, and re-layouts: 4.44 us -> 2.66 us
    ppermute x5 -> x7, waiting for transfers between devices: 4.15 us -> 3.54 us  [swap(): return lax.ppermute(value, 'gz', ways)]
    pallas_call x14 -> x12, Pallas kernels: 26.8 us -> 26.4 us  [call(): pl.pallas_call(body, out_shape=outs, in_specs=specs, out_specs=[pl.BlockS...]
  transfers between devices with their start and end apart: 6 -> 8, of which waited for: 3 -> 3; matrix products, arithmetic and copies ran while one was open for 0% -> 0% of each run, Pallas kernels for 0% -> 0%
where the time goes in v4:
time: 185 us
  blocking collectives  109 us (59%)
  starting transfers between devices  31.6 us (17%)
  Pallas kernels  26.4 us (14%)
  waiting for transfers between devices  12.8 us (7%)
  local copies, waits for them, and re-layouts  3.76 us (2%)
    all_gather x14, blocking collectives, gather(): lax.all_gather(value, 'gz', axis_index_groups=pairs(first, step, size))  85.6 us
    ppermute x7, starting transfers between devices, swap(): return lax.ppermute(value, 'gz', ways)  28.2 us
    pallas_call x12, Pallas kernels, call(): pl.pallas_call(body, out_shape=outs, in_specs=specs, out_specs=[pl.BlockS...  26.4 us
    all_gather x2, blocking collectives, row_pairs(): return lax.all_gather(value, ('gz', 'gy'), axis_index_groups=members)  12.8 us
    all_to_all x1, blocking collectives, local(): rows = lax.all_to_all(low, 'gy', split_axis=0, concat_axis=0, tiled=True)  10.4 us
    all_to_all x1, waiting for transfers between devices, local(): rows = lax.all_to_all(low, 'gy', split_axis=0, concat_axis=0, tiled=True)  9.24 us
  transfers between devices with their start and end apart: 8, of which 3 were waited for; matrix products, arithmetic and copies ran while one was open for 0% of the time, Pallas kernels for 0%

profile of v4, /device:TPU:1, one launch (start us, length us, event | category | flops | bytes accessed | tf_op | source)
XLA Modules:
  0.0 184.6 jit_solution(1980924283819019575)
XLA Ops:
  3.4 12.3 %all-gather = f32[8,8,4,512]{3,1,2,0:T(8,128)S(1)} all-gather(f32[4,8,4,512]{3,1,2,0:T(8,128)S(1)} %copy.4), channel_id=2, replica_groups={{0,8},{16,24},{32,40},{48,56},{64,72},{80,88},{96,104},{112,120},{128,1..., dimensions={0}, use_global_device_ids=true | all-gather | bytes 786432 | tf_op jit(solution)/shard_map/all_gather | solution.py:470
  16.1 7.1 %all-gather.1 = f32[16,8,2,512]{3,1,2,0:T(8,128)S(1)} all-gather(f32[8,8,2,512]{3,1,2,0:T(8,128)S(1)} %slice_select_fusion.1), channel_id=3, replica_groups={{0,1},{2,3},{4,5},{6,7},{9,10},{11,12},{13,14},{15,8},{16,17},{18,19},{..., dimensions={0}, use_global_device_ids=true | all-gather | bytes 786432 | tf_op jit(solution)/shard_map/all_gather | solution.py:495
  23.3 2.2 %all-gather.12 = f32[16,8,2,512]{3,1,2,0:T(8,128)S(1)} all-gather(f32[8,8,2,512]{3,1,2,0:T(8,128)S(1)} %slice_select_fusion), channel_id=14, replica_groups={{0,8},{16,24},{32,40},{48,56},{64,72},{80,88},{96,104},{112,120},{128,1..., dimensions={0}, use_global_device_ids=true | all-gather | bytes 786432 | tf_op jit(solution)/shard_map/all_gather | solution.py:470
  28.7 11.5 %all-gather.2 = f32[12,4,8,512]{3,2,1,0:T(8,128)S(1)} all-gather(f32[6,4,8,512]{3,2,1,0:T(8,128)S(1)} %get-tuple-element.36), channel_id=4, replica_groups={{8,16},{24,32},{40,48},{56,64},{72,80},{88,96},{104,112},{120,128},{136..., dimensions={0}, use_global_device_ids=true | all-gather | bytes 1179648 | tf_op jit(solution)/shard_map/all_gather | solution.py:470
  40.2 4.1 %fine_down_first.1 = (f32[14,4,8,512]{3,2,1,0:T(8,128)S(1)}, f32[10,4,8,512]{3,2,1,0:T(8,128)S(1)}, f32[8,2,2,2,4,256]{5,4,3,2,1,0:T(4,128)}, f32[256,128]{1,0:T...) custom-call(s32[4]{0:T(128)S(1)} %pad_add_fusion.prm, ...), custom_call_target="tpu_custom_call" | custom-call | tf_op jit(solution)/shard_map/fine_down_first/pallas_call | solution.py:453
  45.2 3.4 %all-to-all-start = ((f32[8,2,2,2,4,256]{5,4,3,2,1,0:T(4,128)}), f32[8,2,2,2,4,256]{5,4,3,2,1,0:T(4,128)S(1)}, u32[]{:S(2)}, u32[]{:S(2)}) async-start(f32[8,2,2,2,4,256]{5,4,3,2,1,0:T(4,128)} %get-tuple-element.39), calls=%async_computation | async-start | bytes 524288 | tf_op jit(solution)/shard_map/all_to_all | solution.py:544
  48.6 9.2 %all-to-all-done.rows = f32[8,2,2,2,4,256]{5,4,3,2,1,0:T(4,128)S(1)} async-done(((f32[8,2,2,2,4,256]{5,4,3,2,1,0:T(4,128)}), f32[8,2,2,2,4,256]{5,4,3,2,1,0:T(4,128)S(1)}, u32[]{:S(2)}, u32[]{:S(2)}) %all-to-all-start) | async-done | bytes 262176 | tf_op jit(solution)/shard_map/all_to_all | solution.py:544
  58.4 12.2 %all-gather.3 = f32[10,2,2,2,4,256]{5,4,3,2,1,0:T(4,128)S(1)} all-gather(f32[5,2,2,2,4,256]{5,4,3,2,1,0:T(4,128)S(1)} %pick.2), channel_id=5, replica_groups={{0,8},{16,24},{32,40},{48,56},{64,72},{80,88},{96,104},{112,120},{128,1..., dimensions={0}, use_global_device_ids=true | all-gather | bytes 491520 | tf_op jit(solution)/shard_map/all_gather | solution.py:470
  70.6 7.5 %all-gather.4 = f32[4,5,2,2,2,4,256]{6,5,4,3,2,1,0:T(4,128)S(1)} all-gather(f32[2,5,2,2,2,4,256]{6,5,4,3,2,1,0:T(4,128)S(1)} %bitcast.23), channel_id=6, replica_groups={{8,16},{24,32},{40,48},{56,64},{72,80},{88,96},{104,112},{120,128},{136..., dimensions={0}, use_global_device_ids=true | all-gather | bytes 983040 | tf_op jit(solution)/shard_map/all_gather | solution.py:470
  78.1 5.3 %all_gather.99.far = f32[2,2,5,2,2,2,4,256]{7,6,5,4,3,2,1,0:T(4,128)S(1)} all-gather(f32[1,2,5,2,2,2,4,256]{7,6,5,4,3,2,1,0:T(4,128)S(1)} %constant_dynamic-slice_fusion.1), channel_id=1, replica_groups={{0,8},{16,24},{32,40},{48,56},{64,72},{80,88},{96,104},{112,120},{128,1..., dimensions={0}, use_global_device_ids=true | all-gather | bytes 983040 | tf_op jit(solution)/shard_map/all_gather | solution.py:470
  83.4 2.2 %middle_down_first.1 = (f32[12,2,24,256]{3,2,1,0:T(8,128)S(1)}, f32[8,2,24,256]{3,2,1,0:T(8,128)S(1)}, f32[2,2,24,128]{3,2,1,0:T(8,128)S(1)}, f32[352,128]{1,0:T...) custom-call(s32[4]{0:T(128)S(1)} %pad_add_fusion.prm, ...), custom_call_target="tpu_custom_call" | custom-call | tf_op jit(solution)/shard_map/middle_down_first/pallas_call | solution.py:453
  89.5 9.3 %collective-permute-start.2 = (f32[96,128]{1,0:T(8,128)S(1)}, f32[96,128]{1,0:T(8,128)S(1)}, u32[]{:S(2)}, u32[]{:S(2)}) collective-permute-start(f32[96,128]{1,0:T(8,128)S(1)} %bitcast.33), channel_id=1, source_target_pairs={{8,32},{32,8},{24,48},{48,24},{40,64},{64,40},{56,80},{80,56},{72,... | collective-permute-start | bytes 147464 | tf_op jit(solution)/shard_map/ppermute | solution.py:486
  100.9 3.4 %all-gather.5 = f32[1600,128]{1,0:T(8,128)S(1)} all-gather(f32[800,128]{1,0:T(8,128)S(1)} %pad_maximum_fusion), channel_id=7, replica_groups={{0,8},{16,24},{32,40},{48,56},{64,72},{80,88},{96,104},{112,120},{128,1..., dimensions={0}, use_global_device_ids=true | all-gather | bytes 1228800 | tf_op jit(solution)/shard_map/all_gather | solution.py:470
  104.3 5.2 %up_first.1 = (f32[4,4,4,512]{3,2,1,0:T(4,128)S(1)}, f32[4,4,4,512]{3,2,1,0:T(4,128)S(1)}, f32[14,2,16,256]{3,2,1,0:T(8,128)S(1)}, f32[14,1,24,128]{3,2,1,0:T(8,128)S(1)}, f32[14,1,24,128]{3,2,1,0:T(8,128)S(1)}) custom-call(s32[4]{0:T(128)S(1)} %pad_add_fusion.prm, f32[2,2,24,128]{3,2,1,0:T(8,128)S(1)} %get-tuple-element.40.low, ...), custom_call_target="tpu_custom_call" | custom-call | tf_op jit(solution)/shard_map/up_first/pallas_call | solution.py:453
  111.6 5.7 %all-gather.7 = f32[16,4,2,512]{3,1,2,0:T(4,128)S(1)} all-gather(f32[8,4,2,512]{3,1,2,0:T(4,128)S(1)} %copy.7), channel_id=9, replica_groups={{0,1},{2,3},{4,5},{6,7},{9,10},{11,12},{13,14},{15,8},{16,17},{18,19},{..., dimensions={0}, use_global_device_ids=true | all-gather | bytes 393216 | tf_op jit(solution)/shard_map/all_gather | solution.py:495
  120.3 9.0 %all-gather.8 = f32[12,4,8,512]{3,2,1,0:T(8,128)S(1)} all-gather(f32[6,4,8,512]{3,2,1,0:T(8,128)S(1)} %get-tuple-element.53), channel_id=10, replica_groups={{8,16},{24,32},{40,48},{56,64},{72,80},{88,96},{104,112},{120,128},{136..., dimensions={0}, use_global_device_ids=true | all-gather | bytes 1179648 | tf_op jit(solution)/shard_map/all_gather | solution.py:470
  129.3 2.9 %fine_down.1 = (f32[14,4,8,512]{3,2,1,0:T(8,128)S(1)}, f32[10,4,8,512]{3,2,1,0:T(8,128)S(1)}, f32[8,1,2,2,4,256]{5,4,3,2,1,0:T(4,128)S(1)}, f32[256,128]{1,0:T(8,128)S(1)}) custom-call(s32[4]{0:T(128)S(1)} %pad_add_fusion.prm, f32[8,4,8,512]{3,2,1,0:T(8,128)S(1)} %get-tuple-element.52.refs_0_, f32[2,6,4,8,512]{4,3,2,1,0:T(8,128)S(1)} %bitcast.22, ...), custom_call_target="tpu_custom_call" | custom-call | tf_op jit(solution)/shard_map/fine_down/pallas_call | solution.py:453
  132.3 10.4 %all_to_all.10.rows = f32[8,1,2,2,4,256]{5,4,3,2,1,0:T(4,128)S(1)} all-to-all(f32[8,1,2,2,4,256]{5,4,3,2,1,0:T(4,128)S(1)} %get-tuple-element.54), channel_id=1, replica_groups=mesh['gz'=96,'gy'=8] {'gy'}, dimensions={0} | all-to-all | bytes 262144 | tf_op jit(solution)/shard_map/all_to_all | solution.py:544
  143.2 5.1 %all-gather.9 = f32[10,1,2,2,4,256]{5,4,3,2,1,0:T(4,128)S(1)} all-gather(f32[5,1,2,2,4,256]{5,4,3,2,1,0:T(4,128)S(1)} %pick.3), channel_id=11, replica_groups={{0,8},{16,24},{32,40},{48,56},{64,72},{80,88},{96,104},{112,120},{128,1..., dimensions={0}, use_global_device_ids=true | all-gather | bytes 245760 | tf_op jit(solution)/shard_map/all_gather | solution.py:470
  148.4 5.7 %all-gather.10 = f32[4,5,1,2,2,4,256]{6,5,4,3,2,1,0:T(4,128)S(1)} all-gather(f32[2,5,1,2,2,4,256]{6,5,4,3,2,1,0:T(4,128)S(1)} %bitcast.29), channel_id=12, replica_groups={{8,16},{24,32},{40,48},{56,64},{72,80},{88,96},{104,112},{120,128},{136..., dimensions={0}, use_global_device_ids=true | all-gather | bytes 491520 | tf_op jit(solution)/shard_map/all_gather | solution.py:470
  154.1 5.1 %all_gather.113.far = f32[2,2,5,1,2,2,4,256]{7,6,5,4,3,2,1,0:T(4,128)S(1)} all-gather(f32[1,2,5,1,2,2,4,256]{7,6,5,4,3,2,1,0:T(4,128)S(1)} %constant_dynamic-slice_fusion), channel_id=1, replica_groups={{0,8},{16,24},{32,40},{48,56},{64,72},{80,88},{96,104},{112,120},{128,1..., dimensions={0}, use_global_device_ids=true | all-gather | bytes 491520 | tf_op jit(solution)/shard_map/all_gather | solution.py:470
  164.9 9.3 %collective-permute-start.5 = (f32[48,128]{1,0:T(8,128)S(1)}, f32[48,128]{1,0:T(8,128)S(1)}, u32[]{:S(2)}, u32[]{:S(2)}) collective-permute-start(f32[48,128]{1,0:T(8,128)S(1)} %bitcast.35), channel_id=1, source_target_pairs={{8,32},{32,8},{24,48},{48,24},{40,64},{64,40},{56,80},{80,56},{72,... | collective-permute-start | bytes 73736 | tf_op jit(solution)/shard_map/ppermute | solution.py:486
  175.7 2.2 %all-gather.11 = f32[1184,128]{1,0:T(8,128)S(1)} all-gather(f32[592,128]{1,0:T(8,128)S(1)} %pad_maximum_fusion.1), channel_id=13, replica_groups={{0,8},{16,24},{32,40},{48,56},{64,72},{80,88},{96,104},{112,120},{128,1..., dimensions={0}, use_global_device_ids=true | all-gather | bytes 909312 | tf_op jit(solution)/shard_map/all_gather | solution.py:470
  178.0 5.1 %up.1 = (f32[4,4,4,512]{3,2,1,0:T(4,128)S(1)}, f32[4,4,4,512]{3,2,1,0:T(4,128)S(1)}) custom-call(s32[4]{0:T(128)S(1)} %pad_add_fusion.prm, f32[1,2,24,128]{3,2,1,0:T(8,128)S(1)} %get-tuple-element.55.low, f32[2,592,128]{2,1,0:T(8,128)S(1)} %bitcast.25, f32[8,2,24,256]{3,2,1,0:T(8,128)S(1)} %get-tuple-element.58.middle, ...), custom_call_target="tpu_custom_call" | custom-call | tf_op jit(solution)/shard_map/up/pallas_call | solution.py:453
  (45 shorter events, 28.1 us)
Async XLA Ops:
  0.7 0.9 copy-start.2
  1.6 0.9 copy-start.3
  26.8 13.5 %collective-permute-start = (f32[6,4,8,512]{3,2,1,0:T(8,128)S(1)}, f32[6,4,8,512]{3,2,1,0:T(8,128)S(1)}, u32[]{:S(2)}, u32[]{:S(2)}) collective-permute-start(f32[6,4,8,512]{3,2,1,0:T(8,128)S(1)} %get-tuple-element.38), channel_id=1, source_target_pairs={{8,16},{16,8},{24,32},{32,24},{40,48},{48,40},{56,64},{64,56},{72,... | collective-permute-start | bytes 1179656 | tf_op jit(solution)/shard_map/ppermute | solution.py:486
  44.3 0.9 copy-start
  45.2 12.7 %all-to-all-start = ((f32[8,2,2,2,4,256]{5,4,3,2,1,0:T(4,128)}), f32[8,2,2,2,4,256]{5,4,3,2,1,0:T(4,128)S(1)}, u32[]{:S(2)}, u32[]{:S(2)}) async-start(f32[8,2,2,2,4,256]{5,4,3,2,1,0:T(4,128)} %get-tuple-element.39), calls=%async_computation | async-start | bytes 524288 | tf_op jit(solution)/shard_map/all_to_all | solution.py:544
  85.7 15.2 %collective-permute-start.1 = (f32[352,128]{1,0:T(8,128)S(1)}, f32[352,128]{1,0:T(8,128)S(1)}, u32[]{:S(2)}, u32[]{:S(2)}) collective-permute-start(f32[352,128]{1,0:T(8,128)S(1)} %get-tuple-element.42), channel_id=1, source_target_pairs={{8,16},{16,8},{24,32},{32,24},{40,48},{48,40},{56,64},{64,56},{72,... | collective-permute-start | bytes 540680 | tf_op jit(solution)/shard_map/ppermute | solution.py:486
  87.6 11.2 %collective-permute-start.3 = (f32[96,128]{1,0:T(8,128)S(1)}, f32[96,128]{1,0:T(8,128)S(1)}, u32[]{:S(2)}, u32[]{:S(2)}) collective-permute-start(f32[96,128]{1,0:T(8,128)S(1)} %bitcast.32), channel_id=1, source_target_pairs={{8,48},{48,8},{24,64},{64,24},{40,80},{80,40},{56,96},{96,56},{72,... | collective-permute-start | bytes 147464 | tf_op jit(solution)/shard_map/ppermute | solution.py:486
  89.5 11.4 %collective-permute-start.2 = (f32[96,128]{1,0:T(8,128)S(1)}, f32[96,128]{1,0:T(8,128)S(1)}, u32[]{:S(2)}, u32[]{:S(2)}) collective-permute-start(f32[96,128]{1,0:T(8,128)S(1)} %bitcast.33), channel_id=1, source_target_pairs={{8,32},{32,8},{24,48},{48,24},{40,64},{64,40},{56,80},{80,56},{72,... | collective-permute-start | bytes 147464 | tf_op jit(solution)/shard_map/ppermute | solution.py:486
  100.9 3.4 %copy-start.1 = (f32[10,4,8,512]{3,2,1,0:T(8,128)S(1)}, f32[10,4,8,512]{3,2,1,0:T(8,128)}, u32[]{:S(2)}) copy-start(f32[10,4,8,512]{3,2,1,0:T(8,128)} %copy-done) | copy-start | bytes 1966084
  161.1 14.6 %collective-permute-start.4 = (f32[240,128]{1,0:T(8,128)S(1)}, f32[240,128]{1,0:T(8,128)S(1)}, u32[]{:S(2)}, u32[]{:S(2)}) collective-permute-start(f32[240,128]{1,0:T(8,128)S(1)} %get-tuple-element.57), channel_id=1, source_target_pairs={{8,16},{16,8},{24,32},{32,24},{40,48},{48,40},{56,64},{64,56},{72,... | collective-permute-start | bytes 368648 | tf_op jit(solution)/shard_map/ppermute | solution.py:486
  163.0 11.2 %collective-permute-start.6 = (f32[48,128]{1,0:T(8,128)S(1)}, f32[48,128]{1,0:T(8,128)S(1)}, u32[]{:S(2)}, u32[]{:S(2)}) collective-permute-start(f32[48,128]{1,0:T(8,128)S(1)} %bitcast.34), channel_id=1, source_target_pairs={{8,48},{48,8},{24,64},{64,24},{40,80},{80,40},{56,96},{96,56},{72,... | collective-permute-start | bytes 73736 | tf_op jit(solution)/shard_map/ppermute | solution.py:486
  164.9 10.8 %collective-permute-start.5 = (f32[48,128]{1,0:T(8,128)S(1)}, f32[48,128]{1,0:T(8,128)S(1)}, u32[]{:S(2)}, u32[]{:S(2)}) collective-permute-start(f32[48,128]{1,0:T(8,128)S(1)} %bitcast.35), channel_id=1, source_target_pairs={{8,32},{32,8},{24,48},{48,24},{40,64},{64,40},{56,80},{80,56},{72,... | collective-permute-start | bytes 73736 | tf_op jit(solution)/shard_map/ppermute | solution.py:486

commit v5 on v4

--- a/solution.py
+++ b/solution.py
@@ -90,42 +90,30 @@
     return out
 
 
-def first_step(lo, hi, rhs, inv, w, dw, size, beta, group=1):
-    def body(step, carry):
-        for z in [lo + step * group + g for g in range(group)]:
-            for d in range(size):
-                for c in range(size):
-                    value = (beta * rhs[z, d, :, lanes(c)]) * inv[z, d, :, lanes(c)]
-                    w[z, d, :, lanes(c)] = value
-                    dw[z, d, :, lanes(c)] = value
-        return carry
-
-    lax.fori_loop(0, (hi - lo) // group, body, 0)
-
-
-def sweep(lo, hi, src, dst, dst_shift, dw, rhs, inv, shift, size, scale, alpha, beta, loader=load, group=1):
-    def body(step, carry):
-        start = lo + step * group
-        planes = {g: load(src, start + g, size) for g in range(-1, group + 1)}
-        done = []
-        for g in range(group):
-            z, here = start + g, planes[g]
-            near = neighbours(planes[g - 1], here, planes[g + 1], size)
-            f = loader(rhs, z + shift, size)
-            i = loader(inv, z + shift, size)
-            for d in range(size):
-                for c in range(size):
-                    q = i[d][c] * (f[d][c] + scale * near[d][c]) - here[d][c]
-                    change = beta * q
-                    if alpha != 0.0:
-                        change = change + alpha * dw[z, d, :, lanes(c)]
-                    done.append((z, d, c, change, here[d][c] + change))
-        for z, d, c, change, value in done:
-            dw[z, d, :, lanes(c)] = change
-            dst[z + dst_shift, d, :, lanes(c)] = value
-        return carry
-
-    lax.fori_loop(0, (hi - lo) // group, body, 0)
+def first_step(lo, hi, rhs, inv, w, dw, size, beta):
+    for z in range(lo, hi):
+        for d in range(size):
+            for c in range(size):
+                value = (beta * rhs[z, d, :, lanes(c)]) * inv[z, d, :, lanes(c)]
+                w[z, d, :, lanes(c)] = value
+                dw[z, d, :, lanes(c)] = value
+
+
+def sweep(lo, hi, src, dst, dst_shift, dw, rhs, inv, shift, size, scale, alpha, beta, loader=load):
+    planes = {z: load(src, z, size) for z in range(lo - 1, hi + 1)}
+    for z in range(lo, hi):
+        here = planes[z]
+        near = neighbours(planes[z - 1], here, planes[z + 1], size)
+        f = loader(rhs, z + shift, size)
+        i = loader(inv, z + shift, size)
+        for d in range(size):
+            for c in range(size):
+                q = i[d][c] * (f[d][c] + scale * near[d][c]) - here[d][c]
+                change = beta * q
+                if alpha != 0.0:
+                    change = change + alpha * dw[z, d, :, lanes(c)]
+                dw[z, d, :, lanes(c)] = change
+                dst[z + dst_shift, d, :, lanes(c)] = here[d][c] + change
 
 
 def residual_plane(src, z, rhs, inv, zr, size, scale):
@@ -176,9 +164,13 @@
     )
 
 
-def prepare_kernel(source, cond, out, work):
-    rows = jnp.concatenate([source[...].reshape(64, 512), cond[...].reshape(64, 512)], axis=0)
-    tiles = reorder(rows, True)
+def prepare_kernel(source, cond, out, both, work, sems):
+    copies = [pltpu.make_async_copy(ref, both.at[a], sems.at[a]) for a, ref in enumerate((source, cond))]
+    for copy in copies:
+        copy.start()
+    for copy in copies:
+        copy.wait()
+    tiles = reorder(both[...].reshape(128, 512), True)
     for c in range(4):
         work[c] = tiles[:, lanes(c)]
     for a in range(2):
@@ -242,12 +234,8 @@
                 cond[8 + t] = side_k[t]
 
     if first:
-
-        def fill(t, carry):
+        for t in range(14):
             inv[t] = inverse_of(cond[t], SCALES[0])
-            return carry
-
-        lax.fori_loop(0, 14, fill, 0)
     steps = chebyshev(DEGREE)
     first_step(0, 14, rhs, inv, wa, dw, 4, steps[0][1])
     sweep(1, 13, wa, wb, 0, dw, rhs, inv, 0, 4, SCALES[0], *steps[1])
@@ -301,16 +289,12 @@
             if first:
                 cond[t, d, 12:16, :] = jnp.ones((4, 256), jnp.float32)
     if first:
-
-        def fill(t, carry):
+        for t in range(12):
             inv[t] = inverse_of(cond[t], SCALES[1])
-            return carry
-
-        lax.fori_loop(0, 12, fill, 0)
     steps = chebyshev(DEGREE)
-    first_step(0, 12, rhs, inv, wa, dw, 2, steps[0][1], group=2)
-    sweep(1, 11, wa, wb, 0, dw, rhs, inv, 0, 2, SCALES[1], *steps[1], group=2)
-    sweep(2, 10, wb, field, -2, dw, rhs, inv, 0, 2, SCALES[1], *steps[2], group=2)
+    first_step(0, 12, rhs, inv, wa, dw, 2, steps[0][1])
+    sweep(1, 11, wa, wb, 0, dw, rhs, inv, 0, 2, SCALES[1], *steps[1])
+    sweep(2, 10, wb, field, -2, dw, rhs, inv, 0, 2, SCALES[1], *steps[2])
     for h in range(2):
         z = 4 + 2 * h
         one = residual_plane(field, z - 2, rhs, inv, z, 2, SCALES[1])
@@ -356,10 +340,10 @@
                 low_cond[t, 0] = value
                 low_inv[t, 0] = inverse_of(value, SCALES[2])
     steps = chebyshev(COARSE_DEGREE)
-    first_step(0, 14, low_rhs, low_inv, la, ldw, 1, steps[0][1], group=14)
-    sweep(1, 13, la, lb, 0, ldw, low_rhs, low_inv, 0, 1, SCALES[2], *steps[1], group=6)
-    sweep(2, 12, lb, la, 0, ldw, low_rhs, low_inv, 0, 1, SCALES[2], *steps[2], group=5)
-    sweep(3, 11, la, lb, 0, ldw, low_rhs, low_inv, 0, 1, SCALES[2], *steps[3], group=4)
+    first_step(0, 14, low_rhs, low_inv, la, ldw, 1, steps[0][1])
+    sweep(1, 13, la, lb, 0, ldw, low_rhs, low_inv, 0, 1, SCALES[2], *steps[1])
+    sweep(2, 12, lb, la, 0, ldw, low_rhs, low_inv, 0, 1, SCALES[2], *steps[2])
+    sweep(3, 11, la, lb, 0, ldw, low_rhs, low_inv, 0, 1, SCALES[2], *steps[3])
 
     for t in range(3):
         store(start, t, unpack(far, 0, 256 + 64 * t))
@@ -400,14 +384,14 @@
 
     steps = chebyshev(DEGREE)
     shift = 2 * core - 1
-    sweep(1, 11, mid_a, mid_b, 0, mid_dw, mid_rhs, mid_inv, shift, 2, SCALES[1], *steps[0], loader=load_ends, group=2)
-    sweep(2, 10, mid_b, mid_a, 0, mid_dw, mid_rhs, mid_inv, shift, 2, SCALES[1], *steps[1], loader=load_ends, group=2)
-    sweep(3, 9, mid_a, mid_b, 0, mid_dw, mid_rhs, mid_inv, shift, 2, SCALES[1], *steps[2], loader=load_ends, group=2)
+    sweep(1, 11, mid_a, mid_b, 0, mid_dw, mid_rhs, mid_inv, shift, 2, SCALES[1], *steps[0], loader=load_ends)
+    sweep(2, 10, mid_b, mid_a, 0, mid_dw, mid_rhs, mid_inv, shift, 2, SCALES[1], *steps[1], loader=load_ends)
+    sweep(3, 9, mid_a, mid_b, 0, mid_dw, mid_rhs, mid_inv, shift, 2, SCALES[1], *steps[2], loader=load_ends)
 
     near = lax.broadcasted_iota(jnp.int32, (8, LANES), 0) < 6
     ahead = 2 - 2 * core
 
-    def correct(t, carry):
+    for t in range(3, 9):
         k = load(ends, t + 2 * core, 2)
         for d in range(2):
             for c in range(2):
@@ -420,14 +404,12 @@
                             wa[v, dd, :, lanes(cc)] = (
                                 wa[v, dd, :, lanes(cc)] + cond[v + ahead, dd, :, lanes(cc)] * value
                             )
-        return carry
-
-    lax.fori_loop(3, 9, correct, 0)
+
     sweep(1, 11, wa, wb, 0, dw, rhs, inv, ahead, 4, SCALES[0], *steps[0])
     sweep(2, 10, wb, wa, 0, dw, rhs, inv, ahead, 4, SCALES[0], *steps[1])
     sweep(3, 9, wa, wb, 0, dw, rhs, inv, ahead, 4, SCALES[0], *steps[2])
 
-    def finish(t, carry):
+    for t in range(4):
         left = residual_plane(wb, t + 4, rhs, inv, t + 4 + ahead, 4, SCALES[0])
         for d in range(4):
             for c in range(4):
@@ -437,17 +419,14 @@
                     value = value + before[t, d, :, lanes(c)]
                 adjoint[t, d, :, lanes(c)] = value
                 remain[t, d, :, lanes(c)] = left[d][c][0:4]
-        return carry
-
-    lax.fori_loop(0, 4, finish, 0)
 
 
 def f32(*shape):
     return jax.ShapeDtypeStruct(shape, jnp.float32)
 
 
-def call(body, outs, scratch, *args, scalars=True, name=None):
-    specs = [pl.BlockSpec(memory_space=pltpu.VMEM) if scalars else pl.BlockSpec()] * len(args)
+def call(body, outs, scratch, *args, scalars=True, space=pltpu.VMEM, sems=0, name=None):
+    specs = [pl.BlockSpec(memory_space=space)] * len(args)
     if scalars:
         specs[0] = pl.BlockSpec(memory_space=pltpu.SMEM)
     return pl.pallas_call(
@@ -455,7 +434,8 @@
         out_shape=outs,
         in_specs=specs,
         out_specs=[pl.BlockSpec(memory_space=pltpu.VMEM)] * len(outs),
-        scratch_shapes=[pltpu.VMEM(s, jnp.float32) for s in scratch],
+        scratch_shapes=[pltpu.VMEM(s, jnp.float32) for s in scratch]
+        + ([pltpu.SemaphoreType.DMA((sems,))] if sems else []),
         compiler_params=pltpu.CompilerParams(vmem_limit_bytes=VMEM_LIMIT),
         name=name,
     )(*args)
@@ -506,7 +486,15 @@
     prm = jnp.stack([core, y % 2, y, z]).astype(jnp.int32)
     place = (core + y) % 2
     (remain,) = call(
-        prepare_kernel, [f32(4, 8, 4, 512)], [(4, 128, 128)], source, conduct, scalars=False, name="prepare"
+        prepare_kernel,
+        [f32(4, 8, 4, 512)],
+        [(2, 4, 16, 512), (4, 128, 128)],
+        source,
+        conduct,
+        scalars=False,
+        space=pl.ANY,
+        sems=2,
+        name="prepare",
     )
     adjoint = None
     kept = None

time: 185 us -> 176 us (0.951)
  Pallas kernels: 26.4 us -> 16.8 us
    pallas_call x12, Pallas kernels: 26.4 us -> 16.8 us  [call(): pl.pallas_call(body, out_shape=outs, in_specs=specs, out_specs=[pl.BlockS...]
where the time goes in v5:
time: 176 us; the launch traced here: 175 us
  blocking collectives  109 us (62%)
  starting transfers between devices  31.6 us (18%)
  Pallas kernels  16.8 us (10%)
  waiting for transfers between devices  12.8 us (7%)
  local copies, waits for them, and re-layouts  3.76 us (2%)
    all_gather x14, blocking collectives, gather(): lax.all_gather(value, 'gz', axis_index_groups=pairs(first, step, size))  85.6 us
    ppermute x7, starting transfers between devices, swap(): return lax.ppermute(value, 'gz', ways)  28.2 us
    pallas_call x12, Pallas kernels, call(): pl.pallas_call(body, out_shape=outs, in_specs=specs, out_specs=[pl.BlockS...  16.8 us
    all_gather x2, blocking collectives, row_pairs(): return lax.all_gather(value, ('gz', 'gy'), axis_index_groups=members)  12.8 us
    all_to_all x1, blocking collectives, local(): rows = lax.all_to_all(low, 'gy', split_axis=0, concat_axis=0, tiled=True)  10.4 us
    all_to_all x1, waiting for transfers between devices, local(): rows = lax.all_to_all(low, 'gy', split_axis=0, concat_axis=0, tiled=True)  9.24 us
    ppermute x7, waiting for transfers between devices, swap(): return lax.ppermute(value, 'gz', ways)  3.54 us
  transfers between devices with their start and end apart: 8, of which 3 were waited for; matrix products, arithmetic and copies ran while one was open for 0% of the time, Pallas kernels for 0%

profile of v5, /device:TPU:1, one launch (start us, length us, event | category | flops | bytes accessed | tf_op | source)
XLA Modules:
  0.0 175.0 jit_solution(3496253521489198511)
XLA Ops:
  3.7 12.3 %all-gather = f32[8,8,4,512]{3,1,2,0:T(8,128)S(1)} all-gather(f32[4,8,4,512]{3,1,2,0:T(8,128)S(1)} %copy.4), channel_id=2, replica_groups={{0,8},{16,24},{32,40},{48,56},{64,72},{80,88},{96,104},{112,120},{128,1..., dimensions={0}, use_global_device_ids=true | all-gather | bytes 786432 | tf_op jit(solution)/shard_map/all_gather | solution.py:450
  16.4 7.1 %all-gather.1 = f32[16,8,2,512]{3,1,2,0:T(8,128)S(1)} all-gather(f32[8,8,2,512]{3,1,2,0:T(8,128)S(1)} %slice_select_fusion.1), channel_id=3, replica_groups={{0,1},{2,3},{4,5},{6,7},{9,10},{11,12},{13,14},{15,8},{16,17},{18,19},{..., dimensions={0}, use_global_device_ids=true | all-gather | bytes 786432 | tf_op jit(solution)/shard_map/all_gather | solution.py:475
  23.6 2.2 %all-gather.12 = f32[16,8,2,512]{3,1,2,0:T(8,128)S(1)} all-gather(f32[8,8,2,512]{3,1,2,0:T(8,128)S(1)} %slice_select_fusion), channel_id=14, replica_groups={{0,8},{16,24},{32,40},{48,56},{64,72},{80,88},{96,104},{112,120},{128,1..., dimensions={0}, use_global_device_ids=true | all-gather | bytes 786432 | tf_op jit(solution)/shard_map/all_gather | solution.py:450
  29.0 11.5 %all-gather.2 = f32[12,4,8,512]{3,2,1,0:T(8,128)S(1)} all-gather(f32[6,4,8,512]{3,2,1,0:T(8,128)S(1)} %get-tuple-element.36), channel_id=4, replica_groups={{8,16},{24,32},{40,48},{56,64},{72,80},{88,96},{104,112},{120,128},{136..., dimensions={0}, use_global_device_ids=true | all-gather | bytes 1179648 | tf_op jit(solution)/shard_map/all_gather | solution.py:450
  40.5 2.4 %fine_down_first.1 = (f32[14,4,8,512]{3,2,1,0:T(8,128)S(1)}, f32[10,4,8,512]{3,2,1,0:T(8,128)S(1)}, f32[8,2,2,2,4,256]{5,4,3,2,1,0:T(4,128)}, f32[256,128]{1,0:T...) custom-call(s32[4]{0:T(128)S(1)} %pad_add_fusion.prm, ...), custom_call_target="tpu_custom_call" | custom-call | tf_op jit(solution)/shard_map/fine_down_first/pallas_call | solution.py:432
  43.8 3.4 %all-to-all-start = ((f32[8,2,2,2,4,256]{5,4,3,2,1,0:T(4,128)}), f32[8,2,2,2,4,256]{5,4,3,2,1,0:T(4,128)S(1)}, u32[]{:S(2)}, u32[]{:S(2)}) async-start(f32[8,2,2,2,4,256]{5,4,3,2,1,0:T(4,128)} %get-tuple-element.39), calls=%async_computation | async-start | bytes 524288 | tf_op jit(solution)/shard_map/all_to_all | solution.py:532
  47.3 9.2 %all-to-all-done.rows = f32[8,2,2,2,4,256]{5,4,3,2,1,0:T(4,128)S(1)} async-done(((f32[8,2,2,2,4,256]{5,4,3,2,1,0:T(4,128)}), f32[8,2,2,2,4,256]{5,4,3,2,1,0:T(4,128)S(1)}, u32[]{:S(2)}, u32[]{:S(2)}) %all-to-all-start) | async-done | bytes 262176 | tf_op jit(solution)/shard_map/all_to_all | solution.py:532
  57.1 12.3 %all-gather.3 = f32[10,2,2,2,4,256]{5,4,3,2,1,0:T(4,128)S(1)} all-gather(f32[5,2,2,2,4,256]{5,4,3,2,1,0:T(4,128)S(1)} %pick.2), channel_id=5, replica_groups={{0,8},{16,24},{32,40},{48,56},{64,72},{80,88},{96,104},{112,120},{128,1..., dimensions={0}, use_global_device_ids=true | all-gather | bytes 491520 | tf_op jit(solution)/shard_map/all_gather | solution.py:450
  69.3 7.5 %all-gather.4 = f32[4,5,2,2,2,4,256]{6,5,4,3,2,1,0:T(4,128)S(1)} all-gather(f32[2,5,2,2,2,4,256]{6,5,4,3,2,1,0:T(4,128)S(1)} %bitcast.23), channel_id=6, replica_groups={{8,16},{24,32},{40,48},{56,64},{72,80},{88,96},{104,112},{120,128},{136..., dimensions={0}, use_global_device_ids=true | all-gather | bytes 983040 | tf_op jit(solution)/shard_map/all_gather | solution.py:450
  76.8 5.3 %all_gather.99.far = f32[2,2,5,2,2,2,4,256]{7,6,5,4,3,2,1,0:T(4,128)S(1)} all-gather(f32[1,2,5,2,2,2,4,256]{7,6,5,4,3,2,1,0:T(4,128)S(1)} %constant_dynamic-slice_fusion.1), channel_id=1, replica_groups={{0,8},{16,24},{32,40},{48,56},{64,72},{80,88},{96,104},{112,120},{128,1..., dimensions={0}, use_global_device_ids=true | all-gather | bytes 983040 | tf_op jit(solution)/shard_map/all_gather | solution.py:450
  87.4 9.3 %collective-permute-start.2 = (f32[96,128]{1,0:T(8,128)S(1)}, f32[96,128]{1,0:T(8,128)S(1)}, u32[]{:S(2)}, u32[]{:S(2)}) collective-permute-start(f32[96,128]{1,0:T(8,128)S(1)} %bitcast.33), channel_id=1, source_target_pairs={{8,32},{32,8},{24,48},{48,24},{40,64},{64,40},{56,80},{80,56},{72,... | collective-permute-start | bytes 147464 | tf_op jit(solution)/shard_map/ppermute | solution.py:466
  96.7 2.0 %collective-permute-done.2 = f32[96,128]{1,0:T(8,128)S(1)} collective-permute-done((f32[96,128]{1,0:T(8,128)S(1)}, f32[96,128]{1,0:T(8,128)S(1)}, u32[]{:S(2)}, u32[]{:S(2)}) %collective-permute-start.2) | collective-permute-done | bytes 49184 | tf_op jit(solution)/shard_map/ppermute | solution.py:466
  98.8 3.4 %all-gather.5 = f32[1600,128]{1,0:T(8,128)S(1)} all-gather(f32[800,128]{1,0:T(8,128)S(1)} %pad_maximum_fusion), channel_id=7, replica_groups={{0,8},{16,24},{32,40},{48,56},{64,72},{80,88},{96,104},{112,120},{128,1..., dimensions={0}, use_global_device_ids=true | all-gather | bytes 1228800 | tf_op jit(solution)/shard_map/all_gather | solution.py:450
  102.2 2.4 %up_first.1 = (f32[4,4,4,512]{3,2,1,0:T(4,128)S(1)}, f32[4,4,4,512]{3,2,1,0:T(4,128)S(1)}, f32[14,2,16,256]{3,2,1,0:T(8,128)S(1)}, f32[14,1,24,128]{3,2,1,0:T(8,128)S(1)}, f32[14,1,24,128]{3,2,1,0:T(8,128)S(1)}) custom-call(s32[4]{0:T(128)S(1)} %pad_add_fusion.prm, f32[2,2,24,128]{3,2,1,0:T(8,128)S(1)} %get-tuple-element.40.low, ...), custom_call_target="tpu_custom_call" | custom-call | tf_op jit(solution)/shard_map/up_first/pallas_call | solution.py:432
  104.6 2.0 %all-gather.6 = f32[8,4,4,512]{3,2,1,0:T(4,128)S(1)} all-gather(f32[4,4,4,512]{3,2,1,0:T(4,128)S(1)} %get-tuple-element.51), channel_id=8, replica_groups={{0,8},{16,24},{32,40},{48,56},{64,72},{80,88},{96,104},{112,120},{128,1..., dimensions={0}, use_global_device_ids=true | all-gather | bytes 393216 | tf_op jit(solution)/shard_map/all_gather | solution.py:450
  106.7 5.7 %all-gather.7 = f32[16,4,2,512]{3,1,2,0:T(4,128)S(1)} all-gather(f32[8,4,2,512]{3,1,2,0:T(4,128)S(1)} %copy.7), channel_id=9, replica_groups={{0,1},{2,3},{4,5},{6,7},{9,10},{11,12},{13,14},{15,8},{16,17},{18,19},{..., dimensions={0}, use_global_device_ids=true | all-gather | bytes 393216 | tf_op jit(solution)/shard_map/all_gather | solution.py:475
  115.4 9.0 %all-gather.8 = f32[12,4,8,512]{3,2,1,0:T(8,128)S(1)} all-gather(f32[6,4,8,512]{3,2,1,0:T(8,128)S(1)} %get-tuple-element.53), channel_id=10, replica_groups={{8,16},{24,32},{40,48},{56,64},{72,80},{88,96},{104,112},{120,128},{136..., dimensions={0}, use_global_device_ids=true | all-gather | bytes 1179648 | tf_op jit(solution)/shard_map/all_gather | solution.py:450
  126.0 10.4 %all_to_all.10.rows = f32[8,1,2,2,4,256]{5,4,3,2,1,0:T(4,128)S(1)} all-to-all(f32[8,1,2,2,4,256]{5,4,3,2,1,0:T(4,128)S(1)} %get-tuple-element.54), channel_id=1, replica_groups=mesh['gz'=96,'gy'=8] {'gy'}, dimensions={0} | all-to-all | bytes 262144 | tf_op jit(solution)/shard_map/all_to_all | solution.py:532
  137.0 5.1 %all-gather.9 = f32[10,1,2,2,4,256]{5,4,3,2,1,0:T(4,128)S(1)} all-gather(f32[5,1,2,2,4,256]{5,4,3,2,1,0:T(4,128)S(1)} %pick.3), channel_id=11, replica_groups={{0,8},{16,24},{32,40},{48,56},{64,72},{80,88},{96,104},{112,120},{128,1..., dimensions={0}, use_global_device_ids=true | all-gather | bytes 245760 | tf_op jit(solution)/shard_map/all_gather | solution.py:450
  142.1 5.7 %all-gather.10 = f32[4,5,1,2,2,4,256]{6,5,4,3,2,1,0:T(4,128)S(1)} all-gather(f32[2,5,1,2,2,4,256]{6,5,4,3,2,1,0:T(4,128)S(1)} %bitcast.29), channel_id=12, replica_groups={{8,16},{24,32},{40,48},{56,64},{72,80},{88,96},{104,112},{120,128},{136..., dimensions={0}, use_global_device_ids=true | all-gather | bytes 491520 | tf_op jit(solution)/shard_map/all_gather | solution.py:450
  147.8 5.1 %all_gather.113.far = f32[2,2,5,1,2,2,4,256]{7,6,5,4,3,2,1,0:T(4,128)S(1)} all-gather(f32[1,2,5,1,2,2,4,256]{7,6,5,4,3,2,1,0:T(4,128)S(1)} %constant_dynamic-slice_fusion), channel_id=1, replica_groups={{0,8},{16,24},{32,40},{48,56},{64,72},{80,88},{96,104},{112,120},{128,1..., dimensions={0}, use_global_device_ids=true | all-gather | bytes 491520 | tf_op jit(solution)/shard_map/all_gather | solution.py:450
  158.0 9.3 %collective-permute-start.5 = (f32[48,128]{1,0:T(8,128)S(1)}, f32[48,128]{1,0:T(8,128)S(1)}, u32[]{:S(2)}, u32[]{:S(2)}) collective-permute-start(f32[48,128]{1,0:T(8,128)S(1)} %bitcast.35), channel_id=1, source_target_pairs={{8,32},{32,8},{24,48},{48,24},{40,64},{64,40},{56,80},{80,56},{72,... | collective-permute-start | bytes 73736 | tf_op jit(solution)/shard_map/ppermute | solution.py:466
  168.8 2.2 %all-gather.11 = f32[1184,128]{1,0:T(8,128)S(1)} all-gather(f32[592,128]{1,0:T(8,128)S(1)} %pad_maximum_fusion.1), channel_id=13, replica_groups={{0,8},{16,24},{32,40},{48,56},{64,72},{80,88},{96,104},{112,120},{128,1..., dimensions={0}, use_global_device_ids=true | all-gather | bytes 909312 | tf_op jit(solution)/shard_map/all_gather | solution.py:450
  171.1 2.5 %up.1 = (f32[4,4,4,512]{3,2,1,0:T(4,128)S(1)}, f32[4,4,4,512]{3,2,1,0:T(4,128)S(1)}) custom-call(s32[4]{0:T(128)S(1)} %pad_add_fusion.prm, f32[1,2,24,128]{3,2,1,0:T(8,128)S(1)} %get-tuple-element.55.low, f32[2,592,128]{2,1,0:T(8,128)S(1)} %bitcast.25, f32[8,2,24,256]{3,2,1,0:T(8,128)S(1)} %get-tuple-element.58.middle, ...), custom_call_target="tpu_custom_call" | custom-call | tf_op jit(solution)/shard_map/up/pallas_call | solution.py:432
  (45 shorter events, 26.7 us)
Async XLA Ops:
  0.7 0.9 copy-start.2
  1.6 0.9 copy-start.3
  27.1 13.4 %collective-permute-start = (f32[6,4,8,512]{3,2,1,0:T(8,128)S(1)}, f32[6,4,8,512]{3,2,1,0:T(8,128)S(1)}, u32[]{:S(2)}, u32[]{:S(2)}) collective-permute-start(f32[6,4,8,512]{3,2,1,0:T(8,128)S(1)} %get-tuple-element.38), channel_id=1, source_target_pairs={{8,16},{16,8},{24,32},{32,24},{40,48},{48,40},{56,64},{64,56},{72,... | collective-permute-start | bytes 1179656 | tf_op jit(solution)/shard_map/ppermute | solution.py:466
  43.0 0.9 copy-start
  43.8 12.7 %all-to-all-start = ((f32[8,2,2,2,4,256]{5,4,3,2,1,0:T(4,128)}), f32[8,2,2,2,4,256]{5,4,3,2,1,0:T(4,128)S(1)}, u32[]{:S(2)}, u32[]{:S(2)}) async-start(f32[8,2,2,2,4,256]{5,4,3,2,1,0:T(4,128)} %get-tuple-element.39), calls=%async_computation | async-start | bytes 524288 | tf_op jit(solution)/shard_map/all_to_all | solution.py:532
  83.5 15.2 %collective-permute-start.1 = (f32[352,128]{1,0:T(8,128)S(1)}, f32[352,128]{1,0:T(8,128)S(1)}, u32[]{:S(2)}, u32[]{:S(2)}) collective-permute-start(f32[352,128]{1,0:T(8,128)S(1)} %get-tuple-element.42), channel_id=1, source_target_pairs={{8,16},{16,8},{24,32},{32,24},{40,48},{48,40},{56,64},{64,56},{72,... | collective-permute-start | bytes 540680 | tf_op jit(solution)/shard_map/ppermute | solution.py:466
  85.4 11.2 %collective-permute-start.3 = (f32[96,128]{1,0:T(8,128)S(1)}, f32[96,128]{1,0:T(8,128)S(1)}, u32[]{:S(2)}, u32[]{:S(2)}) collective-permute-start(f32[96,128]{1,0:T(8,128)S(1)} %bitcast.32), channel_id=1, source_target_pairs={{8,48},{48,8},{24,64},{64,24},{40,80},{80,40},{56,96},{96,56},{72,... | collective-permute-start | bytes 147464 | tf_op jit(solution)/shard_map/ppermute | solution.py:466
  87.4 11.4 %collective-permute-start.2 = (f32[96,128]{1,0:T(8,128)S(1)}, f32[96,128]{1,0:T(8,128)S(1)}, u32[]{:S(2)}, u32[]{:S(2)}) collective-permute-start(f32[96,128]{1,0:T(8,128)S(1)} %bitcast.33), channel_id=1, source_target_pairs={{8,32},{32,8},{24,48},{48,24},{40,64},{64,40},{56,80},{80,56},{72,... | collective-permute-start | bytes 147464 | tf_op jit(solution)/shard_map/ppermute | solution.py:466
  98.8 3.4 %copy-start.1 = (f32[10,4,8,512]{3,2,1,0:T(8,128)S(1)}, f32[10,4,8,512]{3,2,1,0:T(8,128)}, u32[]{:S(2)}) copy-start(f32[10,4,8,512]{3,2,1,0:T(8,128)} %copy-done) | copy-start | bytes 1966084
  154.2 14.6 %collective-permute-start.4 = (f32[240,128]{1,0:T(8,128)S(1)}, f32[240,128]{1,0:T(8,128)S(1)}, u32[]{:S(2)}, u32[]{:S(2)}) collective-permute-start(f32[240,128]{1,0:T(8,128)S(1)} %get-tuple-element.57), channel_id=1, source_target_pairs={{8,16},{16,8},{24,32},{32,24},{40,48},{48,40},{56,64},{64,56},{72,... | collective-permute-start | bytes 368648 | tf_op jit(solution)/shard_map/ppermute | solution.py:466
  156.1 11.2 %collective-permute-start.6 = (f32[48,128]{1,0:T(8,128)S(1)}, f32[48,128]{1,0:T(8,128)S(1)}, u32[]{:S(2)}, u32[]{:S(2)}) collective-permute-start(f32[48,128]{1,0:T(8,128)S(1)} %bitcast.34), channel_id=1, source_target_pairs={{8,48},{48,8},{24,64},{64,24},{40,80},{80,40},{56,96},{96,56},{72,... | collective-permute-start | bytes 73736 | tf_op jit(solution)/shard_map/ppermute | solution.py:466
  158.0 10.8 %collective-permute-start.5 = (f32[48,128]{1,0:T(8,128)S(1)}, f32[48,128]{1,0:T(8,128)S(1)}, u32[]{:S(2)}, u32[]{:S(2)}) collective-permute-start(f32[48,128]{1,0:T(8,128)S(1)} %bitcast.35), channel_id=1, source_target_pairs={{8,32},{32,8},{24,48},{48,24},{40,64},{64,40},{56,80},{80,56},{72,... | collective-permute-start | bytes 73736 | tf_op jit(solution)/shard_map/ppermute | solution.py:466

commit v6 on v5

--- a/solution.py
+++ b/solution.py
@@ -425,7 +425,7 @@
     return jax.ShapeDtypeStruct(shape, jnp.float32)
 
 
-def call(body, outs, scratch, *args, scalars=True, space=pltpu.VMEM, sems=0, name=None):
+def call(body, outs, scratch, *args, scalars=True, space=pltpu.VMEM, sems=0, limit=VMEM_LIMIT, name=None):
     specs = [pl.BlockSpec(memory_space=space)] * len(args)
     if scalars:
         specs[0] = pl.BlockSpec(memory_space=pltpu.SMEM)
@@ -436,7 +436,7 @@
         out_specs=[pl.BlockSpec(memory_space=pltpu.VMEM)] * len(outs),
         scratch_shapes=[pltpu.VMEM(s, jnp.float32) for s in scratch]
         + ([pltpu.SemaphoreType.DMA((sems,))] if sems else []),
-        compiler_params=pltpu.CompilerParams(vmem_limit_bytes=VMEM_LIMIT),
+        compiler_params=pltpu.CompilerParams(vmem_limit_bytes=limit),
         name=name,
     )(*args)
 
@@ -480,8 +480,8 @@
 
 
 def local(source, conduct):
-    z = lax.axis_index("gz")
-    y = lax.axis_index("gy")
+    z = lax.axis_index("gz").astype(jnp.uint32)
+    y = lax.axis_index("gy").astype(jnp.uint32)
     core = z % 2
     prm = jnp.stack([core, y % 2, y, z]).astype(jnp.int32)
     place = (core + y) % 2
@@ -494,6 +494,7 @@
         scalars=False,
         space=pl.ANY,
         sems=2,
+        limit=60 * 1024 * 1024,
         name="prepare",
     )
     adjoint = None

time: 176 us -> 174 us (0.989)
  blocking collectives: 109 us -> 121 us
  waiting for transfers between devices: 12.8 us -> 3.54 us
  starting transfers between devices: 31.6 us -> 28.2 us
    all_to_all x1 -> x2, blocking collectives: 10.4 us -> 22.1 us  [local(): rows = lax.all_to_all(low, 'gy', split_axis=0, concat_axis=0, tiled=True)]
    all_to_all x1 -> x0, waiting for transfers between devices: 9.24 us -> none  [local(): rows = lax.all_to_all(low, 'gy', split_axis=0, concat_axis=0, tiled=True)]
    all_to_all x1 -> x0, starting transfers between devices: 3.41 us -> none  [local(): rows = lax.all_to_all(low, 'gy', split_axis=0, concat_axis=0, tiled=True)]
    unnamed x8 -> x0, local copies, waits for them, and re-layouts: 2.66 us -> none
  transfers between devices with their start and end apart: 8 -> 7, of which waited for: 3 -> 2; matrix products, arithmetic and copies ran while one was open for 0% -> 0% of each run, Pallas kernels for 0% -> 0%
where the time goes in v6:
time: 174 us
  blocking collectives  121 us (70%)
  starting transfers between devices  28.2 us (16%)
  Pallas kernels  17.6 us (10%)
  waiting for transfers between devices  3.54 us (2%)
  local copies, waits for them, and re-layouts  2.04 us (1%)
    all_gather x14, blocking collectives, gather(): lax.all_gather(value, 'gz', axis_index_groups=pairs(first, step, size))  86.1 us
    ppermute x7, starting transfers between devices, swap(): return lax.ppermute(value, 'gz', ways)  28.2 us
    all_to_all x2, blocking collectives, local(): rows = lax.all_to_all(low, 'gy', split_axis=0, concat_axis=0, tiled=True)  22.1 us
    pallas_call x12, Pallas kernels, call(): pl.pallas_call(body, out_shape=outs, in_specs=specs, out_specs=[pl.BlockS...  17.6 us
    all_gather x2, blocking collectives, row_pairs(): return lax.all_gather(value, ('gz', 'gy'), axis_index_groups=members)  12.8 us
    ppermute x7, waiting for transfers between devices, swap(): return lax.ppermute(value, 'gz', ways)  3.54 us
  transfers between devices with their start and end apart: 7, of which 2 were waited for; matrix products, arithmetic and copies ran while one was open for 0% of the time, Pallas kernels for 0%

profile of v6, /device:TPU:1, one launch (start us, length us, event | category | flops | bytes accessed | tf_op | source)
XLA Modules:
  0.0 173.8 jit_solution(4195523694710930481)
XLA Ops:
  0.6 2.5 %prepare.1 = f32[4,8,4,512]{3,2,1,0:T(4,128)} custom-call(f32[4,16,512]{2,1,0:T(8,128)} %source.1, f32[4,16,512]{2,1,0:T(8,128)} %cond.1), custom_call_target="tpu_custom_call" | custom-call | tf_op jit(solution)/shard_map/prepare/pallas_call | solution.py:432
  4.2 12.3 %all-gather = f32[8,8,4,512]{3,1,2,0:T(8,128)S(1)} all-gather(f32[4,8,4,512]{3,1,2,0:T(8,128)S(1)} %copy.4), channel_id=2, replica_groups={{0,8},{16,24},{32,40},{48,56},{64,72},{80,88},{96,104},{112,120},{128,1..., dimensions={0}, use_global_device_ids=true | all-gather | bytes 786432 | tf_op jit(solution)/shard_map/all_gather | solution.py:450
  16.9 7.1 %all-gather.1 = f32[16,8,2,512]{3,1,2,0:T(8,128)S(1)} all-gather(f32[8,8,2,512]{3,1,2,0:T(8,128)S(1)} %slice_select_fusion.1), channel_id=3, replica_groups={{0,1},{2,3},{4,5},{6,7},{9,10},{11,12},{13,14},{15,8},{16,17},{18,19},{..., dimensions={0}, use_global_device_ids=true | all-gather | bytes 786432 | tf_op jit(solution)/shard_map/all_gather | solution.py:475
  24.1 2.2 %all-gather.12 = f32[16,8,2,512]{3,1,2,0:T(8,128)S(1)} all-gather(f32[8,8,2,512]{3,1,2,0:T(8,128)S(1)} %slice_select_fusion), channel_id=14, replica_groups={{0,8},{16,24},{32,40},{48,56},{64,72},{80,88},{96,104},{112,120},{128,1..., dimensions={0}, use_global_device_ids=true | all-gather | bytes 786432 | tf_op jit(solution)/shard_map/all_gather | solution.py:450
  29.5 11.5 %all-gather.2 = f32[12,4,8,512]{3,2,1,0:T(8,128)S(1)} all-gather(f32[6,4,8,512]{3,2,1,0:T(8,128)S(1)} %get-tuple-element.36), channel_id=4, replica_groups={{8,16},{24,32},{40,48},{56,64},{72,80},{88,96},{104,112},{120,128},{136..., dimensions={0}, use_global_device_ids=true | all-gather | bytes 1179648 | tf_op jit(solution)/shard_map/all_gather | solution.py:450
  42.8 11.7 %all_to_all.10.rows = f32[8,2,2,2,4,256]{5,4,3,2,1,0:T(4,128)S(1)} all-to-all(f32[8,2,2,2,4,256]{5,4,3,2,1,0:T(4,128)S(1)} %get-tuple-element.39), channel_id=1, replica_groups=mesh['gz'=96,'gy'=8] {'gy'}, dimensions={0} | all-to-all | bytes 524288 | tf_op jit(solution)/shard_map/all_to_all | solution.py:533
  55.1 13.0 %all-gather.3 = f32[10,2,2,2,4,256]{5,4,3,2,1,0:T(4,128)S(1)} all-gather(f32[5,2,2,2,4,256]{5,4,3,2,1,0:T(4,128)S(1)} %pick.2), channel_id=5, replica_groups={{0,8},{16,24},{32,40},{48,56},{64,72},{80,88},{96,104},{112,120},{128,1..., dimensions={0}, use_global_device_ids=true | all-gather | bytes 491520 | tf_op jit(solution)/shard_map/all_gather | solution.py:450
  68.1 7.5 %all-gather.4 = f32[4,5,2,2,2,4,256]{6,5,4,3,2,1,0:T(4,128)S(1)} all-gather(f32[2,5,2,2,2,4,256]{6,5,4,3,2,1,0:T(4,128)S(1)} %bitcast.23), channel_id=6, replica_groups={{8,16},{24,32},{40,48},{56,64},{72,80},{88,96},{104,112},{120,128},{136..., dimensions={0}, use_global_device_ids=true | all-gather | bytes 983040 | tf_op jit(solution)/shard_map/all_gather | solution.py:450
  75.6 5.3 %all_gather.99.far = f32[2,2,5,2,2,2,4,256]{7,6,5,4,3,2,1,0:T(4,128)S(1)} all-gather(f32[1,2,5,2,2,2,4,256]{7,6,5,4,3,2,1,0:T(4,128)S(1)} %constant_dynamic-slice_fusion.1), channel_id=1, replica_groups={{0,8},{16,24},{32,40},{48,56},{64,72},{80,88},{96,104},{112,120},{128,1..., dimensions={0}, use_global_device_ids=true | all-gather | bytes 983040 | tf_op jit(solution)/shard_map/all_gather | solution.py:450
  86.1 9.3 %collective-permute-start.2 = (f32[96,128]{1,0:T(8,128)S(1)}, f32[96,128]{1,0:T(8,128)S(1)}, u32[]{:S(2)}, u32[]{:S(2)}) collective-permute-start(f32[96,128]{1,0:T(8,128)S(1)} %bitcast.33), channel_id=1, source_target_pairs={{8,32},{32,8},{24,48},{48,24},{40,64},{64,40},{56,80},{80,56},{72,... | collective-permute-start | bytes 147464 | tf_op jit(solution)/shard_map/ppermute | solution.py:466
  95.5 2.0 %collective-permute-done.2 = f32[96,128]{1,0:T(8,128)S(1)} collective-permute-done((f32[96,128]{1,0:T(8,128)S(1)}, f32[96,128]{1,0:T(8,128)S(1)}, u32[]{:S(2)}, u32[]{:S(2)}) %collective-permute-start.2) | collective-permute-done | bytes 49184 | tf_op jit(solution)/shard_map/ppermute | solution.py:466
  97.5 3.3 %all-gather.5 = f32[1600,128]{1,0:T(8,128)S(1)} all-gather(f32[800,128]{1,0:T(8,128)S(1)} %pad_maximum_fusion), channel_id=7, replica_groups={{0,8},{16,24},{32,40},{48,56},{64,72},{80,88},{96,104},{112,120},{128,1..., dimensions={0}, use_global_device_ids=true | all-gather | bytes 1228800 | tf_op jit(solution)/shard_map/all_gather | solution.py:450
  100.8 2.5 %up_first.1 = (f32[4,4,4,512]{3,2,1,0:T(4,128)S(1)}, f32[4,4,4,512]{3,2,1,0:T(4,128)S(1)}, f32[14,2,16,256]{3,2,1,0:T(8,128)S(1)}, f32[14,1,24,128]{3,2,1,0:T(8,128)S(1)}, f32[14,1,24,128]{3,2,1,0:T(8,128)S(1)}) custom-call(s32[4]{0:T(128)S(1)} %add_convert_fusion.prm, f32[2,2,24,128]{3,2,1,0:T(8,128)S(1)} %get-tuple-element.40.low, ...), custom_call_target="tpu_custom_call" | custom-call | tf_op jit(solution)/shard_map/up_first/pallas_call | solution.py:432
  103.3 2.0 %all-gather.6 = f32[8,4,4,512]{3,2,1,0:T(4,128)S(1)} all-gather(f32[4,4,4,512]{3,2,1,0:T(4,128)S(1)} %get-tuple-element.51), channel_id=8, replica_groups={{0,8},{16,24},{32,40},{48,56},{64,72},{80,88},{96,104},{112,120},{128,1..., dimensions={0}, use_global_device_ids=true | all-gather | bytes 393216 | tf_op jit(solution)/shard_map/all_gather | solution.py:450
  105.4 5.7 %all-gather.7 = f32[16,4,2,512]{3,1,2,0:T(4,128)S(1)} all-gather(f32[8,4,2,512]{3,1,2,0:T(4,128)S(1)} %copy.7), channel_id=9, replica_groups={{0,1},{2,3},{4,5},{6,7},{9,10},{11,12},{13,14},{15,8},{16,17},{18,19},{..., dimensions={0}, use_global_device_ids=true | all-gather | bytes 393216 | tf_op jit(solution)/shard_map/all_gather | solution.py:475
  111.3 2.0 %all-gather.13 = f32[16,4,2,512]{3,1,2,0:T(4,128)S(1)} all-gather(f32[8,4,2,512]{3,1,2,0:T(4,128)S(1)} %copy.10), channel_id=15, replica_groups={{0,8},{16,24},{32,40},{48,56},{64,72},{80,88},{96,104},{112,120},{128,1..., dimensions={0}, use_global_device_ids=true | all-gather | bytes 393216 | tf_op jit(solution)/shard_map/all_gather | solution.py:450
  114.2 9.0 %all-gather.8 = f32[12,4,8,512]{3,2,1,0:T(8,128)S(1)} all-gather(f32[6,4,8,512]{3,2,1,0:T(8,128)S(1)} %get-tuple-element.53), channel_id=10, replica_groups={{8,16},{24,32},{40,48},{56,64},{72,80},{88,96},{104,112},{120,128},{136..., dimensions={0}, use_global_device_ids=true | all-gather | bytes 1179648 | tf_op jit(solution)/shard_map/all_gather | solution.py:450
  124.7 10.4 %all_to_all.11.rows = f32[8,1,2,2,4,256]{5,4,3,2,1,0:T(4,128)S(1)} all-to-all(f32[8,1,2,2,4,256]{5,4,3,2,1,0:T(4,128)S(1)} %get-tuple-element.54), channel_id=1, replica_groups=mesh['gz'=96,'gy'=8] {'gy'}, dimensions={0} | all-to-all | bytes 262144 | tf_op jit(solution)/shard_map/all_to_all | solution.py:533
  135.7 5.1 %all-gather.9 = f32[10,1,2,2,4,256]{5,4,3,2,1,0:T(4,128)S(1)} all-gather(f32[5,1,2,2,4,256]{5,4,3,2,1,0:T(4,128)S(1)} %pick.3), channel_id=11, replica_groups={{0,8},{16,24},{32,40},{48,56},{64,72},{80,88},{96,104},{112,120},{128,1..., dimensions={0}, use_global_device_ids=true | all-gather | bytes 245760 | tf_op jit(solution)/shard_map/all_gather | solution.py:450
  140.8 5.7 %all-gather.10 = f32[4,5,1,2,2,4,256]{6,5,4,3,2,1,0:T(4,128)S(1)} all-gather(f32[2,5,1,2,2,4,256]{6,5,4,3,2,1,0:T(4,128)S(1)} %bitcast.29), channel_id=12, replica_groups={{8,16},{24,32},{40,48},{56,64},{72,80},{88,96},{104,112},{120,128},{136..., dimensions={0}, use_global_device_ids=true | all-gather | bytes 491520 | tf_op jit(solution)/shard_map/all_gather | solution.py:450
  146.5 5.1 %all_gather.113.far = f32[2,2,5,1,2,2,4,256]{7,6,5,4,3,2,1,0:T(4,128)S(1)} all-gather(f32[1,2,5,1,2,2,4,256]{7,6,5,4,3,2,1,0:T(4,128)S(1)} %constant_dynamic-slice_fusion), channel_id=1, replica_groups={{0,8},{16,24},{32,40},{48,56},{64,72},{80,88},{96,104},{112,120},{128,1..., dimensions={0}, use_global_device_ids=true | all-gather | bytes 491520 | tf_op jit(solution)/shard_map/all_gather | solution.py:450
  156.7 9.3 %collective-permute-start.5 = (f32[48,128]{1,0:T(8,128)S(1)}, f32[48,128]{1,0:T(8,128)S(1)}, u32[]{:S(2)}, u32[]{:S(2)}) collective-permute-start(f32[48,128]{1,0:T(8,128)S(1)} %bitcast.35), channel_id=1, source_target_pairs={{8,32},{32,8},{24,48},{48,24},{40,64},{64,40},{56,80},{80,56},{72,... | collective-permute-start | bytes 73736 | tf_op jit(solution)/shard_map/ppermute | solution.py:466
  167.5 2.2 %all-gather.11 = f32[1184,128]{1,0:T(8,128)S(1)} all-gather(f32[592,128]{1,0:T(8,128)S(1)} %pad_maximum_fusion.1), channel_id=13, replica_groups={{0,8},{16,24},{32,40},{48,56},{64,72},{80,88},{96,104},{112,120},{128,1..., dimensions={0}, use_global_device_ids=true | all-gather | bytes 909312 | tf_op jit(solution)/shard_map/all_gather | solution.py:450
  169.8 2.5 %up.1 = (f32[4,4,4,512]{3,2,1,0:T(4,128)S(1)}, f32[4,4,4,512]{3,2,1,0:T(4,128)S(1)}) custom-call(s32[4]{0:T(128)S(1)} %add_convert_fusion.prm, f32[1,2,24,128]{3,2,1,0:T(8,128)S(1)} %get-tuple-element.55.low, f32[2,592,128]{2,1,0:T(8,128)S(1)} %bitcast.25, f32[8,2,24,256]{3,2,1,0:T(8,128)S(1)} %get-tuple-element.58.middle, ...), custom_call_target="tpu_custom_call" | custom-call | tf_op jit(solution)/shard_map/up/pallas_call | solution.py:432
  (36 shorter events, 23.7 us)
Async XLA Ops:
  27.6 13.4 %collective-permute-start = (f32[6,4,8,512]{3,2,1,0:T(8,128)S(1)}, f32[6,4,8,512]{3,2,1,0:T(8,128)S(1)}, u32[]{:S(2)}, u32[]{:S(2)}) collective-permute-start(f32[6,4,8,512]{3,2,1,0:T(8,128)S(1)} %get-tuple-element.38), channel_id=1, source_target_pairs={{8,16},{16,8},{24,32},{32,24},{40,48},{48,40},{56,64},{64,56},{72,... | collective-permute-start | bytes 1179656 | tf_op jit(solution)/shard_map/ppermute | solution.py:466
  82.3 15.2 %collective-permute-start.1 = (f32[352,128]{1,0:T(8,128)S(1)}, f32[352,128]{1,0:T(8,128)S(1)}, u32[]{:S(2)}, u32[]{:S(2)}) collective-permute-start(f32[352,128]{1,0:T(8,128)S(1)} %get-tuple-element.42), channel_id=1, source_target_pairs={{8,16},{16,8},{24,32},{32,24},{40,48},{48,40},{56,64},{64,56},{72,... | collective-permute-start | bytes 540680 | tf_op jit(solution)/shard_map/ppermute | solution.py:466
  84.2 11.2 %collective-permute-start.3 = (f32[96,128]{1,0:T(8,128)S(1)}, f32[96,128]{1,0:T(8,128)S(1)}, u32[]{:S(2)}, u32[]{:S(2)}) collective-permute-start(f32[96,128]{1,0:T(8,128)S(1)} %bitcast.32), channel_id=1, source_target_pairs={{8,48},{48,8},{24,64},{64,24},{40,80},{80,40},{56,96},{96,56},{72,... | collective-permute-start | bytes 147464 | tf_op jit(solution)/shard_map/ppermute | solution.py:466
  86.1 11.4 %collective-permute-start.2 = (f32[96,128]{1,0:T(8,128)S(1)}, f32[96,128]{1,0:T(8,128)S(1)}, u32[]{:S(2)}, u32[]{:S(2)}) collective-permute-start(f32[96,128]{1,0:T(8,128)S(1)} %bitcast.33), channel_id=1, source_target_pairs={{8,32},{32,8},{24,48},{48,24},{40,64},{64,40},{56,80},{80,56},{72,... | collective-permute-start | bytes 147464 | tf_op jit(solution)/shard_map/ppermute | solution.py:466
  152.9 14.6 %collective-permute-start.4 = (f32[240,128]{1,0:T(8,128)S(1)}, f32[240,128]{1,0:T(8,128)S(1)}, u32[]{:S(2)}, u32[]{:S(2)}) collective-permute-start(f32[240,128]{1,0:T(8,128)S(1)} %get-tuple-element.57), channel_id=1, source_target_pairs={{8,16},{16,8},{24,32},{32,24},{40,48},{48,40},{56,64},{64,56},{72,... | collective-permute-start | bytes 368648 | tf_op jit(solution)/shard_map/ppermute | solution.py:466
  154.8 11.2 %collective-permute-start.6 = (f32[48,128]{1,0:T(8,128)S(1)}, f32[48,128]{1,0:T(8,128)S(1)}, u32[]{:S(2)}, u32[]{:S(2)}) collective-permute-start(f32[48,128]{1,0:T(8,128)S(1)} %bitcast.34), channel_id=1, source_target_pairs={{8,48},{48,8},{24,64},{64,24},{40,80},{80,40},{56,96},{96,56},{72,... | collective-permute-start | bytes 73736 | tf_op jit(solution)/shard_map/ppermute | solution.py:466
  156.7 10.8 %collective-permute-start.5 = (f32[48,128]{1,0:T(8,128)S(1)}, f32[48,128]{1,0:T(8,128)S(1)}, u32[]{:S(2)}, u32[]{:S(2)}) collective-permute-start(f32[48,128]{1,0:T(8,128)S(1)} %bitcast.35), channel_id=1, source_target_pairs={{8,32},{32,8},{24,48},{48,24},{40,64},{64,40},{56,80},{80,56},{72,... | collective-permute-start | bytes 73736 | tf_op jit(solution)/shard_map/ppermute | solution.py:466

commit v7 on v6

--- a/solution.py
+++ b/solution.py
@@ -164,13 +164,9 @@
     )
 
 
-def prepare_kernel(source, cond, out, both, work, sems):
-    copies = [pltpu.make_async_copy(ref, both.at[a], sems.at[a]) for a, ref in enumerate((source, cond))]
-    for copy in copies:
-        copy.start()
-    for copy in copies:
-        copy.wait()
-    tiles = reorder(both[...].reshape(128, 512), True)
+def prepare_kernel(source, cond, out, work):
+    rows = jnp.concatenate([source[...].reshape(64, 512), cond[...].reshape(64, 512)], axis=0)
+    tiles = reorder(rows, True)
     for c in range(4):
         work[c] = tiles[:, lanes(c)]
     for a in range(2):
@@ -425,8 +421,8 @@
     return jax.ShapeDtypeStruct(shape, jnp.float32)
 
 
-def call(body, outs, scratch, *args, scalars=True, space=pltpu.VMEM, sems=0, limit=VMEM_LIMIT, name=None):
-    specs = [pl.BlockSpec(memory_space=space)] * len(args)
+def call(body, outs, scratch, *args, scalars=True, name=None):
+    specs = [pl.BlockSpec(memory_space=pltpu.VMEM)] * len(args)
     if scalars:
         specs[0] = pl.BlockSpec(memory_space=pltpu.SMEM)
     return pl.pallas_call(
@@ -434,9 +430,8 @@
         out_shape=outs,
         in_specs=specs,
         out_specs=[pl.BlockSpec(memory_space=pltpu.VMEM)] * len(outs),
-        scratch_shapes=[pltpu.VMEM(s, jnp.float32) for s in scratch]
-        + ([pltpu.SemaphoreType.DMA((sems,))] if sems else []),
-        compiler_params=pltpu.CompilerParams(vmem_limit_bytes=limit),
+        scratch_shapes=[pltpu.VMEM(s, jnp.float32) for s in scratch],
+        compiler_params=pltpu.CompilerParams(vmem_limit_bytes=VMEM_LIMIT),
         name=name,
     )(*args)
 
@@ -488,13 +483,10 @@
     (remain,) = call(
         prepare_kernel,
         [f32(4, 8, 4, 512)],
-        [(2, 4, 16, 512), (4, 128, 128)],
+        [(4, 128, 128)],
         source,
         conduct,
         scalars=False,
-        space=pl.ANY,
-        sems=2,
-        limit=60 * 1024 * 1024,
         name="prepare",
     )
     adjoint = None

time: 174 us -> 174 us (level)
    unnamed x0 -> x4, local copies, waits for them, and re-layouts: none -> 1.8 us
where the time goes in v7:
time: 174 us; the launch traced here: 173 us
  blocking collectives  121 us (70%)
  starting transfers between devices  28.2 us (16%)
  Pallas kernels  16 us (9%)
  waiting for transfers between devices  3.54 us (2%)
  local copies, waits for them, and re-layouts  2.89 us (2%)
    all_gather x14, blocking collectives, gather(): lax.all_gather(value, 'gz', axis_index_groups=pairs(first, step, size))  86.1 us
    ppermute x7, starting transfers between devices, swap(): return lax.ppermute(value, 'gz', ways)  28.2 us
    all_to_all x2, blocking collectives, local(): rows = lax.all_to_all(low, 'gy', split_axis=0, concat_axis=0, tiled=True)  22.1 us
    pallas_call x12, Pallas kernels, call(): pl.pallas_call(body, out_shape=outs, in_specs=specs, out_specs=[pl.BlockS...  16 us
    all_gather x2, blocking collectives, row_pairs(): return lax.all_gather(value, ('gz', 'gy'), axis_index_groups=members)  12.8 us
    ppermute x7, waiting for transfers between devices, swap(): return lax.ppermute(value, 'gz', ways)  3.54 us
  transfers between devices with their start and end apart: 7, of which 2 were waited for; matrix products, arithmetic and copies ran while one was open for 0% of the time, Pallas kernels for 0%

profile of v7, /device:TPU:1, one launch (start us, length us, event | category | flops | bytes accessed | tf_op | source)
XLA Modules:
  0.0 173.0 jit_solution(17956240506762038742)
XLA Ops:
  3.4 12.3 %all-gather = f32[8,8,4,512]{3,1,2,0:T(8,128)S(1)} all-gather(f32[4,8,4,512]{3,1,2,0:T(8,128)S(1)} %copy.4), channel_id=2, replica_groups={{0,8},{16,24},{32,40},{48,56},{64,72},{80,88},{96,104},{112,120},{128,1..., dimensions={0}, use_global_device_ids=true | all-gather | bytes 786432 | tf_op jit(solution)/shard_map/all_gather | solution.py:445
  16.1 7.1 %all-gather.1 = f32[16,8,2,512]{3,1,2,0:T(8,128)S(1)} all-gather(f32[8,8,2,512]{3,1,2,0:T(8,128)S(1)} %slice_select_fusion.1), channel_id=3, replica_groups={{0,1},{2,3},{4,5},{6,7},{9,10},{11,12},{13,14},{15,8},{16,17},{18,19},{..., dimensions={0}, use_global_device_ids=true | all-gather | bytes 786432 | tf_op jit(solution)/shard_map/all_gather | solution.py:470
  23.2 2.2 %all-gather.12 = f32[16,8,2,512]{3,1,2,0:T(8,128)S(1)} all-gather(f32[8,8,2,512]{3,1,2,0:T(8,128)S(1)} %slice_select_fusion), channel_id=14, replica_groups={{0,8},{16,24},{32,40},{48,56},{64,72},{80,88},{96,104},{112,120},{128,1..., dimensions={0}, use_global_device_ids=true | all-gather | bytes 786432 | tf_op jit(solution)/shard_map/all_gather | solution.py:445
  28.7 11.5 %all-gather.2 = f32[12,4,8,512]{3,2,1,0:T(8,128)S(1)} all-gather(f32[6,4,8,512]{3,2,1,0:T(8,128)S(1)} %get-tuple-element.36), channel_id=4, replica_groups={{8,16},{24,32},{40,48},{56,64},{72,80},{88,96},{104,112},{120,128},{136..., dimensions={0}, use_global_device_ids=true | all-gather | bytes 1179648 | tf_op jit(solution)/shard_map/all_gather | solution.py:445
  42.0 11.7 %all_to_all.10.rows = f32[8,2,2,2,4,256]{5,4,3,2,1,0:T(4,128)S(1)} all-to-all(f32[8,2,2,2,4,256]{5,4,3,2,1,0:T(4,128)S(1)} %get-tuple-element.39), channel_id=1, replica_groups=mesh['gz'=96,'gy'=8] {'gy'}, dimensions={0} | all-to-all | bytes 524288 | tf_op jit(solution)/shard_map/all_to_all | solution.py:525
  54.3 13.0 %all-gather.3 = f32[10,2,2,2,4,256]{5,4,3,2,1,0:T(4,128)S(1)} all-gather(f32[5,2,2,2,4,256]{5,4,3,2,1,0:T(4,128)S(1)} %pick.2), channel_id=5, replica_groups={{0,8},{16,24},{32,40},{48,56},{64,72},{80,88},{96,104},{112,120},{128,1..., dimensions={0}, use_global_device_ids=true | all-gather | bytes 491520 | tf_op jit(solution)/shard_map/all_gather | solution.py:445
  67.3 7.5 %all-gather.4 = f32[4,5,2,2,2,4,256]{6,5,4,3,2,1,0:T(4,128)S(1)} all-gather(f32[2,5,2,2,2,4,256]{6,5,4,3,2,1,0:T(4,128)S(1)} %bitcast.23), channel_id=6, replica_groups={{8,16},{24,32},{40,48},{56,64},{72,80},{88,96},{104,112},{120,128},{136..., dimensions={0}, use_global_device_ids=true | all-gather | bytes 983040 | tf_op jit(solution)/shard_map/all_gather | solution.py:445
  74.7 5.3 %all_gather.99.far = f32[2,2,5,2,2,2,4,256]{7,6,5,4,3,2,1,0:T(4,128)S(1)} all-gather(f32[1,2,5,2,2,2,4,256]{7,6,5,4,3,2,1,0:T(4,128)S(1)} %constant_dynamic-slice_fusion.1), channel_id=1, replica_groups={{0,8},{16,24},{32,40},{48,56},{64,72},{80,88},{96,104},{112,120},{128,1..., dimensions={0}, use_global_device_ids=true | all-gather | bytes 983040 | tf_op jit(solution)/shard_map/all_gather | solution.py:445
  85.3 9.3 %collective-permute-start.2 = (f32[96,128]{1,0:T(8,128)S(1)}, f32[96,128]{1,0:T(8,128)S(1)}, u32[]{:S(2)}, u32[]{:S(2)}) collective-permute-start(f32[96,128]{1,0:T(8,128)S(1)} %bitcast.33), channel_id=1, source_target_pairs={{8,32},{32,8},{24,48},{48,24},{40,64},{64,40},{56,80},{80,56},{72,... | collective-permute-start | bytes 147464 | tf_op jit(solution)/shard_map/ppermute | solution.py:461
  94.6 2.0 %collective-permute-done.2 = f32[96,128]{1,0:T(8,128)S(1)} collective-permute-done((f32[96,128]{1,0:T(8,128)S(1)}, f32[96,128]{1,0:T(8,128)S(1)}, u32[]{:S(2)}, u32[]{:S(2)}) %collective-permute-start.2) | collective-permute-done | bytes 49184 | tf_op jit(solution)/shard_map/ppermute | solution.py:461
  96.7 3.3 %all-gather.5 = f32[1600,128]{1,0:T(8,128)S(1)} all-gather(f32[800,128]{1,0:T(8,128)S(1)} %pad_maximum_fusion), channel_id=7, replica_groups={{0,8},{16,24},{32,40},{48,56},{64,72},{80,88},{96,104},{112,120},{128,1..., dimensions={0}, use_global_device_ids=true | all-gather | bytes 1228800 | tf_op jit(solution)/shard_map/all_gather | solution.py:445
  100.0 2.5 %up_first.1 = (f32[4,4,4,512]{3,2,1,0:T(4,128)S(1)}, f32[4,4,4,512]{3,2,1,0:T(4,128)S(1)}, f32[14,2,16,256]{3,2,1,0:T(8,128)S(1)}, f32[14,1,24,128]{3,2,1,0:T(8,128)S(1)}, f32[14,1,24,128]{3,2,1,0:T(8,128)S(1)}) custom-call(s32[4]{0:T(128)S(1)} %add_convert_fusion.prm, f32[2,2,24,128]{3,2,1,0:T(8,128)S(1)} %get-tuple-element.40.low, ...), custom_call_target="tpu_custom_call" | custom-call | tf_op jit(solution)/shard_map/up_first/pallas_call | solution.py:428
  102.5 2.0 %all-gather.6 = f32[8,4,4,512]{3,2,1,0:T(4,128)S(1)} all-gather(f32[4,4,4,512]{3,2,1,0:T(4,128)S(1)} %get-tuple-element.51), channel_id=8, replica_groups={{0,8},{16,24},{32,40},{48,56},{64,72},{80,88},{96,104},{112,120},{128,1..., dimensions={0}, use_global_device_ids=true | all-gather | bytes 393216 | tf_op jit(solution)/shard_map/all_gather | solution.py:445
  104.6 5.7 %all-gather.7 = f32[16,4,2,512]{3,1,2,0:T(4,128)S(1)} all-gather(f32[8,4,2,512]{3,1,2,0:T(4,128)S(1)} %copy.7), channel_id=9, replica_groups={{0,1},{2,3},{4,5},{6,7},{9,10},{11,12},{13,14},{15,8},{16,17},{18,19},{..., dimensions={0}, use_global_device_ids=true | all-gather | bytes 393216 | tf_op jit(solution)/shard_map/all_gather | solution.py:470
  110.5 2.0 %all-gather.13 = f32[16,4,2,512]{3,1,2,0:T(4,128)S(1)} all-gather(f32[8,4,2,512]{3,1,2,0:T(4,128)S(1)} %copy.10), channel_id=15, replica_groups={{0,8},{16,24},{32,40},{48,56},{64,72},{80,88},{96,104},{112,120},{128,1..., dimensions={0}, use_global_device_ids=true | all-gather | bytes 393216 | tf_op jit(solution)/shard_map/all_gather | solution.py:445
  113.3 9.0 %all-gather.8 = f32[12,4,8,512]{3,2,1,0:T(8,128)S(1)} all-gather(f32[6,4,8,512]{3,2,1,0:T(8,128)S(1)} %get-tuple-element.53), channel_id=10, replica_groups={{8,16},{24,32},{40,48},{56,64},{72,80},{88,96},{104,112},{120,128},{136..., dimensions={0}, use_global_device_ids=true | all-gather | bytes 1179648 | tf_op jit(solution)/shard_map/all_gather | solution.py:445
  123.9 10.4 %all_to_all.11.rows = f32[8,1,2,2,4,256]{5,4,3,2,1,0:T(4,128)S(1)} all-to-all(f32[8,1,2,2,4,256]{5,4,3,2,1,0:T(4,128)S(1)} %get-tuple-element.54), channel_id=1, replica_groups=mesh['gz'=96,'gy'=8] {'gy'}, dimensions={0} | all-to-all | bytes 262144 | tf_op jit(solution)/shard_map/all_to_all | solution.py:525
  134.9 5.1 %all-gather.9 = f32[10,1,2,2,4,256]{5,4,3,2,1,0:T(4,128)S(1)} all-gather(f32[5,1,2,2,4,256]{5,4,3,2,1,0:T(4,128)S(1)} %pick.3), channel_id=11, replica_groups={{0,8},{16,24},{32,40},{48,56},{64,72},{80,88},{96,104},{112,120},{128,1..., dimensions={0}, use_global_device_ids=true | all-gather | bytes 245760 | tf_op jit(solution)/shard_map/all_gather | solution.py:445
  140.0 5.7 %all-gather.10 = f32[4,5,1,2,2,4,256]{6,5,4,3,2,1,0:T(4,128)S(1)} all-gather(f32[2,5,1,2,2,4,256]{6,5,4,3,2,1,0:T(4,128)S(1)} %bitcast.29), channel_id=12, replica_groups={{8,16},{24,32},{40,48},{56,64},{72,80},{88,96},{104,112},{120,128},{136..., dimensions={0}, use_global_device_ids=true | all-gather | bytes 491520 | tf_op jit(solution)/shard_map/all_gather | solution.py:445
  145.7 5.1 %all_gather.113.far = f32[2,2,5,1,2,2,4,256]{7,6,5,4,3,2,1,0:T(4,128)S(1)} all-gather(f32[1,2,5,1,2,2,4,256]{7,6,5,4,3,2,1,0:T(4,128)S(1)} %constant_dynamic-slice_fusion), channel_id=1, replica_groups={{0,8},{16,24},{32,40},{48,56},{64,72},{80,88},{96,104},{112,120},{128,1..., dimensions={0}, use_global_device_ids=true | all-gather | bytes 491520 | tf_op jit(solution)/shard_map/all_gather | solution.py:445
  152.1 1.9 %collective-permute-start.4 = (f32[240,128]{1,0:T(8,128)S(1)}, f32[240,128]{1,0:T(8,128)S(1)}, u32[]{:S(2)}, u32[]{:S(2)}) collective-permute-start(f32[240,128]{1,0:T(8,128)S(1)} %get-tuple-element.57), channel_id=1, source_target_pairs={{8,16},{16,8},{24,32},{32,24},{40,48},{48,40},{56,64},{64,56},{72,... | collective-permute-start | bytes 368648 | tf_op jit(solution)/shard_map/ppermute | solution.py:461
  155.9 9.3 %collective-permute-start.5 = (f32[48,128]{1,0:T(8,128)S(1)}, f32[48,128]{1,0:T(8,128)S(1)}, u32[]{:S(2)}, u32[]{:S(2)}) collective-permute-start(f32[48,128]{1,0:T(8,128)S(1)} %bitcast.35), channel_id=1, source_target_pairs={{8,32},{32,8},{24,48},{48,24},{40,64},{64,40},{56,80},{80,56},{72,... | collective-permute-start | bytes 73736 | tf_op jit(solution)/shard_map/ppermute | solution.py:461
  166.7 2.2 %all-gather.11 = f32[1184,128]{1,0:T(8,128)S(1)} all-gather(f32[592,128]{1,0:T(8,128)S(1)} %pad_maximum_fusion.1), channel_id=13, replica_groups={{0,8},{16,24},{32,40},{48,56},{64,72},{80,88},{96,104},{112,120},{128,1..., dimensions={0}, use_global_device_ids=true | all-gather | bytes 909312 | tf_op jit(solution)/shard_map/all_gather | solution.py:445
  169.0 2.5 %up.1 = (f32[4,4,4,512]{3,2,1,0:T(4,128)S(1)}, f32[4,4,4,512]{3,2,1,0:T(4,128)S(1)}) custom-call(s32[4]{0:T(128)S(1)} %add_convert_fusion.prm, f32[1,2,24,128]{3,2,1,0:T(8,128)S(1)} %get-tuple-element.55.low, f32[2,592,128]{2,1,0:T(8,128)S(1)} %bitcast.25, f32[8,2,24,256]{3,2,1,0:T(8,128)S(1)} %get-tuple-element.58.middle, ...), custom_call_target="tpu_custom_call" | custom-call | tf_op jit(solution)/shard_map/up/pallas_call | solution.py:428
  (40 shorter events, 23.4 us)
Async XLA Ops:
  0.6 0.9 copy-start
  1.5 0.9 copy-start.1
  26.7 13.4 %collective-permute-start = (f32[6,4,8,512]{3,2,1,0:T(8,128)S(1)}, f32[6,4,8,512]{3,2,1,0:T(8,128)S(1)}, u32[]{:S(2)}, u32[]{:S(2)}) collective-permute-start(f32[6,4,8,512]{3,2,1,0:T(8,128)S(1)} %get-tuple-element.38), channel_id=1, source_target_pairs={{8,16},{16,8},{24,32},{32,24},{40,48},{48,40},{56,64},{64,56},{72,... | collective-permute-start | bytes 1179656 | tf_op jit(solution)/shard_map/ppermute | solution.py:461
  81.4 15.2 %collective-permute-start.1 = (f32[352,128]{1,0:T(8,128)S(1)}, f32[352,128]{1,0:T(8,128)S(1)}, u32[]{:S(2)}, u32[]{:S(2)}) collective-permute-start(f32[352,128]{1,0:T(8,128)S(1)} %get-tuple-element.42), channel_id=1, source_target_pairs={{8,16},{16,8},{24,32},{32,24},{40,48},{48,40},{56,64},{64,56},{72,... | collective-permute-start | bytes 540680 | tf_op jit(solution)/shard_map/ppermute | solution.py:461
  83.4 11.2 %collective-permute-start.3 = (f32[96,128]{1,0:T(8,128)S(1)}, f32[96,128]{1,0:T(8,128)S(1)}, u32[]{:S(2)}, u32[]{:S(2)}) collective-permute-start(f32[96,128]{1,0:T(8,128)S(1)} %bitcast.32), channel_id=1, source_target_pairs={{8,48},{48,8},{24,64},{64,24},{40,80},{80,40},{56,96},{96,56},{72,... | collective-permute-start | bytes 147464 | tf_op jit(solution)/shard_map/ppermute | solution.py:461
  85.3 11.4 %collective-permute-start.2 = (f32[96,128]{1,0:T(8,128)S(1)}, f32[96,128]{1,0:T(8,128)S(1)}, u32[]{:S(2)}, u32[]{:S(2)}) collective-permute-start(f32[96,128]{1,0:T(8,128)S(1)} %bitcast.33), channel_id=1, source_target_pairs={{8,32},{32,8},{24,48},{48,24},{40,64},{64,40},{56,80},{80,56},{72,... | collective-permute-start | bytes 147464 | tf_op jit(solution)/shard_map/ppermute | solution.py:461
  152.1 14.6 %collective-permute-start.4 = (f32[240,128]{1,0:T(8,128)S(1)}, f32[240,128]{1,0:T(8,128)S(1)}, u32[]{:S(2)}, u32[]{:S(2)}) collective-permute-start(f32[240,128]{1,0:T(8,128)S(1)} %get-tuple-element.57), channel_id=1, source_target_pairs={{8,16},{16,8},{24,32},{32,24},{40,48},{48,40},{56,64},{64,56},{72,... | collective-permute-start | bytes 368648 | tf_op jit(solution)/shard_map/ppermute | solution.py:461
  154.0 11.2 %collective-permute-start.6 = (f32[48,128]{1,0:T(8,128)S(1)}, f32[48,128]{1,0:T(8,128)S(1)}, u32[]{:S(2)}, u32[]{:S(2)}) collective-permute-start(f32[48,128]{1,0:T(8,128)S(1)} %bitcast.34), channel_id=1, source_target_pairs={{8,48},{48,8},{24,64},{64,24},{40,80},{80,40},{56,96},{96,56},{72,... | collective-permute-start | bytes 73736 | tf_op jit(solution)/shard_map/ppermute | solution.py:461
  155.9 10.8 %collective-permute-start.5 = (f32[48,128]{1,0:T(8,128)S(1)}, f32[48,128]{1,0:T(8,128)S(1)}, u32[]{:S(2)}, u32[]{:S(2)}) collective-permute-start(f32[48,128]{1,0:T(8,128)S(1)} %bitcast.35), channel_id=1, source_target_pairs={{8,32},{32,8},{24,48},{48,24},{40,64},{64,40},{56,80},{80,56},{72,... | collective-permute-start | bytes 73736 | tf_op jit(solution)/shard_map/ppermute | solution.py:461
